TPU v7x, 32 devices: a whole 2x2x4 slice. The times are simulated.
32 devices in a mesh: dp: 8 (over y, x, core), mp: 4 (over z).
Axes of the slice: x: 2, y: 2, z: 4, core: 2. Of those that a mesh axis runs over, the one named last changes fastest.
Arguments:
- hidden_in: bfloat16 [16384, 1024], P(('dp', 'mp')), may hold values from -6 to 6
- first_in: bfloat16 [16384, 1024], P(('dp', 'mp'))
- segment_ids: int32 [16384], P('dp'), may hold values from 0 to 23, as said below
- valid_tokens: int32 [16384], P('dp'), may hold values from 0 to 1, as said below
- w_query: bfloat16 [1024, 1024], P(None, 'mp'), may hold values from -0.1875 to 0.1875
- w_key: bfloat16 [1024, 1024], P(None, 'mp'), may hold values from -0.1875 to 0.1875
- w_value: bfloat16 [1024, 1024], P(None, 'mp'), may hold values from -0.1875 to 0.1875
- w_first_value: bfloat16 [1024, 1024], P(None, 'mp'), may hold values from -0.1875 to 0.1875
- w_out: bfloat16 [1024, 1024], P('mp'), may hold values from -1 to 1
- w_gate: bfloat16 [1024, 2816], P(None, 'mp'), may hold values from -0.1875 to 0.1875
- w_up: bfloat16 [1024, 2816], P(None, 'mp'), may hold values from -0.1875 to 0.1875
- w_down: bfloat16 [2816, 1024], P('mp'), may hold values from -0.109375 to 0.109375
- gain_attn: float32 [1024], replicated, may hold values from 0.5 to 1.5
- gain_mlp: float32 [1024], replicated, may hold values from 0.5 to 1.5
- out_cotangent: bfloat16 [16384, 1024], P('dp'), may hold values from -6 to 6
Outputs:
- block_out: bfloat16 [16384, 1024], P(('dp', 'mp'))
- grad_input: bfloat16 [16384, 1024], P(('dp', 'mp'))
- grad_query: float32 [1024, 1024], P(None, 'mp')
- grad_key: float32 [1024, 1024], P(None, 'mp')
- grad_value: float32 [1024, 1024], P(None, 'mp')
- grad_first_value: float32 [1024, 1024], P(None, 'mp')
- grad_out: float32 [1024, 1024], P('mp')
- grad_gate: float32 [1024, 2816], P(None, 'mp')
- grad_up: float32 [1024, 2816], P(None, 'mp')
- grad_down: float32 [2816, 1024], P('mp')
- grad_gain_attn: float32 [1024], replicated
- grad_gain_mlp: float32 [1024], replicated
- first_power: float32 [], replicated
- blend_power: float32 [], replicated
Inputs may be any that keep to these rules, and one draw needn't show every extreme that they name: `segment_ids`: each packed sequence of 2048 tokens starts a new document, holds a short document, a long one and padding at its end; ids are distinct across sequences and never fall. `valid_tokens`: 0 exactly on the padding at the end of each sequence; padding has a segment id of its own.
All inputs are finite; a program needn't handle non-finite values.
Results may differ from a plain program's by a relative error of at most 0.022.
Values may be sent and summed in bfloat16 or wider, within the bound.
No kernel may reach another device: no remote copies, remote signals or barrier semaphores. Data moves between devices by JAX's collectives and lax.ppermute only.
A program may use at most 192 MiB of HBM per device.

v0:
```python
import math

import jax
import jax.numpy as jnp
from jax import lax
from jax.sharding import PartitionSpec as P

HD = 64
SEQ = 2048


norm_eps = 1e-06


def token_places(segment_ids):
    n_tokens = segment_ids.shape[0]
    indices = jnp.arange(n_tokens, dtype=jnp.int32)
    starts_new = jnp.concatenate([jnp.ones((1,), jnp.bool_), segment_ids[1:] != segment_ids[:-1]])
    begins = lax.cummax(jnp.where(starts_new, indices, jnp.zeros_like(indices)), axis=0)
    return indices - begins


def rotate(values, places, turn_sign):
    half_size = values.shape[-1] // 2
    frequency = jnp.exp(
        jnp.arange(half_size, dtype=jnp.float32) * (-2.0 * math.log(10000.0) / values.shape[-1])
    )
    angles = places.astype(jnp.float32)[:, None] * frequency[None, :]
    cosine = jnp.cos(angles)[:, None, :]
    sine_part = turn_sign * jnp.sin(angles)[:, None, :]
    first_half = values[..., :half_size]
    second_half = values[..., half_size:]
    return jnp.concatenate(
        [
            first_half * cosine - second_half * sine_part,
            second_half * cosine + first_half * sine_part,
        ],
        -1,
    )


def rms_parts(values):
    inverse = lax.rsqrt(jnp.mean(values * values, axis=-1, keepdims=True) + norm_eps)
    return (values * inverse, inverse)


def rms_back(grad_rows, normed, inverse, gain_vec):
    grad_normed = grad_rows * gain_vec
    return inverse * (grad_normed - normed * jnp.mean(grad_normed * normed, axis=-1, keepdims=True))


def block_mask(segment_ids, valid_tokens, row_first, seq_first, block_rows):
    row_ids = lax.dynamic_slice_in_dim(segment_ids, row_first, block_rows, 0)
    row_place = row_first + jnp.arange(block_rows, dtype=jnp.int32)
    col_place = seq_first + jnp.arange(SEQ, dtype=jnp.int32)
    allowed = (row_ids[:, None] == segment_ids[None, :]) & (
        col_place[None, :] <= row_place[:, None]
    )
    return allowed & ((valid_tokens[None, :] == 1) | (col_place[None, :] == row_place[:, None]))


def block_scores(queries, key_rows, segment_ids, valid_tokens, row_first, seq_first, block_rows):
    q_block = lax.dynamic_slice_in_dim(queries, row_first, block_rows, 0)
    scores = jnp.einsum(
        "qhd,khd->hqk", q_block, key_rows, preferred_element_type=jnp.float32
    ) * queries.shape[-1] ** (-0.5)
    allowed = block_mask(segment_ids, valid_tokens, row_first, seq_first, block_rows)
    return (q_block, key_rows, jnp.where(allowed[None], scores, -1e30), allowed)


def attend_forward(queries, key_rows, blended, segment_ids, valid_tokens, block_rows):
    n_tokens, n_heads, head_size = queries.shape

    def one_block(block_index):
        row_first = block_index * block_rows
        seq_first = row_first // SEQ * SEQ
        q_block, k_block, scores, allowed = block_scores(
            queries, key_rows, segment_ids, valid_tokens, row_first, seq_first, block_rows
        )
        row_peak = jnp.max(scores, -1, keepdims=True)
        exp_scores = jnp.exp(scores - row_peak)
        totals = jnp.sum(exp_scores, -1, keepdims=True)
        probs = (exp_scores / totals).astype(jnp.bfloat16)
        out_block = jnp.einsum("hqk,khd->qhd", probs, blended, preferred_element_type=jnp.float32)
        return (out_block, (row_peak + jnp.log(totals))[..., 0])

    block_outs, logsum = lax.map(one_block, jnp.arange(n_tokens // block_rows, dtype=jnp.int32))
    return (block_outs.reshape(n_tokens, n_heads, head_size), logsum)


def attend_backward(
    queries, key_rows, blended, grad_mixed, segment_ids, valid_tokens, logsum, block_rows
):
    n_tokens, n_heads, head_size = queries.shape
    score_scale = head_size ** (-0.5)
    empty = jnp.zeros((n_tokens, n_heads, head_size), jnp.float32)

    def one_block(running, block_index):
        grad_keys, grad_values = running
        row_first = block_index * block_rows
        seq_first = row_first // SEQ * SEQ
        q_block, k_block, scores, allowed = block_scores(
            queries, key_rows, segment_ids, valid_tokens, row_first, seq_first, block_rows
        )
        g_block = lax.dynamic_slice_in_dim(grad_mixed, row_first, block_rows, 0)
        probs = jnp.where(allowed[None], jnp.exp(scores - logsum[block_index][..., None]), 0.0)
        grad_probs = jnp.einsum(
            "qhd,khd->hqk", g_block, blended, preferred_element_type=jnp.float32
        )
        row_inner = jnp.sum(grad_probs * probs, -1, keepdims=True)
        grad_scores = (probs * (grad_probs - row_inner)).astype(jnp.bfloat16)
        grad_q = (
            jnp.einsum("hqk,khd->qhd", grad_scores, k_block, preferred_element_type=jnp.float32)
            * score_scale
        )
        part_keys = (
            jnp.einsum("hqk,qhd->khd", grad_scores, q_block, preferred_element_type=jnp.float32)
            * score_scale
        )
        part_values = jnp.einsum(
            "hqk,qhd->khd", probs.astype(jnp.bfloat16), g_block, preferred_element_type=jnp.float32
        )
        grad_keys = grad_keys + part_keys
        grad_values = grad_values + part_values
        return ((grad_keys, grad_values), grad_q)

    (grad_keys, grad_values), grad_queries = lax.scan(
        one_block, (empty, empty), jnp.arange(n_tokens // block_rows, dtype=jnp.int32)
    )
    return (grad_queries.reshape(n_tokens, n_heads, head_size), grad_keys, grad_values)


def shards(
    hidden_in,
    first_in,
    segment_ids,
    valid_tokens,
    w_query,
    w_key,
    w_value,
    w_first_value,
    w_out,
    w_gate,
    w_up,
    w_down,
    gain_attn,
    gain_mlp,
    out_cotangent,
):
    own_rows = hidden_in.shape[0]
    n_tokens = segment_ids.shape[0]
    head_cols = w_query.shape[1]
    local_heads = head_cols // HD
    ffn_cols = w_gate.shape[1]
    block_rows = min(512, SEQ)
    places = token_places(segment_ids)
    live_rows = valid_tokens.astype(jnp.float32)[:, None]
    x_float = hidden_in.astype(jnp.float32)
    normed_one, inverse_one = rms_parts(x_float)
    normed_all = lax.all_gather(
        (normed_one * gain_attn).astype(jnp.bfloat16), "mp", axis=0, tiled=True
    )
    w_inner = jnp.concatenate([w_query, w_key, w_value], 1)
    projected = jnp.dot(normed_all, w_inner, preferred_element_type=jnp.float32)
    queries = rotate(
        projected[:, :head_cols].reshape(n_tokens, local_heads, HD), places, 1.0
    ).astype(jnp.bfloat16)
    key_rows = rotate(
        projected[:, head_cols : 2 * head_cols].reshape(n_tokens, local_heads, HD), places, 1.0
    ).astype(jnp.bfloat16)
    first_all = lax.all_gather(first_in, "mp", axis=0, tiled=True)
    first_values = jnp.dot(first_all, w_first_value, preferred_element_type=jnp.float32).astype(
        jnp.bfloat16
    )
    blended = (0.5 * projected[:, 2 * head_cols :] + 0.5 * first_values.astype(jnp.float32)).astype(
        jnp.bfloat16
    )
    blend_heads = blended.reshape(n_tokens, local_heads, HD)
    attended, logsum = attend_forward(
        queries, key_rows, blend_heads, segment_ids, valid_tokens, block_rows
    )
    attn_mixed = (attended.reshape(n_tokens, head_cols) * live_rows).astype(jnp.bfloat16)
    residual = x_float + lax.psum_scatter(
        jnp.dot(attn_mixed, w_out, preferred_element_type=jnp.float32),
        "mp",
        scatter_dimension=0,
        tiled=True,
    )
    normed_two, inverse_two = rms_parts(residual)
    mid_all = lax.all_gather((normed_two * gain_mlp).astype(jnp.bfloat16), "mp", axis=0, tiled=True)
    w_gate_up = jnp.concatenate([w_gate, w_up], 1)
    gate_up = jnp.dot(mid_all, w_gate_up, preferred_element_type=jnp.float32)
    gate_pre = gate_up[:, :ffn_cols]
    up_pre = gate_up[:, ffn_cols:]
    gate_sigmoid = jax.nn.sigmoid(gate_pre)
    silu_value = gate_pre * gate_sigmoid
    ffn_hidden = (silu_value * up_pre).astype(jnp.bfloat16)
    block_out = (
        residual
        + lax.psum_scatter(
            jnp.dot(ffn_hidden, w_down, preferred_element_type=jnp.float32).astype(jnp.bfloat16),
            "mp",
            scatter_dimension=0,
            tiled=True,
        ).astype(jnp.float32)
    ).astype(jnp.bfloat16)
    grad_rows = lax.dynamic_slice_in_dim(
        out_cotangent, lax.axis_index("mp") * own_rows, own_rows, 0
    ).astype(jnp.float32)
    grad_down = jnp.einsum(
        "tf,td->fd", ffn_hidden, out_cotangent, preferred_element_type=jnp.float32
    )
    grad_hidden = (
        jnp.einsum("td,fd->tf", out_cotangent, w_down, preferred_element_type=jnp.float32)
        .astype(jnp.bfloat16)
        .astype(jnp.float32)
    )
    grad_gate_pre = (
        grad_hidden * up_pre * gate_sigmoid * (1.0 + gate_pre * (1.0 - gate_sigmoid))
    ).astype(jnp.bfloat16)
    grad_up_pre = (grad_hidden * silu_value).astype(jnp.bfloat16)
    grad_gate_up = jnp.concatenate([grad_gate_pre, grad_up_pre], 1)
    grad_w_gate_up = jnp.einsum(
        "td,tf->df", mid_all, grad_gate_up, preferred_element_type=jnp.float32
    )
    grad_mid = lax.psum_scatter(
        jnp.einsum("tf,df->td", grad_gate_up, w_gate_up, preferred_element_type=jnp.float32).astype(
            jnp.bfloat16
        ),
        "mp",
        scatter_dimension=0,
        tiled=True,
    ).astype(jnp.float32)
    grad_resid = grad_rows + rms_back(grad_mid, normed_two, inverse_two, gain_mlp)
    part_gain_mlp = jnp.sum(grad_mid * normed_two, 0)
    grad_attn_all = lax.all_gather(grad_resid.astype(jnp.bfloat16), "mp", axis=0, tiled=True)
    grad_w_out = jnp.einsum(
        "tw,td->wd", attn_mixed, grad_attn_all, preferred_element_type=jnp.float32
    )
    grad_attn_rounded = jnp.einsum(
        "td,wd->tw", grad_attn_all, w_out, preferred_element_type=jnp.float32
    ).astype(jnp.bfloat16)
    grad_mixed = (grad_attn_rounded.astype(jnp.float32) * live_rows).astype(jnp.bfloat16)
    grad_queries, grad_keys, grad_values = attend_backward(
        queries,
        key_rows,
        blend_heads,
        grad_mixed.reshape(n_tokens, local_heads, HD),
        segment_ids,
        valid_tokens,
        logsum,
        block_rows,
    )
    grad_blend = grad_values.reshape(n_tokens, head_cols).astype(jnp.bfloat16)
    grad_half = (grad_blend.astype(jnp.float32) * 0.5).astype(jnp.bfloat16)
    grad_query_pre = (
        rotate(grad_queries, places, -1.0).reshape(n_tokens, head_cols).astype(jnp.bfloat16)
    )
    grad_key_pre = rotate(grad_keys, places, -1.0).reshape(n_tokens, head_cols).astype(jnp.bfloat16)
    grad_projected = jnp.concatenate([grad_query_pre, grad_key_pre, grad_half], 1)
    grad_w_inner = jnp.einsum(
        "td,tc->dc", normed_all, grad_projected, preferred_element_type=jnp.float32
    )
    grad_normed = lax.psum_scatter(
        jnp.einsum("tc,dc->td", grad_projected, w_inner, preferred_element_type=jnp.float32).astype(
            jnp.bfloat16
        ),
        "mp",
        scatter_dimension=0,
        tiled=True,
    ).astype(jnp.float32)
    grad_input = (grad_resid + rms_back(grad_normed, normed_one, inverse_one, gain_attn)).astype(
        jnp.bfloat16
    )
    part_gain_attn = jnp.sum(grad_normed * normed_one, 0)
    grad_first = jnp.einsum("td,tc->dc", first_all, grad_half, preferred_element_type=jnp.float32)
    summed = (
        lax.psum(grad_w_inner.astype(jnp.bfloat16), "dp").astype(jnp.float32),
        lax.psum(grad_first.astype(jnp.bfloat16), "dp").astype(jnp.float32),
        lax.psum(grad_w_out.astype(jnp.bfloat16), "dp").astype(jnp.float32),
        lax.psum(grad_w_gate_up.astype(jnp.bfloat16), "dp").astype(jnp.float32),
        lax.psum(grad_down.astype(jnp.bfloat16), "dp").astype(jnp.float32),
    )
    first_float = first_values.astype(jnp.float32)
    blend_float = blended.astype(jnp.float32)
    small_totals = lax.psum(
        (
            part_gain_attn,
            part_gain_mlp,
            jnp.sum(first_float * first_float),
            jnp.sum(blend_float * blend_float),
        ),
        ("dp", "mp"),
    )
    element_count = float(n_tokens * lax.axis_size("dp") * hidden_in.shape[1])
    inner_sum = summed[0]
    gate_up_sum = summed[3]
    return (
        block_out,
        grad_input,
        inner_sum[:, :head_cols],
        inner_sum[:, head_cols : 2 * head_cols],
        inner_sum[:, 2 * head_cols :],
        summed[1],
        summed[2],
        gate_up_sum[:, :ffn_cols],
        gate_up_sum[:, ffn_cols:],
        summed[4],
        small_totals[0],
        small_totals[1],
        small_totals[2] / element_count,
        small_totals[3] / element_count,
    )


def solution(mesh):
    placed = (
        P(("dp", "mp"), None),
        P(("dp", "mp"), None),
        P("dp"),
        P("dp"),
        P(None, "mp"),
        P(None, "mp"),
        P(None, "mp"),
        P(None, "mp"),
        P("mp", None),
        P(None, "mp"),
        P(None, "mp"),
        P("mp", None),
        P(),
        P(),
        P("dp", None),
    )
    return jax.shard_map(
        shards,
        mesh=mesh,
        in_specs=placed,
        out_specs=(
            P(("dp", "mp"), None),
            P(("dp", "mp"), None),
            P(None, "mp"),
            P(None, "mp"),
            P(None, "mp"),
            P(None, "mp"),
            P("mp", None),
            P(None, "mp"),
            P(None, "mp"),
            P("mp", None),
            P(),
            P(),
            P(),
            P(),
        ),
        check_vma=False,
    )
```

profile of v0, /device:TPU:0, one launch (start us, length us, event | category | flops | bytes accessed | tf_op | source)
XLA Modules:
  0.0 1290.2 jit_solution(1636348525661726412)
XLA Ops:
  16.7 78.4 %all-gather.5.cloned.1.call-done = bf16[2048,1024]{1,0:T(8,128)(2,1)} async-done(((bf16[512,1024]{1,0:T(8,128)(2,1)}), bf16[2048,1024]{1,0:T(8,128)(2,1)}) %all-gather.5.cloned.1.call-update) | async-done | bytes 4194320 | tf_op jit(solution)/shard_map/all_gather | solution.py:160
  104.0 72.1 %all-gather.7.cloned.1.call-done = bf16[2048,1024]{1,0:T(8,128)(2,1)} async-done(((bf16[512,1024]{1,0:T(8,128)(2,1)}), bf16[2048,1024]{1,0:T(8,128)(2,1)}) %all-gather.7.cloned.1.call-update) | async-done | bytes 4194320 | tf_op jit(solution)/shard_map/all_gather | solution.py:171
  187.3 127.1 %while.31 = (s32[]{:T(128)}, f32[4,512,4,64]{1,0,3,2:T(4,128)}, f32[4,4,512]{2,1,0:T(4,128)}, s32[4]{0:T(128)S(1)}, s32[2048]{0:T(1024)S(1)}, /*index=5*/s32[204...) while((s32[]{:T(128)}, f32[4,512,4,64]{1,0,3,2:T(4,128)}, ...), condition=%wide.region_6.7_spmd, body=%wide.region_3.6_spmd.sunk | while | flops 1130367488 | bytes 59619720 | solution.py:87
  208.1 11.1 dynamic_update_slice.26
  239.7 11.1 dynamic_update_slice.26
  271.4 11.1 dynamic_update_slice.26
  303.1 11.1 dynamic_update_slice.26
  322.9 143.1 %reduce-scatter.5.cloned.1.call-done = f32[512,1024]{1,0:T(8,128)} async-done(((f32[2048,1024]{1,0:T(8,128)}), f32[512,1024]{1,0:T(8,128)}) %reduce-scatter.5.cloned.1.call-update) | async-done | bytes 2097168 | tf_op jit(solution)/shard_map/reduce_scatter | solution.py:183
  474.5 77.7 %all-gather.9.cloned.1.call-done = bf16[2048,1024]{1,0:T(8,128)(2,1)} async-done(((bf16[512,1024]{1,0:T(8,128)(2,1)}), bf16[2048,1024]{1,0:T(8,128)(2,1)}) %all-gather.9.cloned.1.call-update) | async-done | bytes 4194320 | tf_op jit(solution)/shard_map/all_gather | solution.py:190
  570.3 10.2 convolution_convert_fusion.1
  581.0 75.0 %reduce-scatter.9.cloned.1.call-done = bf16[512,1024]{1,0:T(8,128)(2,1)} async-done(((bf16[2048,1024]{1,0:T(8,128)(2,1)}), bf16[512,1024]{1,0:T(8,128)(2,1)}) %reduce-scatter.9.cloned.1.call-update) | async-done | bytes 1048592 | tf_op jit(solution)/shard_map/reduce_scatter | solution.py:226
  677.9 65.8 %all-gather.11.cloned.1.call-done = bf16[2048,1024]{1,0:T(8,128)(2,1)} async-done(((bf16[512,1024]{1,0:T(8,128)(2,1)}), bf16[2048,1024]{1,0:T(8,128)(2,1)}) %all-gather.11.cloned.1.call-update) | async-done | bytes 4194320 | tf_op jit(solution)/shard_map/all_gather | solution.py:236
  749.8 236.1 %while.32 = (s32[]{:T(128)}, f32[2048,4,64]{0,2,1:T(8,128)}, f32[2048,4,64]{0,2,1:T(8,128)}, f32[4,512,4,64]{1,0,3,2:T(4,128)}, s32[4]{0:T(128)S(1)}, /*index=5*...) while((s32[]{:T(128)}, f32[2048,4,64]{0,2,1:T(8,128)}, ...), condition=%wide.region_14.15_spmd.clone, body=%wide.region_12.14_spmd.clone.sunk | while | flops 2735344128 | bytes 176773616 | solution.py:127
  767.0 9.7 multiply_reduce_fusion.4
  796.7 11.1 dynamic_update_slice.27
  825.6 9.7 multiply_reduce_fusion.4
  856.0 11.1 dynamic_update_slice.27
  915.3 11.1 dynamic_update_slice.27
  944.2 9.7 multiply_reduce_fusion.4
  974.6 11.1 dynamic_update_slice.27
  1021.7 95.1 %all-reduce.4.cloned.1.call-done = (bf16[1024,768]{1,0:T(8,128)(2,1)}, bf16[1024,256]{0,1:T(8,128)(2,1)}, bf16[1024,1408]{1,0:T(8,128)(2,1)}, bf16[256,1024]{1,0:T(8,128)(2,1)}, bf16[704,1024]{1,0:T(8,128)(2,1)}) async-done(((bf16[1024,768]{1,0:T(8,128)(2,1)}, bf16[1024,256]{0,1:T(8,128)(2,1)}, bf16[1024,1408]{1,0:T(8,128)(2,1)}, bf16[256,1024]{1,0:T(8,128)(2,1)}, bf16[704,1024]{1,0:T(8,128)(2,1)}), ...) | async-done | bytes 6946832 | tf_op jit(solution)/shard_map/psum | solution.py:278
  1138.2 57.8 %reduce-scatter.11.cloned.1.call-done = bf16[512,1024]{1,0:T(8,128)(2,1)} async-done(((bf16[2048,1024]{1,0:T(8,128)(2,1)}), bf16[512,1024]{1,0:T(8,128)(2,1)}) %reduce-scatter.11.cloned.1.call-update) | async-done | bytes 1048592 | tf_op jit(solution)/shard_map/reduce_scatter | solution.py:264
  1198.6 46.0 %all-reduce = (f32[1024]{0:T(1024)}, f32[1024]{0:T(1024)}, f32[]{:T(128)}, f32[]{:T(128)}) all-reduce(f32[1024]{0:T(1024)} %get-tuple-element.355, f32[1024]{0:T(1024)} %get-tuple-element.353, f32[]{:T(128)} %get-tuple-element.436, f32[]{:T(128)} %get-tuple-element.408), channel_id=1, replica_groups=mesh['dp'=8,'mp'=4] {'dp','mp'}, use_global_device_ids=true, to_apply=%region_23.24 | all-reduce | flops 2050 | bytes 16400 | tf_op jit(solution)/shard_map/psum | solution.py:286
  1247.2 29.6 %reduce-scatter.7.cloned.1.call-done = bf16[512,1024]{1,0:T(8,128)(2,1)} async-done(((bf16[2048,1024]{1,0:T(8,128)(2,1)}), bf16[512,1024]{1,0:T(8,128)(2,1)}) %reduce-scatter.7.cloned.1.call-update) | async-done | bytes 1048592 | tf_op jit(solution)/shard_map/reduce_scatter | solution.py:200
  (281 shorter events, 390.6 us)
Async XLA Ops:
  7.2 554.0 %copy-start = (bf16[704,1024]{1,0:T(8,128)(2,1)S(1)}, bf16[704,1024]{1,0:T(8,128)(2,1)}, u32[]{:S(2)}) copy-start(bf16[704,1024]{1,0:T(8,128)(2,1)} %param.30) | copy-start | bytes 4325380
  7.2 87.9 %all-gather.5.cloned.1.call-start = ((), (), s32[]{:S(2)}) async-start(), calls=%async_computation.4 | async-start | bytes 5242880 | tf_op jit(solution)/shard_map/all_gather | solution.py:160
  11.6 164.5 %all-gather.7.cloned.1.call-start = ((), (), s32[]{:S(2)}) async-start(), calls=%async_computation.5 | async-start | bytes 5242880 | tf_op jit(solution)/shard_map/all_gather | solution.py:171
  12.3 453.7 %reduce-scatter.5.cloned.1.call-start = ((), (), s32[]{:S(2)}) async-start(), calls=%async_computation.6 | async-start | bytes 10485760 | tf_op jit(solution)/shard_map/reduce_scatter | solution.py:183
  16.7 167.0 %copy-start.13 = (f32[2048,32]{0,1:T(8,128)}, f32[2048,32]{0,1:T(8,128)S(1)}, u32[]{:S(2)}) copy-start(f32[2048,32]{0,1:T(8,128)S(1)} %get-tuple-element.443) | copy-start | bytes 786436
  16.7 159.3 %copy-start.23 = (bf16[1024,256]{1,0:T(8,128)(2,1)S(1)}, bf16[1024,256]{1,0:T(8,128)(2,1)}, u32[]{:S(2)}) copy-start(bf16[1024,256]{1,0:T(8,128)(2,1)} %param.26) | copy-start | bytes 1572868
  322.9 143.2 %copy-start.5 = (bf16[512,1024]{1,0:T(8,128)(2,1)S(1)}, bf16[512,1024]{1,0:T(8,128)(2,1)}, u32[]{:S(2)}) copy-start(bf16[512,1024]{1,0:T(8,128)(2,1)} %param.19) | copy-start | bytes 3145732
  322.9 229.3 %all-gather.9.cloned.1.call-start = ((), (), s32[]{:S(2)}) async-start(), calls=%async_computation.7 | async-start | bytes 5242880 | tf_op jit(solution)/shard_map/all_gather | solution.py:190
  468.0 191.4 %copy-start.36 = (f32[512]{0:T(512)}, f32[512]{0:T(512)S(1)}, u32[]{:S(2)}) copy-start(f32[512]{0:T(512)S(1)} %add_rsqrt_fusion) | copy-start | bytes 6148
  470.5 185.5 %reduce-scatter.9.cloned.1.call-start = ((), (), s32[]{:S(2)}) async-start(), calls=%async_computation.9 | async-start | bytes 5242880 | tf_op jit(solution)/shard_map/reduce_scatter | solution.py:226
  552.2 9.0 copy-start.17
  580.5 75.5 %copy-start.34 = (f32[1024]{0:T(1024)S(1)}, f32[1024]{0:T(1024)}, u32[]{:S(2)}) copy-start(f32[1024]{0:T(1024)} %param.32) | copy-start | bytes 12292
  580.6 163.2 %all-gather.11.cloned.1.call-start = ((), (), s32[]{:S(2)}) async-start(), calls=%async_computation.10 | async-start | bytes 5242880 | tf_op jit(solution)/shard_map/all_gather | solution.py:236
  662.3 454.5 %all-reduce.4.cloned.1.call-start = ((), (), s32[]{:S(2)}) async-start(), calls=%async_computation.12 | async-start | bytes 13893632 | tf_op jit(solution)/shard_map/psum | solution.py:278
  669.8 73.9 %copy-start.25 = (bf16[256,1024]{1,0:T(8,128)(2,1)S(1)}, bf16[256,1024]{1,0:T(8,128)(2,1)}, u32[]{:S(2)}) copy-start(bf16[256,1024]{1,0:T(8,128)(2,1)} %param.27) | copy-start | bytes 1572868
  669.9 73.9 %copy-start.31 = (f32[2048]{0:T(1024)S(1)}, f32[2048]{0:T(1024)}, u32[]{:S(2)}) copy-start(f32[2048]{0:T(1024)} %convert_element_type.173) | copy-start | bytes 24580
  1005.9 190.1 %reduce-scatter.11.cloned.1.call-start = ((), (), s32[]{:S(2)}) async-start(), calls=%async_computation.11 | async-start | bytes 5242880 | tf_op jit(solution)/shard_map/reduce_scatter | solution.py:264
  1014.3 262.4 %reduce-scatter.7.cloned.1.call-start = ((), (), s32[]{:S(2)}) async-start(), calls=%async_computation.8 | async-start | bytes 5242880 | tf_op jit(solution)/shard_map/reduce_scatter | solution.py:200
  1134.9 61.1 %copy-start.6 = (bf16[512,1024]{1,0:T(8,128)(2,1)S(1)}, bf16[512,1024]{1,0:T(8,128)(2,1)}, u32[]{:S(2)}) copy-start(bf16[512,1024]{1,0:T(8,128)(2,1)} %param.19) | copy-start | bytes 3145732
  1134.9 61.1 %copy-start.38 = (f32[1024]{0:T(1024)S(1)}, f32[1024]{0:T(1024)}, u32[]{:S(2)}) copy-start(f32[1024]{0:T(1024)} %param.31) | copy-start | bytes 12292
  1134.9 61.1 %copy-start.40 = (f32[512]{0:T(512)S(1)}, f32[512]{0:T(512)}, u32[]{:S(2)}) copy-start(f32[512]{0:T(512)} %copy-done.39) | copy-start | bytes 6148
  1134.9 141.8 %copy-start.11 = (bf16[512,1024]{1,0:T(8,128)(2,1)S(1)}, bf16[512,1024]{1,0:T(8,128)(2,1)}, u32[]{:S(2)}) copy-start(bf16[512,1024]{1,0:T(8,128)(2,1)} %reduce-scatter.9.cloned.1.call-done) | copy-start | bytes 3145732
  1134.9 141.8 %copy-start.35 = (f32[1024]{0:T(1024)S(1)}, f32[1024]{0:T(1024)}, u32[]{:S(2)}) copy-start(f32[1024]{0:T(1024)} %param.32) | copy-start | bytes 12292
  1134.9 141.8 %copy-start.37 = (f32[512]{0:T(512)S(1)}, f32[512]{0:T(512)}, u32[]{:S(2)}) copy-start(f32[512]{0:T(512)} %copy-done.36) | copy-start | bytes 6148
  (37 other events, 153.7 us)
Sparse Core Ops, SparseCore 0:
  11.7 83.4 all-gather.4
  96.7 79.2 all-gather.6
  323.0 142.9 reduce-scatter.4
  470.6 81.4 all-gather.8
  580.7 75.2 reduce-scatter.8
  662.4 81.2 all-gather.10
  1006.0 110.7 all-reduce.3
  1119.1 76.8 reduce-scatter.10
  1198.4 78.3 reduce-scatter.6
where the time goes:
time: 1300 us; the launch traced here: 1290 us
  waiting for transfers between devices  695 us (53%)
  matrix products  257 us (20%)
  local copies, waits for them, and re-layouts  141 us (11%)
  other arithmetic  119 us (9%)
  blocking collectives  46 us (4%)
  between operations  18.3 us (1%)
    reduce_scatter x1, waiting for transfers between devices, shards(): lax.psum_scatter(jnp.dot(attn_mixed, w_out, preferred_element_type=jnp.fl...  143 us
    psum x1, waiting for transfers between devices, shards(): lax.psum(grad_w_inner.astype(jnp.bfloat16), 'dp').astype(jnp.float32)  95.1 us
    dynamic_update_slice x16, local copies, waits for them, and re-layouts, attend_forward(): lax.map(one_block, jnp.arange(n_tokens // block_rows, dtype=jnp.int32))  93 us
    all_gather x1, waiting for transfers between devices, shards(): lax.all_gather((normed_one * gain_attn).astype(jnp.bfloat16), 'mp', axis=...  78.4 us
    all_gather x1, waiting for transfers between devices, shards(): lax.all_gather((normed_two * gain_mlp).astype(jnp.bfloat16), 'mp', axis=0...  77.7 us
    reduce_scatter x1, waiting for transfers between devices, shards(): lax.psum_scatter(jnp.einsum('tf,df->td', grad_gate_up, w_gate_up, preferr...  75 us
    all_gather x1, waiting for transfers between devices, shards(): first_all = lax.all_gather(first_in, 'mp', axis=0, tiled=True)  72.1 us
    all_gather x1, waiting for transfers between devices, shards(): lax.all_gather(grad_resid.astype(jnp.bfloat16), 'mp', axis=0, tiled=True)  65.8 us
  transfers between devices with their start and end apart: 9, of which 9 were waited for; matrix products, arithmetic and copies ran while one was open for 6% of the time, Pallas kernels for 0%

commit v1 on v0

--- a/solution.py
+++ b/solution.py
@@ -1,12 +1,16 @@
+import functools
 import math
 
 import jax
 import jax.numpy as jnp
 from jax import lax
+from jax.experimental import pallas as pl
+from jax.experimental.pallas import tpu as pltpu
 from jax.sharding import PartitionSpec as P
 
 HD = 64
 SEQ = 2048
+QB = 256
 
 
 norm_eps = 1e-06
@@ -49,85 +53,131 @@
     return inverse * (grad_normed - normed * jnp.mean(grad_normed * normed, axis=-1, keepdims=True))
 
 
-def block_mask(segment_ids, valid_tokens, row_first, seq_first, block_rows):
-    row_ids = lax.dynamic_slice_in_dim(segment_ids, row_first, block_rows, 0)
-    row_place = row_first + jnp.arange(block_rows, dtype=jnp.int32)
-    col_place = seq_first + jnp.arange(SEQ, dtype=jnp.int32)
-    allowed = (row_ids[:, None] == segment_ids[None, :]) & (
-        col_place[None, :] <= row_place[:, None]
-    )
-    return allowed & ((valid_tokens[None, :] == 1) | (col_place[None, :] == row_place[:, None]))
-
-
-def block_scores(queries, key_rows, segment_ids, valid_tokens, row_first, seq_first, block_rows):
-    q_block = lax.dynamic_slice_in_dim(queries, row_first, block_rows, 0)
-    scores = jnp.einsum(
-        "qhd,khd->hqk", q_block, key_rows, preferred_element_type=jnp.float32
-    ) * queries.shape[-1] ** (-0.5)
-    allowed = block_mask(segment_ids, valid_tokens, row_first, seq_first, block_rows)
-    return (q_block, key_rows, jnp.where(allowed[None], scores, -1e30), allowed)
-
-
-def attend_forward(queries, key_rows, blended, segment_ids, valid_tokens, block_rows):
-    n_tokens, n_heads, head_size = queries.shape
-
-    def one_block(block_index):
-        row_first = block_index * block_rows
-        seq_first = row_first // SEQ * SEQ
-        q_block, k_block, scores, allowed = block_scores(
-            queries, key_rows, segment_ids, valid_tokens, row_first, seq_first, block_rows
-        )
-        row_peak = jnp.max(scores, -1, keepdims=True)
-        exp_scores = jnp.exp(scores - row_peak)
-        totals = jnp.sum(exp_scores, -1, keepdims=True)
-        probs = (exp_scores / totals).astype(jnp.bfloat16)
-        out_block = jnp.einsum("hqk,khd->qhd", probs, blended, preferred_element_type=jnp.float32)
-        return (out_block, (row_peak + jnp.log(totals))[..., 0])
-
-    block_outs, logsum = lax.map(one_block, jnp.arange(n_tokens // block_rows, dtype=jnp.int32))
-    return (block_outs.reshape(n_tokens, n_heads, head_size), logsum)
-
-
-def attend_backward(
-    queries, key_rows, blended, grad_mixed, segment_ids, valid_tokens, logsum, block_rows
-):
-    n_tokens, n_heads, head_size = queries.shape
-    score_scale = head_size ** (-0.5)
-    empty = jnp.zeros((n_tokens, n_heads, head_size), jnp.float32)
-
-    def one_block(running, block_index):
-        grad_keys, grad_values = running
-        row_first = block_index * block_rows
-        seq_first = row_first // SEQ * SEQ
-        q_block, k_block, scores, allowed = block_scores(
-            queries, key_rows, segment_ids, valid_tokens, row_first, seq_first, block_rows
-        )
-        g_block = lax.dynamic_slice_in_dim(grad_mixed, row_first, block_rows, 0)
-        probs = jnp.where(allowed[None], jnp.exp(scores - logsum[block_index][..., None]), 0.0)
-        grad_probs = jnp.einsum(
-            "qhd,khd->hqk", g_block, blended, preferred_element_type=jnp.float32
-        )
-        row_inner = jnp.sum(grad_probs * probs, -1, keepdims=True)
-        grad_scores = (probs * (grad_probs - row_inner)).astype(jnp.bfloat16)
-        grad_q = (
-            jnp.einsum("hqk,khd->qhd", grad_scores, k_block, preferred_element_type=jnp.float32)
-            * score_scale
-        )
-        part_keys = (
-            jnp.einsum("hqk,qhd->khd", grad_scores, q_block, preferred_element_type=jnp.float32)
-            * score_scale
-        )
-        part_values = jnp.einsum(
-            "hqk,qhd->khd", probs.astype(jnp.bfloat16), g_block, preferred_element_type=jnp.float32
-        )
-        grad_keys = grad_keys + part_keys
-        grad_values = grad_values + part_values
-        return ((grad_keys, grad_values), grad_q)
-
-    (grad_keys, grad_values), grad_queries = lax.scan(
-        one_block, (empty, empty), jnp.arange(n_tokens // block_rows, dtype=jnp.int32)
-    )
-    return (grad_queries.reshape(n_tokens, n_heads, head_size), grad_keys, grad_values)
+def dot(a, b, ca, cb):
+    return lax.dot_general(a, b, (((ca,), (cb,)), ((), ())), preferred_element_type=jnp.float32)
+
+
+def pair_lane(shape, head):
+    lane = lax.broadcasted_iota(jnp.int32, shape, 1)
+    return (lane < 64) if head == 0 else (lane >= 64)
+
+
+def attend_kernel(order_ref, start_ref, q_ref, k_ref, v_ref, o_ref, lse_ref, *, pieces, rows):
+    z = order_ref[0]
+    subs = rows // QB
+    for j in range(pieces):
+        zj = jnp.bitwise_xor(z, j)
+        for sub in range(subs):
+            first = j * rows + sub * QB
+            q_pair = q_ref[zj, sub * QB:(sub + 1) * QB, :]
+            start = start_ref[0:1, first:first + QB]
+            q_pos = first + lax.broadcasted_iota(jnp.int32, (1, QB), 1)
+            outs = []
+            for head in range(2):
+                qm = jnp.where(pair_lane(q_pair.shape, head), q_pair, jnp.zeros_like(q_pair))
+                blocks = []
+                for i in range(j + 1):
+                    zi = jnp.bitwise_xor(z, i)
+                    n = rows if i < j else (sub + 1) * QB
+                    s = dot(k_ref[zi, :n, :], qm, 1, 1)
+                    k_pos = i * rows + lax.broadcasted_iota(jnp.int32, (n, QB), 0)
+                    keep = k_pos >= start
+                    if i == j:
+                        keep = keep & (k_pos <= q_pos)
+                    blocks.append((zi, n, jnp.where(keep, s, -1e30)))
+                peak = functools.reduce(jnp.maximum, [jnp.max(b[2], 0, keepdims=True) for b in blocks])
+                total = 0.0
+                acc = 0.0
+                for zi, n, s in blocks:
+                    p = jnp.exp(s - peak)
+                    total = total + jnp.sum(p, 0, keepdims=True)
+                    acc = acc + dot(v_ref[zi, :n, :], p.astype(jnp.bfloat16), 0, 0)
+                outs.append((acc / total)[head * 64:(head + 1) * 64])
+                lse_ref[0, head:head + 1, first:first + QB] = peak + jnp.log(total)
+            o_ref[zj, sub * QB:(sub + 1) * QB, :] = jnp.transpose(jnp.concatenate(outs, 0)).astype(o_ref.dtype)
+
+
+def attend(order, start, q, k, v, vmem=48 * 2**20):
+    pieces, rows, width = q.shape
+    pairs = width // 128
+    blk = pl.BlockSpec((pieces, rows, 128), lambda p, *_: (0, 0, p))
+    return pl.pallas_call(
+        functools.partial(attend_kernel, pieces=pieces, rows=rows),
+        grid_spec=pltpu.PrefetchScalarGridSpec(
+            num_scalar_prefetch=1, grid=(pairs,),
+            in_specs=[pl.BlockSpec((1, pieces * rows), lambda p, *_: (0, 0)), blk, blk, blk],
+            out_specs=[blk, pl.BlockSpec((1, 2, pieces * rows), lambda p, *_: (p, 0, 0))],
+        ),
+        out_shape=[jax.ShapeDtypeStruct(q.shape, jnp.bfloat16),
+                   jax.ShapeDtypeStruct((pairs, 2, pieces * rows), jnp.float32)],
+        compiler_params=pltpu.CompilerParams(vmem_limit_bytes=vmem),
+        cost_estimate=pl.CostEstimate(flops=2 * 2 * (pieces * rows)**2 * width, bytes_accessed=8 * pieces * rows * width, transcendentals=pieces * rows * pieces * rows * pairs),
+    )(order, start, q, k, v)
+
+
+def back_kernel(order_ref, start_ref, q_ref, k_ref, v_ref, o_ref, g_ref, lse_ref, dq_ref, dk_ref, dv_ref, acc_k, acc_v, *, pieces, rows):
+    z = order_ref[0]
+    subs = rows // QB
+    acc_k[...] = jnp.zeros_like(acc_k)
+    acc_v[...] = jnp.zeros_like(acc_v)
+    for j in range(pieces):
+        zj = jnp.bitwise_xor(z, j)
+        for sub in range(subs):
+            first = j * rows + sub * QB
+            here = slice(sub * QB, (sub + 1) * QB)
+            q_pair = q_ref[zj, here, :]
+            g_pair = g_ref[zj, here, :]
+            start = start_ref[0:1, first:first + QB]
+            q_pos = first + lax.broadcasted_iota(jnp.int32, (1, QB), 1)
+            inner = jnp.transpose(o_ref[zj, here, :].astype(jnp.float32) * g_pair.astype(jnp.float32))
+            outs = []
+            for head in range(2):
+                mine = pair_lane(q_pair.shape, head)
+                qm = jnp.where(mine, q_pair, jnp.zeros_like(q_pair))
+                gm = jnp.where(mine, g_pair, jnp.zeros_like(g_pair))
+                delta = jnp.sum(inner[head * 64:(head + 1) * 64], 0, keepdims=True)
+                lse = lse_ref[0, head:head + 1, first:first + QB]
+                acc = 0.0
+                for i in range(j + 1):
+                    zi = jnp.bitwise_xor(z, i)
+                    n = rows if i < j else (sub + 1) * QB
+                    k_blk = k_ref[zi, :n, :]
+                    s = dot(k_blk, qm, 1, 1)
+                    k_pos = i * rows + lax.broadcasted_iota(jnp.int32, (n, QB), 0)
+                    keep = k_pos >= start
+                    if i == j:
+                        keep = keep & (k_pos <= q_pos)
+                    p = jnp.exp(jnp.where(keep, s, -1e30) - lse)
+                    dp = dot(v_ref[zi, :n, :], gm, 1, 1)
+                    ds = (p * (dp - delta)).astype(jnp.bfloat16)
+                    acc_v[i, :n, :] += dot(p.astype(jnp.bfloat16), gm, 1, 0)
+                    acc_k[i, :n, :] += dot(ds, qm, 1, 0)
+                    acc = acc + dot(k_blk, ds, 0, 0)
+                outs.append(acc[head * 64:(head + 1) * 64])
+            dq_ref[zj, here, :] = (jnp.transpose(jnp.concatenate(outs, 0)) * 0.125).astype(dq_ref.dtype)
+    for j in range(pieces):
+        zj = jnp.bitwise_xor(z, j)
+        dk_ref[zj] = acc_k[j].astype(dk_ref.dtype)
+        dv_ref[zj] = acc_v[j].astype(dv_ref.dtype)
+
+
+def attend_back(order, start, q, k, v, o, g, lse, vmem=48 * 2**20, dt=jnp.bfloat16):
+    pieces, rows, width = q.shape
+    pairs = width // 128
+    blk = pl.BlockSpec((pieces, rows, 128), lambda p, *_: (0, 0, p))
+    return pl.pallas_call(
+        functools.partial(back_kernel, pieces=pieces, rows=rows),
+        grid_spec=pltpu.PrefetchScalarGridSpec(
+            num_scalar_prefetch=1, grid=(pairs,),
+            in_specs=[pl.BlockSpec((1, pieces * rows), lambda p, *_: (0, 0)), blk, blk, blk, blk, blk,
+                      pl.BlockSpec((1, 2, pieces * rows), lambda p, *_: (p, 0, 0))],
+            out_specs=[blk, blk, blk],
+            scratch_shapes=[pltpu.VMEM((pieces, rows, 128), jnp.float32)] * 2,
+        ),
+        out_shape=[jax.ShapeDtypeStruct(q.shape, dt)] * 3,
+        compiler_params=pltpu.CompilerParams(vmem_limit_bytes=vmem),
+        cost_estimate=pl.CostEstimate(flops=2 * 5 * (pieces * rows)**2 * width, bytes_accessed=20 * pieces * rows * width, transcendentals=pieces * rows * pieces * rows * pairs),
+    )(order, start, q, k, v, o, g, lse)
 
 
 def shards(
@@ -152,7 +202,6 @@
     head_cols = w_query.shape[1]
     local_heads = head_cols // HD
     ffn_cols = w_gate.shape[1]
-    block_rows = min(512, SEQ)
     places = token_places(segment_ids)
     live_rows = valid_tokens.astype(jnp.float32)[:, None]
     x_float = hidden_in.astype(jnp.float32)
@@ -175,11 +224,12 @@
     blended = (0.5 * projected[:, 2 * head_cols :] + 0.5 * first_values.astype(jnp.float32)).astype(
         jnp.bfloat16
     )
-    blend_heads = blended.reshape(n_tokens, local_heads, HD)
-    attended, logsum = attend_forward(
-        queries, key_rows, blend_heads, segment_ids, valid_tokens, block_rows
-    )
-    attn_mixed = (attended.reshape(n_tokens, head_cols) * live_rows).astype(jnp.bfloat16)
+    first_key = jnp.where(valid_tokens == 1, jnp.arange(n_tokens, dtype=jnp.int32) - places, jnp.arange(n_tokens, dtype=jnp.int32))[None]
+    order = jnp.zeros((1,), jnp.int32)
+    cut = lambda a: a.reshape(4, n_tokens // 4, head_cols)
+    q_cut, k_cut, v_cut = cut(queries * jnp.bfloat16(0.125)), cut(key_rows), cut(blended)
+    attended, logsum = attend(order, first_key, q_cut, k_cut, v_cut)
+    attn_mixed = (attended.reshape(n_tokens, head_cols).astype(jnp.float32) * live_rows).astype(jnp.bfloat16)
     residual = x_float + lax.psum_scatter(
         jnp.dot(attn_mixed, w_out, preferred_element_type=jnp.float32),
         "mp",
@@ -241,16 +291,11 @@
         "td,wd->tw", grad_attn_all, w_out, preferred_element_type=jnp.float32
     ).astype(jnp.bfloat16)
     grad_mixed = (grad_attn_rounded.astype(jnp.float32) * live_rows).astype(jnp.bfloat16)
-    grad_queries, grad_keys, grad_values = attend_backward(
-        queries,
-        key_rows,
-        blend_heads,
-        grad_mixed.reshape(n_tokens, local_heads, HD),
-        segment_ids,
-        valid_tokens,
-        logsum,
-        block_rows,
-    )
+    grad_queries, grad_keys, grad_values = attend_back(
+        order, first_key, q_cut, k_cut, v_cut, attended, cut(grad_mixed), logsum
+    )
+    grad_queries = grad_queries.astype(jnp.float32).reshape(n_tokens, local_heads, HD)
+    grad_keys = grad_keys.astype(jnp.float32).reshape(n_tokens, local_heads, HD)
     grad_blend = grad_values.reshape(n_tokens, head_cols).astype(jnp.bfloat16)
     grad_half = (grad_blend.astype(jnp.float32) * 0.5).astype(jnp.bfloat16)
     grad_query_pre = (

time: 1300 us -> 999 us (0.77)
  matrix products: 257 us -> 89.9 us
  other arithmetic: 119 us -> 33 us
  local copies, waits for them, and re-layouts: 141 us -> 55.1 us
  Pallas kernels: 0 us -> 49.9 us
    dot_general x28 -> x0, matrix products: 167 us -> none  [the longest x8 42.8 us: block_scores(): jnp.einsum('qhd,khd->hqk', q_block, key_rows, preferred_element_type=jnp....]
    dynamic_update_slice x16 -> x0, local copies, waits for them, and re-layouts: 93 us -> none  [attend_forward(): lax.map(one_block, jnp.arange(n_tokens // block_rows, dtype=jnp.int32))]
    pallas_call x0 -> x2, Pallas kernels: none -> 49.9 us  [the longest x1 28.7 us: attend_back(): pl.pallas_call(functools.partial(back_kernel, pieces=pieces, rows=rows),...]
    convert_element_type x5 -> x1, other arithmetic: 38.1 us -> 0.34 us  [shards(): (attended.reshape(n_tokens, head_cols).astype(jnp.float32) * live_rows).a...]
    and x8 -> x0, other arithmetic: 25.3 us -> none  [block_mask(): allowed & ((valid_tokens[None, :] == 1) | (col_place[None, :] == row_plac...]
    reduce_sum x4 -> x0, other arithmetic: 17.3 us -> none  [one_block(): totals = jnp.sum(exp_scores, -1, keepdims=True)]
  transfers between devices with their start and end apart: 9 -> 9, of which waited for: 9 -> 9; matrix products, arithmetic and copies ran while one was open for 6% -> 7% of each run, Pallas kernels for 0% -> 0%
where the time goes in v1:
time: 999 us; the launch traced here: 991 us
  waiting for transfers between devices  687 us (69%)
  matrix products  89.9 us (9%)
  local copies, waits for them, and re-layouts  55.1 us (6%)
  Pallas kernels  49.9 us (5%)
  blocking collectives  45.7 us (5%)
  other arithmetic  33 us (3%)
  between operations  18.1 us (2%)
  starting transfers between devices  12.9 us (1%)
    reduce_scatter x1, waiting for transfers between devices, shards(): lax.psum_scatter(jnp.dot(attn_mixed, w_out, preferred_element_type=jnp.fl...  131 us
    psum x1, waiting for transfers between devices, shards(): lax.psum(grad_w_inner.astype(jnp.bfloat16), 'dp').astype(jnp.float32)  96.3 us
    all_gather x1, waiting for transfers between devices, shards(): lax.all_gather((normed_one * gain_attn).astype(jnp.bfloat16), 'mp', axis=...  79.1 us
    all_gather x1, waiting for transfers between devices, shards(): lax.all_gather((normed_two * gain_mlp).astype(jnp.bfloat16), 'mp', axis=0...  77.7 us
    reduce_scatter x1, waiting for transfers between devices, shards(): lax.psum_scatter(jnp.einsum('tf,df->td', grad_gate_up, w_gate_up, preferr...  75.4 us
    all_gather x1, waiting for transfers between devices, shards(): first_all = lax.all_gather(first_in, 'mp', axis=0, tiled=True)  72.1 us
    all_gather x1, waiting for transfers between devices, shards(): lax.all_gather(grad_resid.astype(jnp.bfloat16), 'mp', axis=0, tiled=True)  65.8 us
    reduce_scatter x1, waiting for transfers between devices, shards(): lax.psum_scatter(jnp.einsum('tc,dc->td', grad_projected, w_inner, preferr...  59.4 us
  transfers between devices with their start and end apart: 9, of which 9 were waited for; matrix products, arithmetic and copies ran while one was open for 7% of the time, Pallas kernels for 0%

profile of v1, /device:TPU:0, one launch (start us, length us, event | category | flops | bytes accessed | tf_op | source)
XLA Modules:
  0.0 991.4 jit_solution(402041757958381543)
XLA Ops:
  16.6 79.1 %all-gather.5.cloned.1.call-done = bf16[2048,1024]{1,0:T(8,128)(2,1)} async-done(((bf16[512,1024]{1,0:T(8,128)(2,1)}), bf16[2048,1024]{1,0:T(8,128)(2,1)}) %all-gather.5.cloned.1.call-update) | async-done | bytes 4194320 | tf_op jit(solution)/shard_map/all_gather | solution.py:209
  95.7 8.8 fusion.40
  104.6 72.1 %all-gather.7.cloned.1.call-done = bf16[2048,1024]{1,0:T(8,128)(2,1)} async-done(((bf16[512,1024]{1,0:T(8,128)(2,1)}), bf16[2048,1024]{1,0:T(8,128)(2,1)}) %all-gather.7.cloned.1.call-update) | async-done | bytes 4194320 | tf_op jit(solution)/shard_map/all_gather | solution.py:220
  176.6 7.6 multiply_reduce_fusion
  196.2 21.1 %shard_map.254 = (bf16[4,512,256]{2,1,0:T(8,128)(2,1)S(1)}, f32[2,2,2048]{2,1,0:T(2,128)S(1)}) custom-call(s32[1]{0:T(128)} %constant.18.clone.1.order_ref, s32[1,2048]{1,0:T(1,128)S(1)} %bitcast.57, bf16[4,512,256]{2,1,0:T(8,128)(2,1)S(1)} %copy.40.q_ref, bf16[4,512,256]{2,1,0:T(8,128)(2,1)S(1)} %copy.41.k_ref, bf16[4,512,256]{2,1,0:T(8,128)(2,1)S(1)} %bitcast.56), custom_call_target="tpu_custom_call" | custom-call | flops 4294967296 | bytes 4194304 | tf_op jit(solution)/shard_map/pallas_call | solution.py:104
  224.2 12.3 %all-gather.9.cloned.1.call-start = ((), (), s32[]{:S(2)}) async-start(), calls=%async_computation.7 | async-start | bytes 5242880 | tf_op jit(solution)/shard_map/all_gather | solution.py:240
  236.6 130.8 %reduce-scatter.5.cloned.1.call-done = f32[512,1024]{1,0:T(8,128)} async-done(((f32[2048,1024]{1,0:T(8,128)}), f32[512,1024]{1,0:T(8,128)}) %reduce-scatter.5.cloned.1.call-update) | async-done | bytes 2097168 | tf_op jit(solution)/shard_map/reduce_scatter | solution.py:233
  375.0 77.7 %all-gather.9.cloned.1.call-done = bf16[2048,1024]{1,0:T(8,128)(2,1)} async-done(((bf16[512,1024]{1,0:T(8,128)(2,1)}), bf16[2048,1024]{1,0:T(8,128)(2,1)}) %all-gather.9.cloned.1.call-update) | async-done | bytes 4194320 | tf_op jit(solution)/shard_map/all_gather | solution.py:240
  452.7 9.0 fusion.42
  461.8 6.6 fusion.2
  470.9 10.1 %convolution_convert_fusion.1 = bf16[2048,1024]{1,0:T(8,128)(2,1)} fusion(bf16[1024,1408]{0,1:T(8,128)(2,1)} %constant_dynamic-update-slice_fusion.3, bf16[2048,704]{0,1:T(8,128)(2,1)S(1)} %get-tuple-element.70, bf16[2048,704]{0,1:T(8,128)(2,1)S(1)} %get-tuple-element.69), kind=kOutput, calls=%fused_computation.11 | convolution fusion | flops 5919211520 | bytes 12845056 | tf_op jit(solution)/shard_map/tf,df->td/dot_general | solution.py:277
  481.1 75.4 %reduce-scatter.9.cloned.1.call-done = bf16[512,1024]{1,0:T(8,128)(2,1)} async-done(((bf16[2048,1024]{1,0:T(8,128)(2,1)}), bf16[512,1024]{1,0:T(8,128)(2,1)}) %reduce-scatter.9.cloned.1.call-update) | async-done | bytes 1048592 | tf_op jit(solution)/shard_map/reduce_scatter | solution.py:276
  562.7 7.5 convolution_convert_fusion.8
  570.2 8.1 convolution_convert_fusion
  578.3 65.8 %all-gather.11.cloned.1.call-done = bf16[2048,1024]{1,0:T(8,128)(2,1)} async-done(((bf16[512,1024]{1,0:T(8,128)(2,1)}), bf16[2048,1024]{1,0:T(8,128)(2,1)}) %all-gather.11.cloned.1.call-update) | async-done | bytes 4194320 | tf_op jit(solution)/shard_map/all_gather | solution.py:286
  648.7 28.7 %shard_map.255 = (bf16[4,512,256]{2,1,0:T(8,128)(2,1)S(1)}, bf16[4,512,256]{2,1,0:T(8,128)(2,1)S(1)}, bf16[4,512,256]{2,1,0:T(8,128)(2,1)S(1)}) custom-call(s32[1]{0:T(128)} %constant.18.clone.1.order_ref, s32[1,2048]{1,0:T(1,128)S(1)} %bitcast.58, bf16[4,512,256]{2,1,0:T(8,128)(2,1)S(1)} %copy-done.2, bf16[4,512,256]{2,1,0:T(8,128)(2,1)S(1)} %copy-done.4, ...), custom_call_target="tpu_custom_call" | custom-call | flops 10737418240 | bytes 10485760 | tf_op jit(solution)/shard_map/pallas_call | solution.py:168
  702.7 4.7 convolution_convert_fusion.7
  707.7 7.2 convolution_convert_fusion.3
  715.0 7.0 convolution_convert_fusion.2
  722.0 96.3 %all-reduce.4.cloned.1.call-done = (bf16[1024,768]{1,0:T(8,128)(2,1)}, bf16[1024,256]{0,1:T(8,128)(2,1)}, bf16[1024,1408]{1,0:T(8,128)(2,1)}, bf16[256,1024]{1,0:T(8,128)(2,1)}, bf16[704,1024]{1,0:T(8,128)(2,1)}) async-done(((bf16[1024,768]{1,0:T(8,128)(2,1)}, bf16[1024,256]{0,1:T(8,128)(2,1)}, bf16[1024,1408]{1,0:T(8,128)(2,1)}, bf16[256,1024]{1,0:T(8,128)(2,1)}, bf16[704,1024]{1,0:T(8,128)(2,1)}), ...) | async-done | bytes 6946832 | tf_op jit(solution)/shard_map/psum | solution.py:323
  818.3 5.2 fusion.38
  838.2 59.4 %reduce-scatter.11.cloned.1.call-done = bf16[512,1024]{1,0:T(8,128)(2,1)} async-done(((bf16[2048,1024]{1,0:T(8,128)(2,1)}), bf16[512,1024]{1,0:T(8,128)(2,1)}) %reduce-scatter.11.cloned.1.call-update) | async-done | bytes 1048592 | tf_op jit(solution)/shard_map/reduce_scatter | solution.py:309
  900.5 45.7 %all-reduce = (f32[1024]{0:T(1024)}, f32[1024]{0:T(1024)}, f32[]{:T(128)}, f32[]{:T(128)}) all-reduce(f32[1024]{0:T(1024)} %get-tuple-element.54, f32[1024]{0:T(1024)} %get-tuple-element.52, f32[]{:T(128)} %get-tuple-element.89, f32[]{:T(128)} %get-tuple-element.65), channel_id=1, replica_groups=mesh['dp'=8,'mp'=4] {'dp','mp'}, use_global_device_ids=true, to_apply=%region_16.17 | all-reduce | flops 2050 | bytes 16400 | tf_op jit(solution)/shard_map/psum | solution.py:331
  948.7 29.6 %reduce-scatter.7.cloned.1.call-done = bf16[512,1024]{1,0:T(8,128)(2,1)} async-done(((bf16[2048,1024]{1,0:T(8,128)(2,1)}), bf16[512,1024]{1,0:T(8,128)(2,1)}) %reduce-scatter.7.cloned.1.call-update) | async-done | bytes 1048592 | tf_op jit(solution)/shard_map/reduce_scatter | solution.py:250
  (170 shorter events, 97.6 us)
Async XLA Ops:
  7.2 454.6 %copy-start = (bf16[704,1024]{1,0:T(8,128)(2,1)S(1)}, bf16[704,1024]{1,0:T(8,128)(2,1)}, u32[]{:S(2)}) copy-start(bf16[704,1024]{1,0:T(8,128)(2,1)} %param.26) | copy-start | bytes 4325380
  7.2 88.5 %all-gather.5.cloned.1.call-start = ((), (), s32[]{:S(2)}) async-start(), calls=%async_computation.4 | async-start | bytes 5242880 | tf_op jit(solution)/shard_map/all_gather | solution.py:209
  12.1 164.6 %all-gather.7.cloned.1.call-start = ((), (), s32[]{:S(2)}) async-start(), calls=%async_computation.5 | async-start | bytes 5242880 | tf_op jit(solution)/shard_map/all_gather | solution.py:220
  12.8 354.5 %reduce-scatter.5.cloned.1.call-start = ((), (), s32[]{:S(2)}) async-start(), calls=%async_computation.6 | async-start | bytes 10485760 | tf_op jit(solution)/shard_map/reduce_scatter | solution.py:233
  13.8 203.5 %copy-start.36 = (f32[2048]{0:T(1024)}, f32[2048]{0:T(1024)S(1)}, u32[]{:S(2)}) copy-start(f32[2048]{0:T(1024)S(1)} %get-tuple-element.99) | copy-start | bytes 24580
  16.6 167.6 %copy-start.19 = (f32[2048,32]{0,1:T(8,128)}, f32[2048,32]{0,1:T(8,128)S(1)}, u32[]{:S(2)}) copy-start(f32[2048,32]{0,1:T(8,128)S(1)} %get-tuple-element.96) | copy-start | bytes 786436
  16.6 160.0 %copy-start.25 = (bf16[1024,256]{1,0:T(8,128)(2,1)S(1)}, bf16[1024,256]{1,0:T(8,128)(2,1)}, u32[]{:S(2)}) copy-start(bf16[1024,256]{1,0:T(8,128)(2,1)} %param.22) | copy-start | bytes 1572868
  192.3 25.0 %copy-start.3 = (bf16[4,512,256]{2,1,0:T(8,128)(2,1)}, bf16[4,512,256]{2,1,0:T(8,128)(2,1)S(1)}, u32[]{:S(2)}) copy-start(bf16[4,512,256]{2,1,0:T(8,128)(2,1)S(1)} %copy.41.k_ref) | copy-start | bytes 3145732
  196.2 23.5 %copy-start.26 = (bf16[256,1024]{1,0:T(8,128)(2,1)S(1)}, bf16[256,1024]{1,0:T(8,128)(2,1)}, u32[]{:S(2)}) copy-start(bf16[256,1024]{1,0:T(8,128)(2,1)} %param.23) | copy-start | bytes 1572868
  224.2 145.4 %copy-start.34 = (f32[1024]{0:T(1024)S(1)}, f32[1024]{0:T(1024)}, u32[]{:S(2)}) copy-start(f32[1024]{0:T(1024)} %param.28) | copy-start | bytes 12292
  224.2 228.5 %all-gather.9.cloned.1.call-start = ((), (), s32[]{:S(2)}) async-start(), calls=%async_computation.7 | async-start | bytes 5242880 | tf_op jit(solution)/shard_map/all_gather | solution.py:240
  369.6 189.6 %copy-start.11 = (f32[512,1024]{1,0:T(8,128)}, f32[512,1024]{1,0:T(8,128)S(1)}, u32[]{:S(2)}) copy-start(f32[512,1024]{1,0:T(8,128)S(1)} %get-tuple-element.68) | copy-start | bytes 6291460
  371.1 185.4 %reduce-scatter.9.cloned.1.call-start = ((), (), s32[]{:S(2)}) async-start(), calls=%async_computation.9 | async-start | bytes 5242880 | tf_op jit(solution)/shard_map/reduce_scatter | solution.py:276
  452.7 9.0 copy-start.22
  481.1 163.0 %all-gather.11.cloned.1.call-start = ((), (), s32[]{:S(2)}) async-start(), calls=%async_computation.10 | async-start | bytes 5242880 | tf_op jit(solution)/shard_map/all_gather | solution.py:286
  562.6 255.7 %all-reduce.4.cloned.1.call-start = ((), (), s32[]{:S(2)}) async-start(), calls=%async_computation.12 | async-start | bytes 13893632 | tf_op jit(solution)/shard_map/psum | solution.py:323
  562.7 7.5 copy-start.44
  570.2 73.9 %copy-start.27 = (bf16[256,1024]{1,0:T(8,128)(2,1)S(1)}, bf16[256,1024]{1,0:T(8,128)(2,1)}, u32[]{:S(2)}) copy-start(bf16[256,1024]{1,0:T(8,128)(2,1)} %param.23) | copy-start | bytes 1572868
  570.2 73.9 %copy-start.37 = (f32[2048]{0:T(1024)S(1)}, f32[2048]{0:T(1024)}, u32[]{:S(2)}) copy-start(f32[2048]{0:T(1024)} %copy-done.36) | copy-start | bytes 24580
  707.4 190.1 %reduce-scatter.11.cloned.1.call-start = ((), (), s32[]{:S(2)}) async-start(), calls=%async_computation.11 | async-start | bytes 5242880 | tf_op jit(solution)/shard_map/reduce_scatter | solution.py:309
  715.0 263.3 %reduce-scatter.7.cloned.1.call-start = ((), (), s32[]{:S(2)}) async-start(), calls=%async_computation.8 | async-start | bytes 5242880 | tf_op jit(solution)/shard_map/reduce_scatter | solution.py:250
  834.8 62.7 %copy-start.35 = (f32[1024]{0:T(1024)S(1)}, f32[1024]{0:T(1024)}, u32[]{:S(2)}) copy-start(f32[1024]{0:T(1024)} %param.27) | copy-start | bytes 12292
  834.8 62.7 %copy-start.40 = (f32[512]{0:T(512)S(1)}, f32[512]{0:T(512)}, u32[]{:S(2)}) copy-start(f32[512]{0:T(512)} %copy-done.39) | copy-start | bytes 6148
  834.8 143.4 %copy-start.12 = (f32[512,1024]{1,0:T(8,128)S(1)}, f32[512,1024]{1,0:T(8,128)}, u32[]{:S(2)}) copy-start(f32[512,1024]{1,0:T(8,128)} %copy-done.11) | copy-start | bytes 6291460
  (35 other events, 111.5 us)
Sparse Core Ops, SparseCore 0:
  12.2 83.4 all-gather.4
  97.3 79.2 all-gather.6
  224.3 143.0 reduce-scatter.4
  371.2 81.4 all-gather.8
  481.2 75.2 reduce-scatter.8
  562.8 81.2 all-gather.10
  707.6 110.7 all-reduce.3
  820.6 76.8 reduce-scatter.10
  899.9 78.3 reduce-scatter.6

commit v2 on v0

v2 whole, which is shorter than its diff:
```python
import functools
import math

import jax
import jax.numpy as jnp
from jax import lax
from jax.experimental import pallas as pl
from jax.experimental.pallas import tpu as pltpu
from jax.sharding import PartitionSpec as P

HD = 64
norm_eps = 1e-06


def token_places(segment_ids):
    n_tokens = segment_ids.shape[0]
    indices = jnp.arange(n_tokens, dtype=jnp.int32)
    starts_new = jnp.concatenate([jnp.ones((1,), jnp.bool_), segment_ids[1:] != segment_ids[:-1]])
    begins = lax.cummax(jnp.where(starts_new, indices, jnp.zeros_like(indices)), axis=0)
    return indices - begins


QB = 256
VMEM = 48 * 2**20


def dot(a, b, ca, cb):
    return lax.dot_general(a, b, (((ca,), (cb,)), ((), ())), preferred_element_type=jnp.float32)


def lane_of(shape):
    return lax.broadcasted_iota(jnp.int32, shape, 1)


def turned(values, cosine, sine):
    near = lane_of(values.shape) % HD < HD // 2
    swapped = jnp.where(near, pltpu.roll(values, 128 - HD // 2, 1), pltpu.roll(values, HD // 2, 1))
    return values * cosine + swapped * sine


def project_kernel(h_ref, first_ref, w_ref, cos_ref, sin_ref, out_ref, power_ref):
    h, first = h_ref[...], first_ref[...]
    cosine, sine = cos_ref[...], sin_ref[...]
    at = pl.program_id(0)

    @pl.when(at == 0)
    def _():
        power_ref[...] = jnp.zeros_like(power_ref)

    for half in range(2):
        base = half * 512
        qkv = dot(h, w_ref[:, base : base + 384], 1, 0)
        raw = dot(first, w_ref[:, base + 384 : base + 512], 1, 0).astype(jnp.bfloat16).astype(jnp.float32)
        out_ref[half, :, 0:128] = turned(qkv[:, 0:128], cosine, sine).astype(jnp.bfloat16) * jnp.bfloat16(0.125)
        out_ref[half, :, 128:256] = turned(qkv[:, 128:256], cosine, sine).astype(jnp.bfloat16)
        blend = (0.5 * qkv[:, 256:384] + 0.5 * raw).astype(jnp.bfloat16)
        out_ref[half, :, 256:384] = blend
        blend = blend.astype(jnp.float32)
        power_ref[0:1, :] += jnp.sum(raw * raw, 0, keepdims=True)
        power_ref[1:2, :] += jnp.sum(blend * blend, 0, keepdims=True)


def project(h, first, weight, cosine, sine):
    n, width = h.shape
    rows = n // 2
    subs = rows // QB
    return pl.pallas_call(
        project_kernel,
        grid=(n // QB,),
        in_specs=[
            pl.BlockSpec((QB, width), lambda i: (i, 0)),
            pl.BlockSpec((QB, width), lambda i: (i, 0)),
            pl.BlockSpec(weight.shape, lambda i: (0, 0)),
            pl.BlockSpec((QB, 128), lambda i: (i, 0)),
            pl.BlockSpec((QB, 128), lambda i: (i, 0)),
        ],
        out_specs=[
            pl.BlockSpec((2, QB, 384), lambda i: (i // subs, i % subs, 0)),
            pl.BlockSpec((8, 128), lambda i: (0, 0)),
        ],
        out_shape=[
            jax.ShapeDtypeStruct((4, rows, 384), jnp.bfloat16),
            jax.ShapeDtypeStruct((8, 128), jnp.float32),
        ],
        compiler_params=pltpu.CompilerParams(vmem_limit_bytes=VMEM),
        cost_estimate=pl.CostEstimate(
            flops=2 * n * width * 1024, bytes_accessed=2 * width * (2 * n + 1024), transcendentals=0
        ),
    )(h, first, weight, cosine, sine)


def causal(scores, start, q_pos, i, rows, last):
    k_pos = i * rows + lax.broadcasted_iota(jnp.int32, scores.shape, 0)
    keep = k_pos >= start
    if last:
        keep = keep & (k_pos <= q_pos)
    return jnp.where(keep, scores, -1e30)


def attend_kernel(start_ref, q_ref, k_ref, v_ref, o_ref, lse_ref, *, pieces, rows):
    for j in range(pieces):
        for sub in range(rows // QB):
            first = j * rows + sub * QB
            q_pair = q_ref[j, sub * QB : (sub + 1) * QB, :]
            start = start_ref[0:1, first : first + QB]
            q_pos = first + lane_of((1, QB))
            outs = []
            for head in range(2):
                mine = lane_of(q_pair.shape) // HD == head
                qm = jnp.where(mine, q_pair, jnp.zeros_like(q_pair))
                blocks = []
                for i in range(j + 1):
                    n = rows if i < j else (sub + 1) * QB
                    s = dot(k_ref[i, :n, :], qm, 1, 1)
                    blocks.append((i, n, causal(s, start, q_pos, i, rows, i == j)))
                peak = functools.reduce(jnp.maximum, [jnp.max(b[2], 0, keepdims=True) for b in blocks])
                total = 0.0
                acc = 0.0
                for i, n, s in blocks:
                    p = jnp.exp(s - peak)
                    total = total + jnp.sum(p, 0, keepdims=True)
                    acc = acc + dot(v_ref[i, :n, :], p.astype(jnp.bfloat16), 0, 0)
                outs.append((acc / total)[head * HD : (head + 1) * HD])
                lse_ref[head : head + 1, first : first + QB] = peak + jnp.log(total)
            o_ref[j, sub * QB : (sub + 1) * QB, :] = jnp.transpose(jnp.concatenate(outs, 0)).astype(o_ref.dtype)


def column(pieces, rows, at):
    return pl.BlockSpec((pieces, rows, 128), lambda _: (0, 0, at))


def whole(shape):
    return pl.BlockSpec(shape, lambda _: (0,) * len(shape))


def attend(start, qkv):
    pieces, rows, _ = qkv.shape
    n = pieces * rows
    return pl.pallas_call(
        functools.partial(attend_kernel, pieces=pieces, rows=rows),
        grid=(1,),
        in_specs=[whole((1, n))] + [column(pieces, rows, i) for i in range(3)],
        out_specs=[whole((pieces, rows, 128)), whole((2, n))],
        out_shape=[
            jax.ShapeDtypeStruct((pieces, rows, 128), jnp.bfloat16),
            jax.ShapeDtypeStruct((2, n), jnp.float32),
        ],
        compiler_params=pltpu.CompilerParams(vmem_limit_bytes=VMEM),
        cost_estimate=pl.CostEstimate(flops=8 * n * n * 128, bytes_accessed=8 * n * 128, transcendentals=n * n),
    )(start, qkv, qkv, qkv)


def back_kernel(
    start_ref, q_ref, k_ref, v_ref, o_ref, g_ref, lse_ref, flat_ref, cos_ref, sin_ref, d_ref, acc_k, acc_v, *, pieces, rows
):
    acc_k[...] = jnp.zeros_like(acc_k)
    acc_v[...] = jnp.zeros_like(acc_v)
    low = HD // 2
    for j in range(pieces):
        for sub in range(rows // QB):
            first = j * rows + sub * QB
            here = slice(sub * QB, (sub + 1) * QB)
            q_pair = q_ref[j, here, :]
            g_pair = g_ref[j, here, :]
            start = start_ref[0:1, first : first + QB]
            q_pos = first + lane_of((1, QB))
            inner = jnp.transpose(o_ref[j, here, :].astype(jnp.float32) * g_pair.astype(jnp.float32))
            cosine = flat_ref[0, :, first : first + QB]
            sine = flat_ref[1, :, first : first + QB]
            outs = []
            for head in range(2):
                mine = lane_of(q_pair.shape) // HD == head
                qm = jnp.where(mine, q_pair, jnp.zeros_like(q_pair))
                gm = jnp.where(mine, g_pair, jnp.zeros_like(g_pair))
                delta = jnp.sum(inner[head * HD : (head + 1) * HD], 0, keepdims=True)
                lse = lse_ref[head : head + 1, first : first + QB]
                acc = 0.0
                for i in range(j + 1):
                    n = rows if i < j else (sub + 1) * QB
                    k_blk = k_ref[i, :n, :]
                    s = causal(dot(k_blk, qm, 1, 1), start, q_pos, i, rows, i == j)
                    p = jnp.exp(s - lse)
                    dp = dot(v_ref[i, :n, :], gm, 1, 1)
                    ds = (p * (dp - delta)).astype(jnp.bfloat16)
                    acc_v[i, :n, :] += dot(p.astype(jnp.bfloat16), gm, 1, 0)
                    acc_k[i, :n, :] += dot(ds, qm, 1, 0)
                    acc = acc + dot(k_blk, ds, 0, 0)
                near = acc[head * HD : head * HD + low] * 0.125
                far = acc[head * HD + low : (head + 1) * HD] * 0.125
                outs += [near * cosine + far * sine, far * cosine - near * sine]
            d_ref[j, here, 0:128] = jnp.transpose(jnp.concatenate(outs, 0)).astype(d_ref.dtype)
    for j in range(pieces):
        here = slice(j * rows, (j + 1) * rows)
        d_ref[j, :, 128:256] = turned(acc_k[j], cos_ref[here, :], -sin_ref[here, :]).astype(d_ref.dtype)
        d_ref[j, :, 256:384] = acc_v[j].astype(d_ref.dtype) * jnp.bfloat16(0.5)


def attend_back(start, qkv, o, g, lse, flat, cosine, sine):
    pieces, rows, _ = qkv.shape
    n = pieces * rows
    one = whole((pieces, rows, 128))
    return pl.pallas_call(
        functools.partial(back_kernel, pieces=pieces, rows=rows),
        grid=(1,),
        in_specs=[whole((1, n))]
        + [column(pieces, rows, i) for i in range(3)]
        + [one, one, whole((2, n)), whole(flat.shape), whole((n, 128)), whole((n, 128))],
        out_specs=whole((pieces, rows, 384)),
        scratch_shapes=[pltpu.VMEM((pieces, rows, 128), jnp.float32)] * 2,
        out_shape=jax.ShapeDtypeStruct((pieces, rows, 384), jnp.bfloat16),
        compiler_params=pltpu.CompilerParams(vmem_limit_bytes=VMEM),
        cost_estimate=pl.CostEstimate(flops=20 * n * n * 128, bytes_accessed=20 * n * 128, transcendentals=n * n),
    )(start, qkv, qkv, qkv, o, g, lse, flat, cosine, sine)


def moved(values, bit):
    return lax.ppermute(values, "dp", [(i, i ^ bit) for i in range(lax.axis_size("dp"))])


def cross_pairs(n_dp):
    pairs = []
    for d in range(n_dp):
        for z in range(4):
            pairs.append((d * 4 + z, d * 4 + (z ^ 1) if z // 2 == d % 2 else (d ^ 1) * 4 + (z ^ 2)))
    return pairs


def side_pairs(n_dp):
    return [(d * 4 + z, d * 4 + (z ^ 1)) for d in range(n_dp) for z in range(4) if z // 2 != d % 2]


def tied(values, *others):
    return lax.optimization_barrier((values, others))[0]


class Place:
    def __init__(self):
        self.n_dp = lax.axis_size("dp")
        self.slots = self.n_dp // 2
        self.d = lax.axis_index("dp")
        self.z = lax.axis_index("mp")
        self.core = self.d % 2
        self.slot = self.d // 2
        self.own = (self.z // 2) == self.core
        self.even = (self.z % 2) == 0
        self.sides = [[2 * i + c for i in range(self.slots)] for c in range(2)]

    def cross(self, values):
        return lax.ppermute(values, ("dp", "mp"), cross_pairs(self.n_dp))

    def side(self, values):
        return lax.ppermute(values, ("dp", "mp"), side_pairs(self.n_dp))

    def ordered(self, mine, other):
        return jnp.where(self.core == 0, jnp.concatenate([mine, other], 0), jnp.concatenate([other, mine], 0))

    def slice_of(self, weight):
        rows = weight.shape[0] // self.slots
        return lax.dynamic_slice_in_dim(weight, self.slot * rows, rows, 0)

    def quarters(self, part):
        got = self.cross(part)
        far = self.side(got)
        first = jnp.where(self.own, part, got)
        second = jnp.where(self.own, got, far)
        return jnp.where(self.even, first, second), jnp.where(self.even, second, first)

    def gathered(self, part):
        return lax.all_gather(part, "dp", axis=0, tiled=True, axis_index_groups=self.sides)

    def gathered_direct(self, part):
        if self.slots != 4:
            return self.gathered(part)
        rows = part.shape[0]
        whole_part = jnp.zeros((4 * rows, part.shape[1]), part.dtype)
        for k, piece in enumerate((part, moved(part, 2), moved(part, 4), moved(part, 6))):
            whole_part = lax.dynamic_update_slice_in_dim(whole_part, piece, (self.slot ^ k) * rows, 0)
        return whole_part

    def scattered(self, values):
        return lax.psum_scatter(values, "dp", scatter_dimension=0, tiled=True, axis_index_groups=self.sides)

    def scattered_direct(self, values):
        if self.slots != 4:
            return self.scattered(values)
        rows = values.shape[0] // 4
        pick = lambda k: lax.dynamic_slice_in_dim(values, (self.slot ^ k) * rows, rows, 0)
        parts = [pick(0), moved(pick(1), 2), moved(pick(2), 4), moved(pick(3), 6)]
        return sum(p.astype(jnp.float32) for p in parts).astype(jnp.bfloat16)

    def returned(self, low, high):
        f32, bf16 = jnp.float32, jnp.bfloat16
        rows = low.shape[0]
        first = jnp.where(self.even, low, high)
        second = jnp.where(self.even, high, low)
        total = (first.astype(f32) + self.side(second).astype(f32)).astype(bf16)
        got = self.cross(jnp.where(self.own, second, total))
        part = jnp.where(self.own, (first.astype(f32) + got.astype(f32)).astype(bf16), got)
        half = rows // 2
        cut = lambda which: lax.dynamic_slice_in_dim(part, which * half, half, 0)
        done = (cut(self.core).astype(f32) + moved(cut(1 - self.core), 1).astype(f32)).astype(bf16)
        return lax.all_gather(done, "dp", axis=0, tiled=True)


def exchanged(values):
    return lax.all_to_all(values, "mp", 0, 0, tiled=True)


def rms_parts(values):
    inverse = lax.rsqrt(jnp.mean(values * values, axis=-1, keepdims=True) + norm_eps)
    return (values * inverse, inverse)


def rms_back(grad_rows, normed, inverse, gain_vec):
    grad_normed = grad_rows * gain_vec
    return inverse * (grad_normed - normed * jnp.mean(grad_normed * normed, axis=-1, keepdims=True))


def mm(a, b):
    return dot(a, b, 1, 0)


def mm_t(a, b):
    return dot(a, b, 1, 1)


def t_mm(a, b):
    return dot(a, b, 0, 0)


def shards(
    hidden_in,
    first_in,
    segment_ids,
    valid_tokens,
    w_query,
    w_key,
    w_value,
    w_first_value,
    w_out,
    w_gate,
    w_up,
    w_down,
    gain_attn,
    gain_mlp,
    out_cotangent,
):
    at = Place()
    bf16, f32 = jnp.bfloat16, jnp.float32
    rows, width = hidden_in.shape
    cols = w_query.shape[1]
    pairs = cols // 128
    hid = w_gate.shape[1]
    beside = lambda *parts: jnp.concatenate(parts, 1)

    inner = [at.slice_of(w) for w in (w_query, w_key, w_value, w_first_value)]
    w_pair = []
    for p in range(pairs):
        low, high = at.quarters(beside(*(w[:, p * 128 : (p + 1) * 128] for w in inner)))
        w_pair.append(at.gathered_direct(beside(low, high)))
    low, high = at.quarters(beside(at.slice_of(w_gate), at.slice_of(w_up)))
    full_gu = at.gathered(beside(low[:, :hid], high[:, :hid], low[:, hid:], high[:, hid:]))
    down_rows, out_rows = hid // at.slots, cols // at.slots
    low, high = at.quarters(jnp.concatenate([at.slice_of(w_down), at.slice_of(w_out)], 0))
    both_do = at.gathered(beside(low, high)).reshape(at.slots, down_rows + out_rows, 2, width)
    stack_rows = lambda a: jnp.concatenate([a[:, :, q].reshape(-1, width) for q in range(2)], 0)
    full_d = stack_rows(both_do[:, :down_rows])
    full_o = stack_rows(both_do[:, down_rows:])

    x_all = at.ordered(hidden_in, moved(hidden_in, 1)).astype(f32)
    first_all = at.ordered(first_in, moved(first_in, 1))
    dy_own = lax.dynamic_slice_in_dim(out_cotangent, at.z * rows, rows, 0)
    dy_all = at.ordered(dy_own, moved(dy_own, 1))
    facts = jnp.stack([segment_ids, valid_tokens])
    facts = at.ordered(facts[None], moved(facts, 1)[None])
    seq_places = jax.vmap(token_places)(facts[:, 0])
    live = lax.dynamic_slice_in_dim(facts[:, 1], at.z * rows, rows, 1).reshape(-1, 1).astype(bf16)
    places = lax.dynamic_slice_in_dim(seq_places, at.z * rows, rows, 1).reshape(-1)
    spots = jnp.arange(segment_ids.shape[0], dtype=jnp.int32)
    unit = at.z // 2
    unit_places = lax.dynamic_index_in_dim(seq_places, unit, 0, keepdims=False)
    unit_live = lax.dynamic_index_in_dim(facts[:, 1], unit, 0, keepdims=False)
    first_key = jnp.where(unit_live == 1, spots - unit_places, spots)[None]
    frequency = jnp.exp(jnp.arange(HD // 2, dtype=f32) * (-2.0 * math.log(10000.0) / HD))
    angles = jnp.concatenate([places, unit_places]).astype(f32)[None, :] * frequency[:, None]
    cos_flat, sin_flat = jnp.cos(angles), jnp.sin(angles)
    n_here = 2 * rows
    cosine = jnp.concatenate([cos_flat] * 4, 0).T
    sine = jnp.concatenate([-sin_flat, sin_flat] * 2, 0).T
    flat = jnp.stack([cos_flat[:, n_here:], sin_flat[:, n_here:]])

    normed_one, inverse_one = rms_parts(x_all)
    h_one = (normed_one * gain_attn).astype(bf16)
    kept = []
    mixed = []
    powers = 0.0
    for p in range(pairs):
        sent, power = project(h_one, first_all, w_pair[p], cosine[:n_here], sine[:n_here])
        powers = powers + jnp.sum(power, 1)
        qkv = exchanged(sent)
        attended, logsum = attend(first_key, qkv)
        kept.append((qkv, attended, logsum))
        mixed.append(exchanged(attended))
    laid = lambda parts: jnp.concatenate(
        [beside(*(parts[p][2 * s + q] for q in range(2) for p in range(pairs))) for s in range(2)], 0
    )
    attn_mixed = laid(mixed) * live

    def both(partial):
        sent = partial.astype(bf16)
        return sent.astype(f32) + moved(sent, 1).astype(f32)

    own_rows = lambda a: lax.dynamic_slice_in_dim(a, at.core * rows, rows, 0)
    other_rows = lambda a: lax.dynamic_slice_in_dim(a, (1 - at.core) * rows, rows, 0)

    residual = x_all + both(mm(attn_mixed, full_o))
    normed_two, inverse_two = rms_parts(residual)
    h_two = (normed_two * gain_mlp).astype(bf16)
    d_hidden = mm_t(dy_all, full_d).astype(bf16).astype(f32)
    gate_up = mm(h_two, full_gu)
    gate, up = gate_up[:, : 2 * hid], gate_up[:, 2 * hid :]
    sigmoid = jax.nn.sigmoid(gate)
    silu = gate * sigmoid
    hidden = (silu * up).astype(bf16)
    d_gate = (d_hidden * up * sigmoid * (1.0 + gate * (1.0 - sigmoid))).astype(bf16)
    d_up = (d_hidden * silu).astype(bf16)
    d_gu = beside(d_gate, d_up)
    d_h2 = both(mm_t(d_gu, full_gu))
    d_res = dy_all.astype(f32) + rms_back(d_h2, normed_two, inverse_two, gain_mlp)
    d_attn = d_res.astype(bf16)
    d_mixed = mm_t(d_attn, full_o).astype(bf16) * live
    incoming = []
    for p in range(pairs):
        cut = lambda s, q: d_mixed[s * rows : (s + 1) * rows, (q * pairs + p) * 128 : (q * pairs + p + 1) * 128]
        incoming.append(exchanged(jnp.stack([cut(s, q) for s in range(2) for q in range(2)])))

    hidden, d_gu, h_two, d_attn = tied((hidden, d_gu, h_two, d_attn), d_mixed)
    ffn = mm(hidden, full_d).astype(bf16)
    ffn = own_rows(ffn).astype(f32) + moved(other_rows(ffn), 1).astype(f32)
    block_out = (own_rows(residual) + ffn).astype(bf16)
    g_gu = t_mm(h_two, d_gu).astype(bf16)
    s_gu = at.scattered(g_gu)
    g_down = t_mm(hidden, dy_all).astype(bf16)
    g_out = t_mm(attn_mixed, d_attn).astype(bf16)
    slotted = lambda g, q, n: g[q * n : (q + 1) * n].reshape(at.slots, n // at.slots, width)
    g_do = jnp.concatenate(
        [jnp.concatenate([slotted(g_down, q, hid), slotted(g_out, q, cols)], 1) for q in range(2)], 2
    ).reshape(-1, 2 * width)
    s_do = at.scattered(g_do)
    low = beside(s_gu[:, :hid], s_gu[:, 2 * hid : 3 * hid])
    high = beside(s_gu[:, hid : 2 * hid], s_gu[:, 3 * hid :])
    all_gu = at.returned(low, high)
    all_do = at.returned(s_do[:, :width], s_do[:, width:]).reshape(at.slots, down_rows + out_rows, width)

    d_h1 = 0.0
    inner_sums = []
    for p in range(pairs):
        qkv, attended, logsum = kept[p]
        back = attend_back(first_key, qkv, attended, incoming[p], logsum, flat, cosine[n_here:], sine[n_here:])
        back = exchanged(back)
        d_inner = jnp.concatenate([beside(back[2 * s], back[2 * s + 1]) for s in range(2)], 0)
        d_first = beside(d_inner[:, 256:384], d_inner[:, 640:768])
        w_inner = beside(w_pair[p][:, :384], w_pair[p][:, 512:896])
        d_h1 = d_h1 + mm_t(d_inner, w_inner)
        g_inner = t_mm(h_one, d_inner).astype(bf16)
        g_first = t_mm(first_all, d_first).astype(bf16)
        g_pair = beside(g_inner[:, :384], g_first[:, :128], g_inner[:, 384:], g_first[:, 128:])
        s_pair = at.scattered_direct(g_pair)
        inner_sums.append(at.returned(s_pair[:, :512], s_pair[:, 512:]))
    d_h1 = d_h1.astype(bf16)
    d_h1 = own_rows(d_h1).astype(f32) + moved(other_rows(d_h1), 1).astype(f32)
    own_normed = own_rows(normed_one)
    grad_input = (own_rows(d_res) + rms_back(d_h1, own_normed, own_rows(inverse_one), gain_attn)).astype(bf16)

    gain_parts = jnp.stack([jnp.sum(d_h1 * own_normed, 0), jnp.sum(own_rows(d_h2 * normed_two), 0)])
    small = jnp.concatenate([gain_parts.reshape(-1), powers[:2], jnp.zeros((126,), f32)])
    small = small.reshape(-1, 128)
    bit = 1
    while bit < at.n_dp:
        small = small + moved(small, bit)
        bit *= 2
    for shift in (1, 2):
        small = small + lax.ppermute(small, "mp", [(i, i ^ shift) for i in range(4)])
    small = small.reshape(-1)
    count = float(rows * at.n_dp * 4 * width)
    inner_out = [
        beside(*(inner_sums[p][:, i * 128 : (i + 1) * 128] for p in range(pairs))).astype(f32) for i in range(4)
    ]
    return (
        block_out,
        grad_input,
        *inner_out,
        all_do[:, down_rows:].reshape(cols, width).astype(f32),
        all_gu[:, :hid].astype(f32),
        all_gu[:, hid:].astype(f32),
        all_do[:, :down_rows].reshape(hid, width).astype(f32),
        small[:width],
        small[width : 2 * width],
        small[2 * width] / count,
        small[2 * width + 1] / count,
    )


def solution(mesh):
    placed = (
        P(("dp", "mp"), None),
        P(("dp", "mp"), None),
        P("dp"),
        P("dp"),
        P(None, "mp"),
        P(None, "mp"),
        P(None, "mp"),
        P(None, "mp"),
        P("mp", None),
        P(None, "mp"),
        P(None, "mp"),
        P("mp", None),
        P(),
        P(),
        P("dp", None),
    )
    return jax.shard_map(
        shards,
        mesh=mesh,
        in_specs=placed,
        out_specs=(
            P(("dp", "mp"), None),
            P(("dp", "mp"), None),
            P(None, "mp"),
            P(None, "mp"),
            P(None, "mp"),
            P(None, "mp"),
            P("mp", None),
            P(None, "mp"),
            P(None, "mp"),
            P("mp", None),
            P(),
            P(),
            P(),
            P(),
        ),
        check_vma=False,
    )
```

time: 1300 us -> 697 us (0.54)
  waiting for transfers between devices: 695 us -> 190 us
  matrix products: 257 us -> 73.3 us
  starting transfers between devices: 0.77 us -> 149 us
  Pallas kernels: 0 us -> 67.8 us
  blocking collectives: 46 us -> 0 us
  local copies, waits for them, and re-layouts: 141 us -> 95.8 us
  other arithmetic: 119 us -> 92.2 us
    reduce_scatter x4 -> x2, waiting for transfers between devices: 305 us -> 0.01 us  [scattered(): lax.psum_scatter(values, 'dp', scatter_dimension=0, tiled=True, axis_inde...]
    all_gather x4 -> x6, waiting for transfers between devices: 294 us -> 0.03 us  [the longest x4 0.03 us: returned(): return lax.all_gather(done, 'dp', axis=0, tiled=True)]
    dot_general x42 -> x15, matrix products: 257 us -> 73.3 us  [dot(): lax.dot_general(a, b, (((ca,), (cb,)), ((), ())), preferred_element_type=...]
    ppermute x0 -> x45, starting transfers between devices: none -> 109 us  [the longest x27 91.5 us: moved(): lax.ppermute(values, 'dp', [(i, i ^ bit) for i in range(lax.axis_size('dp...]
    ppermute x0 -> x45, waiting for transfers between devices: none -> 103 us  [the longest x27 55.9 us: moved(): lax.ppermute(values, 'dp', [(i, i ^ bit) for i in range(lax.axis_size('dp...]
    psum x1 -> x0, waiting for transfers between devices: 95.1 us -> none  [shards(): lax.psum(grad_w_inner.astype(jnp.bfloat16), 'dp').astype(jnp.float32)]
    dynamic_update_slice x16 -> x6, local copies, waits for them, and re-layouts: 93 us -> 3.66 us  [gathered_direct(): lax.dynamic_update_slice_in_dim(whole_part, piece, (self.slot ^ k) * rows...]
    all_to_all x0 -> x8, waiting for transfers between devices: none -> 86.9 us  [exchanged(): return lax.all_to_all(values, 'mp', 0, 0, tiled=True)]
  transfers between devices with their start and end apart: 9 -> 61, of which waited for: 9 -> 22; matrix products, arithmetic and copies ran while one was open for 6% -> 28% of each run, Pallas kernels for 0% -> 10%
where the time goes in v2:
time: 697 us; the launch traced here: 688 us
  waiting for transfers between devices  190 us (27%)
  starting transfers between devices  149 us (21%)
  local copies, waits for them, and re-layouts  95.8 us (14%)
  other arithmetic  92.2 us (13%)
  matrix products  73.3 us (11%)
  Pallas kernels  67.8 us (10%)
  between operations  19.8 us (3%)
    ppermute x27, starting transfers between devices, moved(): lax.ppermute(values, 'dp', [(i, i ^ bit) for i in range(lax.axis_size('dp...  91.5 us
    all_to_all x8, waiting for transfers between devices, exchanged(): return lax.all_to_all(values, 'mp', 0, 0, tiled=True)  86.9 us
    dot_general x15, matrix products, dot(): lax.dot_general(a, b, (((ca,), (cb,)), ((), ())), preferred_element_type=...  73.3 us
    ppermute x27, waiting for transfers between devices, moved(): lax.ppermute(values, 'dp', [(i, i ^ bit) for i in range(lax.axis_size('dp...  55.9 us
    ppermute x8, waiting for transfers between devices, cross(): return lax.ppermute(values, ('dp', 'mp'), cross_pairs(self.n_dp))  43.8 us
    all_to_all x8, starting transfers between devices, exchanged(): return lax.all_to_all(values, 'mp', 0, 0, tiled=True)  39.2 us
    pallas_call x2, Pallas kernels, attend_back(): pl.pallas_call(functools.partial(back_kernel, pieces=pieces, rows=rows),...  30.5 us
    unnamed x207, local copies, waits for them, and re-layouts  29.9 us
  transfers between devices with their start and end apart: 61, of which 22 were waited for; matrix products, arithmetic and copies ran while one was open for 28% of the time, Pallas kernels for 10%

profile of v2, /device:TPU:0, one launch (start us, length us, event | category | flops | bytes accessed | tf_op | source)
XLA Modules:
  0.0 687.6 jit_solution(6958014904957193008)
XLA Ops:
  24.5 13.2 %collective-permute-done.13 = bf16[240,1024]{1,0:T(8,128)(2,1)S(1)} collective-permute-done((bf16[240,1024]{1,0:T(8,128)(2,1)}, bf16[240,1024]{1,0:T(8,128)(2,1)S(1)}, u32[]{:S(2)}, u32[]{:S(2)}) %collective-permute-start.13) | collective-permute-done | bytes 491552 | tf_op jit(solution)/shard_map/ppermute | solution.py:249
  38.6 19.7 %collective-permute-start = (bf16[512,1024]{1,0:T(8,128)(2,1)S(1)}, bf16[512,1024]{1,0:T(8,128)(2,1)S(1)}, u32[]{:S(2)}, u32[]{:S(2)}) collective-permute-start(bf16[512,1024]{1,0:T(8,128)(2,1)S(1)} %copy-done.17), channel_id=1, source_target_pairs={{0,4},{4,0},{8,12},{12,8},{16,20},{20,16},{24,28},{28,24},{1,5},{5... | collective-permute-start | bytes 3145736 | tf_op jit(solution)/shard_map/ppermute | solution.py:217
  81.7 12.0 %collective-permute-done.5 = bf16[256,1024]{1,0:T(8,128)(2,1)S(1)} collective-permute-done((bf16[256,1024]{1,0:T(8,128)(2,1)S(1)}, bf16[256,1024]{1,0:T(8,128)(2,1)S(1)}, u32[]{:S(2)}, u32[]{:S(2)}) %collective-permute-start.5) | collective-permute-done | bytes 524320 | tf_op jit(solution)/shard_map/ppermute | solution.py:217
  99.3 14.1 %collective-permute-done.7 = bf16[256,1024]{1,0:T(8,128)(2,1)S(1)} collective-permute-done((bf16[256,1024]{1,0:T(8,128)(2,1)S(1)}, bf16[256,1024]{1,0:T(8,128)(2,1)S(1)}, u32[]{:S(2)}, u32[]{:S(2)}) %collective-permute-start.7) | collective-permute-done | bytes 524320 | tf_op jit(solution)/shard_map/ppermute | solution.py:217
  138.3 10.8 %collective-permute-done.10 = bf16[256,1024]{1,0:T(8,128)(2,1)S(1)} collective-permute-done((bf16[256,1024]{1,0:T(8,128)(2,1)}, bf16[256,1024]{1,0:T(8,128)(2,1)S(1)}, u32[]{:S(2)}, u32[]{:S(2)}) %collective-permute-start.10) | collective-permute-done | bytes 524320 | tf_op jit(solution)/shard_map/ppermute | solution.py:217
  150.0 11.6 %collective-permute-done.11 = bf16[256,1024]{1,0:T(8,128)(2,1)S(1)} collective-permute-done((bf16[256,1024]{1,0:T(8,128)(2,1)}, bf16[256,1024]{1,0:T(8,128)(2,1)S(1)}, u32[]{:S(2)}, u32[]{:S(2)}) %collective-permute-start.11) | collective-permute-done | bytes 524320 | tf_op jit(solution)/shard_map/ppermute | solution.py:217
  185.7 12.2 %shard_map.255 = (bf16[4,512,128]{2,1,0:T(8,128)(2,1)}, f32[2,2048]{1,0:T(2,128)S(1)}) custom-call(s32[1,2048]{1,0:T(1,128)S(1)} %get-tuple-element.102.start_ref, bf16[4,512,384]{2,1,0:T(8,128)(2,1)} %all-to-all-done.q_ref.k_ref.v_ref, bf16[4,512,384]{2,1,0:T(8,128)(2,1)} %all-to-all-done.q_ref.k_ref.v_ref, bf16[4,512,384]{2,1,0:T(8,128)(2,1)} %all-to-all-done.q_ref.k_ref.v_ref), custom_call_target="tpu_custom_call" | custom-call | flops 4294967296 | bytes 2097152 | tf_op jit(solution)/shard_map/pallas_call | solution.py:139
  197.9 24.0 %all-to-all-done.2.q_ref.k_ref.v_ref = bf16[4,512,384]{2,1,0:T(8,128)(2,1)} async-done(((bf16[4,512,384]{2,1,0:T(8,128)(2,1)}), bf16[4,512,384]{2,1,0:T(8,128)(2,1)}, u32[]{:S(2)}, u32[]{:S(2)}) %all-to-all-start.2) | async-done | bytes 1572896 | tf_op jit(solution)/shard_map/all_to_all | solution.py:306
  225.8 12.2 %shard_map.257 = (bf16[4,512,128]{2,1,0:T(8,128)(2,1)}, f32[2,2048]{1,0:T(2,128)S(1)}) custom-call(s32[1,2048]{1,0:T(1,128)S(1)} %get-tuple-element.102.start_ref, bf16[4,512,384]{2,1,0:T(8,128)(2,1)} %all-to-all-done.2.q_ref.k_ref.v_ref, bf16[4,512,384]{2,1,0:T(8,128)(2,1)} %all-to-all-done.2.q_ref.k_ref.v_ref, ...), custom_call_target="tpu_custom_call" | custom-call | flops 4294967296 | bytes 2097152 | tf_op jit(solution)/shard_map/pallas_call | solution.py:139
  244.2 13.0 %all-to-all-done.3 = bf16[4,512,128]{2,1,0:T(8,128)(2,1)S(1)} async-done(((bf16[4,512,128]{2,1,0:T(8,128)(2,1)}), bf16[4,512,128]{2,1,0:T(8,128)(2,1)S(1)}, u32[]{:S(2)}, u32[]{:S(2)}) %all-to-all-start.3) | async-done | bytes 524320 | tf_op jit(solution)/shard_map/all_to_all | solution.py:306
  258.0 10.0 %reshape.171 = bf16[4,240,2,1024]{3,2,1,0:T(2,128)(2,1)} reshape(bf16[960,2048]{1,0:T(8,128)(2,1)} %all-gather.7.cloned.1.call-done) | data formatting | bytes 7864320 | tf_op jit(solution)/shard_map/reshape | solution.py:365
  292.3 12.0 %fusion.124 = f32[1024,2816]{1,0:T(8,128)} fusion(bf16[1024,1024]{1,0:T(8,128)(2,1)} %get-tuple-element.34, bf16[1024,2816]{1,0:T(8,128)(2,1)} %all-gather.9.cloned.1.call-done), kind=kOutput, calls=%fused_computation.301 | convolution fusion | flops 5905580032 | bytes 19398656 | tf_op jit(solution)/shard_map/dot_general | solution.py:28
  304.3 11.5 %fusion.2 = (bf16[1024,1408]{1,0:T(8,128)(2,1)S(1)}, bf16[1024,1408]{1,0:T(8,128)(2,1)}, bf16[1024,1408]{1,0:T(8,128)(2,1)}) fusion(f32[1024,2816]{1,0:T(8,128)} %fusion.124, bf16[704,1024]{1,0:T(8,128)(2,1)S(1)} %bitcast.137, bf16[704,1024]{1,0:T(8,128)(2,1)S(1)} %bitcast.135, bf16[512,1024]{1,0:T(8,128)(2,1)} %collective-permute-done.18, ...), kind=kOutput, calls=%fused_computation.7 | convolution fusion | flops 2992504832 | bytes 25165824 | tf_op jit(solution)/shard_map/dot_general | solution.py:28
  315.8 9.1 %convolution_convert_fusion.5 = bf16[1024,1024]{1,0:T(8,128)(2,1)S(1)} fusion(bf16[1024,2816]{1,0:T(8,128)(2,1)} %all-gather.9.cloned.1.call-done, bf16[1024,1408]{1,0:T(8,128)(2,1)} %get-tuple-element.105, bf16[1024,1408]{1,0:T(8,128)(2,1)S(1)} %get-tuple-element.104), kind=kOutput, calls=%fused_computation.44 | convolution fusion | flops 5918162944 | bytes 13631488 | tf_op jit(solution)/shard_map/dot_general | solution.py:28
  349.8 11.0 %convolution_convert_fusion = bf16[1024,2816]{1,0:T(8,128)(2,1)} fusion(bf16[1024,1024]{1,0:T(8,128)(2,1)} %get-tuple-element.34, bf16[1024,2816]{1,0:T(8,128)(2,1)} %pad_maximum_fusion), kind=kOutput, calls=%fused_computation.13 | convolution fusion | flops 5908463616 | bytes 13631488 | tf_op jit(solution)/shard_map/dot_general | solution.py:28
  391.7 15.2 %shard_map.259 = bf16[4,512,384]{2,1,0:T(8,128)(2,1)S(1)} custom-call(s32[1,2048]{1,0:T(1,128)S(1)} %get-tuple-element.102.start_ref, bf16[4,512,384]{2,1,0:T(8,128)(2,1)} %all-to-all-done.2.q_ref.k_ref.v_ref, bf16[4,512,384]{2,1,0:T(8,128)(2,1)} %all-to-all-done.2.q_ref.k_ref.v_ref, bf16[4,512,384]{2,1,0:T(8,128)(2,1)} %all-to-all-done.2.q_ref.k_ref.v_ref, ...), custom_call_target="tpu_custom_call" | custom-call | flops 10737418240 | bytes 5242880 | tf_op jit(solution)/shard_map/pallas_call | solution.py:202
  415.4 15.2 %shard_map.258 = bf16[4,512,384]{2,1,0:T(8,128)(2,1)S(1)} custom-call(s32[1,2048]{1,0:T(1,128)S(1)} %get-tuple-element.102.start_ref, bf16[4,512,384]{2,1,0:T(8,128)(2,1)} %all-to-all-done.q_ref.k_ref.v_ref, bf16[4,512,384]{2,1,0:T(8,128)(2,1)} %all-to-all-done.q_ref.k_ref.v_ref, bf16[4,512,384]{2,1,0:T(8,128)(2,1)} %all-to-all-done.q_ref.k_ref.v_ref, ...), custom_call_target="tpu_custom_call" | custom-call | flops 10737418240 | bytes 5242880 | tf_op jit(solution)/shard_map/pallas_call | solution.py:202
  431.8 17.9 %all-to-all-done.7 = bf16[4,512,384]{2,1,0:T(8,128)(2,1)} async-done(((bf16[4,512,384]{2,1,0:T(8,128)(2,1)}), bf16[4,512,384]{2,1,0:T(8,128)(2,1)}, u32[]{:S(2)}, u32[]{:S(2)}) %all-to-all-start.7) | async-done | bytes 1572896 | tf_op jit(solution)/shard_map/all_to_all | solution.py:306
  465.3 25.3 %all-to-all-done.5 = bf16[4,512,384]{2,1,0:T(8,128)(2,1)} async-done(((bf16[4,512,384]{2,1,0:T(8,128)(2,1)}), bf16[4,512,384]{2,1,0:T(8,128)(2,1)}, u32[]{:S(2)}, u32[]{:S(2)}) %all-to-all-start.5) | async-done | bytes 1572896 | tf_op jit(solution)/shard_map/all_to_all | solution.py:306
  506.6 9.2 %collective-permute-start.33 = (bf16[128,512]{1,0:T(8,128)(2,1)S(1)}, bf16[128,512]{1,0:T(8,128)(2,1)S(1)}, u32[]{:S(2)}, u32[]{:S(2)}) collective-permute-start(bf16[128,512]{1,0:T(8,128)(2,1)S(1)} %constant_dynamic-slice_fusion.2), channel_id=1, source_target_pairs={{0,4},{4,0},{8,12},{12,8},{16,20},{20,16},{24,28},{28,24},{1,5},{5... | collective-permute-start | bytes 393224 | tf_op jit(solution)/shard_map/ppermute | solution.py:217
  529.7 20.0 %collective-permute-start.27 = (bf16[128,512]{1,0:T(8,128)(2,1)S(1)}, bf16[128,512]{1,0:T(8,128)(2,1)S(1)}, u32[]{:S(2)}, u32[]{:S(2)}) collective-permute-start(bf16[128,512]{1,0:T(8,128)(2,1)S(1)} %constant_dynamic-slice_fusion.6), channel_id=1, source_target_pairs={{0,4},{4,0},{8,12},{12,8},{16,20},{20,16},{24,28},{28,24},{1,5},{5... | collective-permute-start | bytes 393224 | tf_op jit(solution)/shard_map/ppermute | solution.py:217
  551.8 12.0 %collective-permute-done.35 = bf16[240,1024]{1,0:T(8,128)(2,1)S(1)} collective-permute-done((bf16[240,1024]{1,0:T(8,128)(2,1)S(1)}, bf16[240,1024]{1,0:T(8,128)(2,1)S(1)}, u32[]{:S(2)}, u32[]{:S(2)}) %collective-permute-start.35) | collective-permute-done | bytes 491552 | tf_op jit(solution)/shard_map/ppermute | solution.py:249
  576.0 13.2 %collective-permute-done.38 = bf16[256,1408]{1,0:T(8,128)(2,1)S(1)} collective-permute-done((bf16[256,1408]{1,0:T(8,128)(2,1)}, bf16[256,1408]{1,0:T(8,128)(2,1)S(1)}, u32[]{:S(2)}, u32[]{:S(2)}) %collective-permute-start.38) | collective-permute-done | bytes 720928 | tf_op jit(solution)/shard_map/ppermute | solution.py:249
  589.9 18.7 %collective-permute-start.39 = (bf16[128,1408]{1,0:T(8,128)(2,1)S(1)}, bf16[128,1408]{1,0:T(8,128)(2,1)S(1)}, u32[]{:S(2)}, u32[]{:S(2)}) collective-permute-start(bf16[128,1408]{1,0:T(8,128)(2,1)S(1)} %constant_dynamic-slice_fusion), channel_id=1, source_target_pairs={{0,4},{4,0},{8,12},{12,8},{16,20},{20,16},{24,28},{28,24},{1,5},{5... | collective-permute-start | bytes 1081352 | tf_op jit(solution)/shard_map/ppermute | solution.py:217
  (477 shorter events, 324.7 us)
Async XLA Ops:
  7.2 250.8 %all-gather.7.cloned.1.call-start = ((), (), s32[]{:S(2)}) async-start(), calls=%async_computation.10 | async-start | bytes 4915200 | tf_op jit(solution)/shard_map/all_gather | solution.py:269
  11.4 58.5 %collective-permute-start.8 = (bf16[256,512]{1,0:T(8,128)(2,1)}, bf16[256,512]{1,0:T(8,128)(2,1)}, u32[]{:S(2)}, u32[]{:S(2)}) collective-permute-start(bf16[256,512]{1,0:T(8,128)(2,1)} %pad_maximum_fusion.20), channel_id=1, source_target_pairs={{0,1},{1,0},{2,4},{3,5},{4,2},{5,3},{6,7},{7,6},{8,9},{9,8},{10,12... | collective-permute-start | bytes 786440 | tf_op jit(solution)/shard_map/ppermute | solution.py:249
  14.8 51.8 %collective-permute-start.3 = (bf16[256,512]{1,0:T(8,128)(2,1)}, bf16[256,512]{1,0:T(8,128)(2,1)}, u32[]{:S(2)}, u32[]{:S(2)}) collective-permute-start(bf16[256,512]{1,0:T(8,128)(2,1)} %pad_maximum_fusion.19), channel_id=1, source_target_pairs={{0,1},{1,0},{2,4},{3,5},{4,2},{5,3},{6,7},{7,6},{8,9},{9,8},{10,12... | collective-permute-start | bytes 786440 | tf_op jit(solution)/shard_map/ppermute | solution.py:249
  21.4 113.3 %collective-permute-start.16 = (bf16[256,1408]{1,0:T(8,128)(2,1)}, bf16[256,1408]{1,0:T(8,128)(2,1)}, u32[]{:S(2)}, u32[]{:S(2)}) collective-permute-start(bf16[256,1408]{1,0:T(8,128)(2,1)} %pad_maximum_fusion.8), channel_id=1, source_target_pairs={{0,1},{1,0},{2,4},{3,5},{4,2},{5,3},{6,7},{7,6},{8,9},{9,8},{10,12... | collective-permute-start | bytes 2162696 | tf_op jit(solution)/shard_map/ppermute | solution.py:249
  21.5 56.2 %collective-permute-start.2 = (bf16[512,1024]{1,0:T(8,128)(2,1)}, bf16[512,1024]{1,0:T(8,128)(2,1)}, u32[]{:S(2)}, u32[]{:S(2)}) collective-permute-start(bf16[512,1024]{1,0:T(8,128)(2,1)} %param.16), channel_id=1, source_target_pairs={{0,4},{4,0},{8,12},{12,8},{16,20},{20,16},{24,28},{28,24},{1,5},{5... | collective-permute-start | bytes 3145736 | tf_op jit(solution)/shard_map/ppermute | solution.py:217
  38.6 36.8 %collective-permute-start = (bf16[512,1024]{1,0:T(8,128)(2,1)S(1)}, bf16[512,1024]{1,0:T(8,128)(2,1)S(1)}, u32[]{:S(2)}, u32[]{:S(2)}) collective-permute-start(bf16[512,1024]{1,0:T(8,128)(2,1)S(1)} %copy-done.17), channel_id=1, source_target_pairs={{0,4},{4,0},{8,12},{12,8},{16,20},{20,16},{24,28},{28,24},{1,5},{5... | collective-permute-start | bytes 3145736 | tf_op jit(solution)/shard_map/ppermute | solution.py:217
  70.0 60.2 %collective-permute-start.9 = (bf16[256,512]{1,0:T(8,128)(2,1)}, bf16[256,512]{1,0:T(8,128)(2,1)}, u32[]{:S(2)}, u32[]{:S(2)}) collective-permute-start(bf16[256,512]{1,0:T(8,128)(2,1)} %collective-permute-done.8), channel_id=1, source_target_pairs={{2,3},{3,2},{4,5},{5,4},{10,11},{11,10},{12,13},{13,12},{18,19},{1... | collective-permute-start | bytes 786440 | tf_op jit(solution)/shard_map/ppermute | solution.py:252
  77.7 35.8 %collective-permute-start.7 = (bf16[256,1024]{1,0:T(8,128)(2,1)S(1)}, bf16[256,1024]{1,0:T(8,128)(2,1)S(1)}, u32[]{:S(2)}, u32[]{:S(2)}) collective-permute-start(bf16[256,1024]{1,0:T(8,128)(2,1)S(1)} %get-tuple-element.187), channel_id=1, source_target_pairs={{0,24},{4,28},{8,16},{12,20},{16,8},{20,12},{24,0},{28,4},{1,25},{... | collective-permute-start | bytes 1572872 | tf_op jit(solution)/shard_map/ppermute | solution.py:217
  122.5 56.9 %all-to-all-start = ((bf16[4,512,384]{2,1,0:T(8,128)(2,1)}), bf16[4,512,384]{2,1,0:T(8,128)(2,1)}, u32[]{:S(2)}, u32[]{:S(2)}) async-start(bf16[4,512,384]{2,1,0:T(8,128)(2,1)} %copy-done.2), calls=%async_computation | async-start | bytes 3145728 | tf_op jit(solution)/shard_map/all_to_all | solution.py:306
  130.1 162.2 %all-gather.9.cloned.1.call-start = ((), (), s32[]{:S(2)}) async-start(), calls=%async_computation.11 | async-start | bytes 7208960 | tf_op jit(solution)/shard_map/all_gather | solution.py:269
  134.7 27.7 %collective-permute-start.17 = (bf16[256,1408]{1,0:T(8,128)(2,1)}, bf16[256,1408]{1,0:T(8,128)(2,1)S(1)}, u32[]{:S(2)}, u32[]{:S(2)}) collective-permute-start(bf16[256,1408]{1,0:T(8,128)(2,1)} %collective-permute-done.16), channel_id=1, source_target_pairs={{2,3},{3,2},{4,5},{5,4},{10,11},{11,10},{12,13},{13,12},{18,19},{1... | collective-permute-start | bytes 2162696 | tf_op jit(solution)/shard_map/ppermute | solution.py:252
  136.0 33.9 %collective-permute-start.12 = (bf16[256,1024]{1,0:T(8,128)(2,1)}, bf16[256,1024]{1,0:T(8,128)(2,1)}, u32[]{:S(2)}, u32[]{:S(2)}) collective-permute-start(bf16[256,1024]{1,0:T(8,128)(2,1)} %get-tuple-element.197), channel_id=1, source_target_pairs={{0,24},{4,28},{8,16},{12,20},{16,8},{20,12},{24,0},{28,4},{1,25},{... | collective-permute-start | bytes 1572872 | tf_op jit(solution)/shard_map/ppermute | solution.py:217
  179.4 42.5 %all-to-all-start.2 = ((bf16[4,512,384]{2,1,0:T(8,128)(2,1)}), bf16[4,512,384]{2,1,0:T(8,128)(2,1)}, u32[]{:S(2)}, u32[]{:S(2)}) async-start(bf16[4,512,384]{2,1,0:T(8,128)(2,1)} %copy-done.5), calls=%async_computation.2 | async-start | bytes 3145728 | tf_op jit(solution)/shard_map/all_to_all | solution.py:306
  243.2 280.9 %reduce-scatter.3.cloned.1.call-start = ((), (), s32[]{:S(2)}) async-start(), calls=%async_computation.14 | async-start | bytes 4915200 | tf_op jit(solution)/shard_map/reduce_scatter | solution.py:281
  349.8 217.1 %reduce-scatter.5.cloned.1.call-start = ((), (), s32[]{:S(2)}) async-start(), calls=%async_computation.16 | async-start | bytes 7208960 | tf_op jit(solution)/shard_map/reduce_scatter | solution.py:281
  408.1 41.7 %all-to-all-start.7 = ((bf16[4,512,384]{2,1,0:T(8,128)(2,1)}), bf16[4,512,384]{2,1,0:T(8,128)(2,1)}, u32[]{:S(2)}, u32[]{:S(2)}) async-start(bf16[4,512,384]{2,1,0:T(8,128)(2,1)} %copy-done.4), calls=%async_computation.7 | async-start | bytes 3145728 | tf_op jit(solution)/shard_map/all_to_all | solution.py:306
  449.7 40.9 %all-to-all-start.5 = ((bf16[4,512,384]{2,1,0:T(8,128)(2,1)}), bf16[4,512,384]{2,1,0:T(8,128)(2,1)}, u32[]{:S(2)}, u32[]{:S(2)}) async-start(bf16[4,512,384]{2,1,0:T(8,128)(2,1)} %copy-done.3), calls=%async_computation.5 | async-start | bytes 3145728 | tf_op jit(solution)/shard_map/all_to_all | solution.py:306
  454.1 199.5 %all-gather.13.cloned.1.call-start = ((), (), s32[]{:S(2)}) async-start(), calls=%async_computation.13 | async-start | bytes 1179648 | tf_op jit(solution)/shard_map/all_gather | solution.py:302
  461.8 33.6 %collective-permute-start.28 = (bf16[256,1024]{1,0:T(8,128)(2,1)}, bf16[256,1024]{1,0:T(8,128)(2,1)}, u32[]{:S(2)}, u32[]{:S(2)}) collective-permute-start(bf16[256,1024]{1,0:T(8,128)(2,1)} %get-tuple-element.124), channel_id=1, source_target_pairs={{0,8},{4,12},{8,0},{12,4},{16,24},{20,28},{24,16},{28,20},{1,9},{5... | collective-permute-start | bytes 1572872 | tf_op jit(solution)/shard_map/ppermute | solution.py:217
  463.1 32.3 %collective-permute-start.30 = (bf16[256,1024]{1,0:T(8,128)(2,1)S(1)}, bf16[256,1024]{1,0:T(8,128)(2,1)}, u32[]{:S(2)}, u32[]{:S(2)}) collective-permute-start(bf16[256,1024]{1,0:T(8,128)(2,1)S(1)} %get-tuple-element.125), channel_id=1, source_target_pairs={{0,24},{4,28},{8,16},{12,20},{16,8},{20,12},{24,0},{28,4},{1,25},{... | collective-permute-start | bytes 1572872 | tf_op jit(solution)/shard_map/ppermute | solution.py:217
  463.5 31.9 %collective-permute-start.29 = (bf16[256,1024]{1,0:T(8,128)(2,1)S(1)}, bf16[256,1024]{1,0:T(8,128)(2,1)}, u32[]{:S(2)}, u32[]{:S(2)}) collective-permute-start(bf16[256,1024]{1,0:T(8,128)(2,1)S(1)} %get-tuple-element.126), channel_id=1, source_target_pairs={{0,16},{4,20},{8,24},{12,28},{16,0},{20,4},{24,8},{28,12},{1,17},{... | collective-permute-start | bytes 1572872 | tf_op jit(solution)/shard_map/ppermute | solution.py:217
  517.6 137.3 %all-gather.11.cloned.1.call-start = ((), (), s32[]{:S(2)}) async-start(), calls=%async_computation.12 | async-start | bytes 1179648 | tf_op jit(solution)/shard_map/all_gather | solution.py:302
  551.3 109.0 %all-gather.15.cloned.1.call-start = ((), (), s32[]{:S(2)}) async-start(), calls=%async_computation.15 | async-start | bytes 2211840 | tf_op jit(solution)/shard_map/all_gather | solution.py:302
  571.5 94.6 %all-gather.17.cloned.1.call-start = ((), (), s32[]{:S(2)}) async-start(), calls=%async_computation.17 | async-start | bytes 3244032 | tf_op jit(solution)/shard_map/all_gather | solution.py:302
  (134 other events, 1138.1 us)
Sparse Core Ops, SparseCore 0:
  60.8 67.0 all-gather.6
  170.0 66.3 all-gather.8
  349.9 48.7 reduce-scatter.2
  401.5 67.2 reduce-scatter.4
  517.7 22.0 all-gather.12
  551.5 21.7 all-gather.10
  575.2 27.3 all-gather.14
  614.5 32.3 all-gather.16

commit v3 on v2

--- a/solution.py
+++ b/solution.py
@@ -22,6 +22,7 @@
 
 QB = 256
 VMEM = 48 * 2**20
+HINT = pl.CostEstimate(flops=0, bytes_accessed=0, transcendentals=0)
 
 
 def dot(a, b, ca, cb):
@@ -83,9 +84,7 @@
             jax.ShapeDtypeStruct((8, 128), jnp.float32),
         ],
         compiler_params=pltpu.CompilerParams(vmem_limit_bytes=VMEM),
-        cost_estimate=pl.CostEstimate(
-            flops=2 * n * width * 1024, bytes_accessed=2 * width * (2 * n + 1024), transcendentals=0
-        ),
+        cost_estimate=HINT,
     )(h, first, weight, cosine, sine)
 
 
@@ -146,7 +145,7 @@
             jax.ShapeDtypeStruct((2, n), jnp.float32),
         ],
         compiler_params=pltpu.CompilerParams(vmem_limit_bytes=VMEM),
-        cost_estimate=pl.CostEstimate(flops=8 * n * n * 128, bytes_accessed=8 * n * 128, transcendentals=n * n),
+        cost_estimate=HINT,
     )(start, qkv, qkv, qkv)
 
 
@@ -209,8 +208,279 @@
         scratch_shapes=[pltpu.VMEM((pieces, rows, 128), jnp.float32)] * 2,
         out_shape=jax.ShapeDtypeStruct((pieces, rows, 384), jnp.bfloat16),
         compiler_params=pltpu.CompilerParams(vmem_limit_bytes=VMEM),
-        cost_estimate=pl.CostEstimate(flops=20 * n * n * 128, bytes_accessed=20 * n * 128, transcendentals=n * n),
+        cost_estimate=HINT,
     )(start, qkv, qkv, qkv, o, g, lse, flat, cosine, sine)
+
+
+def rows_spec(block, width):
+    return pl.BlockSpec((block, width), lambda i, *_: (i, 0))
+
+
+def fixed(shape):
+    return pl.BlockSpec(shape, lambda i, *_: (0,) * len(shape))
+
+
+def mix_kernel(*refs, pairs, block):
+    parts, (live_ref, w_ref, mixed_ref, out_ref) = refs[:pairs], refs[pairs:]
+    live = live_ref[...]
+    for q in range(2):
+        for p in range(pairs):
+            at = (q * pairs + p) * 128
+            mixed_ref[:, at : at + 128] = parts[p][q] * live
+    out_ref[...] = dot(mixed_ref[...], w_ref[...], 1, 0).astype(out_ref.dtype)
+
+
+def mix(parts, live, weight):
+    pairs = len(parts)
+    rows = parts[0].shape[1]
+    inner, width = weight.shape
+    block = rows
+    return pl.pallas_call(
+        functools.partial(mix_kernel, pairs=pairs, block=block),
+        grid=(2,),
+        in_specs=[pl.BlockSpec((2, block, 128), lambda i: (i, 0, 0))] * pairs
+        + [rows_spec(block, 1), fixed(weight.shape)],
+        out_specs=[rows_spec(block, inner), rows_spec(block, width)],
+        out_shape=[
+            jax.ShapeDtypeStruct((2 * rows, inner), jnp.bfloat16),
+            jax.ShapeDtypeStruct((2 * rows, width), jnp.bfloat16),
+        ],
+        compiler_params=pltpu.CompilerParams(vmem_limit_bytes=VMEM),
+        cost_estimate=HINT,
+    )(*parts, live, weight)
+
+
+def feed_kernel(x_ref, mine_ref, other_ref, gain_ref, dy_ref, *refs):
+    weights, (down_ref, res_ref, h_ref, hid_ref, d_ref, out_ref) = refs[:2], refs[2:]
+    f32 = jnp.float32
+    pad = down_ref.shape[0] // 2
+    res = x_ref[...].astype(f32) + (mine_ref[...].astype(f32) + other_ref[...].astype(f32))
+    res_ref[...] = res
+    inverse = lax.rsqrt(jnp.mean(res * res, axis=-1, keepdims=True) + norm_eps)
+    h = (res * inverse * gain_ref[...]).astype(jnp.bfloat16)
+    h_ref[...] = h
+    dy = dy_ref[...]
+    for q in range(2):
+        for at in range(0, pad, 256):
+            near = slice(q * 2 * pad + at, q * 2 * pad + at + 256)
+            far = slice(q * 2 * pad + pad + at, q * 2 * pad + pad + at + 256)
+            here = slice(q * pad + at, q * pad + at + 256)
+            gate = dot(h, weights[q][:, at : at + 256], 1, 0)
+            up = dot(h, weights[q][:, pad + at : pad + at + 256], 1, 0)
+            d_hid = dot(dy, down_ref[here, :], 1, 1).astype(jnp.bfloat16).astype(f32)
+            sig = 1.0 / (1.0 + jnp.exp(-gate))
+            silu = gate * sig
+            hid_ref[:, here] = (silu * up).astype(jnp.bfloat16)
+            d_ref[:, near] = (d_hid * up * (sig * (1.0 + gate * (1.0 - sig)))).astype(jnp.bfloat16)
+            d_ref[:, far] = (d_hid * silu).astype(jnp.bfloat16)
+    total = dot(d_ref[:, : 2 * pad], weights[0][:, : 2 * pad], 1, 1)
+    total = total + dot(d_ref[:, 2 * pad :], weights[1][:, : 2 * pad], 1, 1)
+    out_ref[...] = total.astype(jnp.bfloat16)
+
+
+def feed(x, mine, other, gain, dy, weights, down):
+    n, width = x.shape
+    pad = down.shape[0] // 2
+    span = weights.shape[1] // 2
+    block = n // 4
+    tokens = rows_spec(block, width)
+    bf16 = jnp.bfloat16
+    quarter = lambda q: pl.BlockSpec((width, span), lambda i: (0, q))
+    return pl.pallas_call(
+        feed_kernel,
+        grid=(n // block,),
+        in_specs=[tokens, tokens, tokens, fixed((1, width)), tokens, quarter(0), quarter(1), fixed(down.shape)],
+        out_specs=[tokens, tokens, rows_spec(block, 2 * pad), rows_spec(block, 4 * pad), tokens],
+        out_shape=[
+            jax.ShapeDtypeStruct((n, width), jnp.float32),
+            jax.ShapeDtypeStruct((n, width), bf16),
+            jax.ShapeDtypeStruct((n, 2 * pad), bf16),
+            jax.ShapeDtypeStruct((n, 4 * pad), bf16),
+            jax.ShapeDtypeStruct((n, width), bf16),
+        ],
+        compiler_params=pltpu.CompilerParams(vmem_limit_bytes=VMEM),
+        cost_estimate=HINT,
+    )(x, mine, other, gain, dy, weights, weights, down)
+
+
+def turn_kernel(core_ref, res_ref, mine_ref, other_ref, dy_ref, gain_ref, w_ref, live_ref, dres_ref, dattn_ref, gains_ref, *outs):
+    f32 = jnp.float32
+    pairs = len(outs)
+    res = res_ref[...]
+    inverse = lax.rsqrt(jnp.mean(res * res, axis=-1, keepdims=True) + norm_eps)
+    normed = res * inverse
+    grad = mine_ref[...].astype(f32) + other_ref[...].astype(f32)
+    scaled = grad * gain_ref[...]
+    d_res = dy_ref[...].astype(f32) + inverse * (scaled - normed * jnp.mean(scaled * normed, axis=-1, keepdims=True))
+    dres_ref[...] = d_res
+    d_attn = d_res.astype(jnp.bfloat16)
+    dattn_ref[...] = d_attn
+    mixed = dot(d_attn, w_ref[...], 1, 1).astype(jnp.bfloat16) * live_ref[...]
+    for q in range(2):
+        for p in range(pairs):
+            at = (q * pairs + p) * 128
+            outs[p][q] = mixed[:, at : at + 128]
+    at = pl.program_id(0)
+
+    @pl.when(at == 0)
+    def _():
+        gains_ref[...] = jnp.zeros_like(gains_ref)
+
+    @pl.when(at // (pl.num_programs(0) // 2) == core_ref[0])
+    def _():
+        gains_ref[0:1, :] += jnp.sum(grad * normed, 0, keepdims=True)
+
+
+def turn(core, res, mine, other, dy, gain, weight, live):
+    n, width = res.shape
+    inner = weight.shape[0]
+    pairs = inner // 256
+    rows = n // 2
+    block = rows // 2
+    subs = rows // block
+    tokens = rows_spec(block, width)
+    packed = pl.BlockSpec((2, block, 128), lambda i, *_: (i // subs, i % subs, 0))
+    return pl.pallas_call(
+        turn_kernel,
+        grid_spec=pltpu.PrefetchScalarGridSpec(
+            num_scalar_prefetch=1,
+            grid=(n // block,),
+            in_specs=[tokens] * 4 + [fixed((1, width)), fixed(weight.shape), rows_spec(block, 1)],
+            out_specs=[tokens, tokens, fixed((8, width))] + [packed] * pairs,
+        ),
+        out_shape=[
+            jax.ShapeDtypeStruct((n, width), jnp.float32),
+            jax.ShapeDtypeStruct((n, width), jnp.bfloat16),
+            jax.ShapeDtypeStruct((8, width), jnp.float32),
+        ]
+        + [jax.ShapeDtypeStruct((4, rows, 128), jnp.bfloat16)] * pairs,
+        compiler_params=pltpu.CompilerParams(vmem_limit_bytes=VMEM),
+        cost_estimate=HINT,
+    )(core, res, mine, other, dy, gain, weight, live)
+
+
+def weigh_kernel(a_ref, b_ref, out_ref):
+    out_ref[...] = dot(a_ref[...], b_ref[...], 0, 0).astype(out_ref.dtype)
+
+
+def weigh(a, b):
+    n, left = a.shape
+    right = b.shape[1]
+    wide = next(w for w in (1024, 768, 512, 256, right) if right % w == 0)
+    return pl.pallas_call(
+        weigh_kernel,
+        grid=(right // wide,),
+        in_specs=[pl.BlockSpec((n, left), lambda i: (0, 0)), pl.BlockSpec((n, wide), lambda i: (0, i))],
+        out_specs=pl.BlockSpec((left, wide), lambda i: (0, i)),
+        out_shape=jax.ShapeDtypeStruct((left, right), jnp.bfloat16),
+        compiler_params=pltpu.CompilerParams(vmem_limit_bytes=VMEM),
+        cost_estimate=HINT,
+    )(a, b)
+
+
+def slices_kernel(slot_ref, *refs, pairs):
+    ins, outs = refs[:4], refs[4:]
+    for p in range(pairs):
+        for i in range(4):
+            outs[p][:, i * 128 : (i + 1) * 128] = ins[i][:, p * 128 : (p + 1) * 128]
+
+
+def inner_slices(slot, weights, slots):
+    width, cols = weights[0].shape
+    rows, pairs = width // slots, cols // 128
+    return pl.pallas_call(
+        functools.partial(slices_kernel, pairs=pairs),
+        grid_spec=pltpu.PrefetchScalarGridSpec(
+            num_scalar_prefetch=1,
+            grid=(1,),
+            in_specs=[pl.BlockSpec((rows, cols), lambda i, slot: (slot[0], 0))] * 4,
+            out_specs=[pl.BlockSpec((rows, 512), lambda i, slot: (0, 0))] * pairs,
+        ),
+        out_shape=[jax.ShapeDtypeStruct((rows, 512), jnp.bfloat16)] * pairs,
+        compiler_params=pltpu.CompilerParams(vmem_limit_bytes=VMEM),
+        cost_estimate=HINT,
+    )(slot, *weights)
+
+
+def spread_gu_kernel(sum_ref, gate_ref, up_ref):
+    hid, pad = gate_ref.shape[1], sum_ref.shape[1] // 2
+    gate_ref[...] = sum_ref[:, :hid].astype(jnp.float32)
+    up_ref[...] = sum_ref[:, pad : pad + hid].astype(jnp.float32)
+
+
+def spread_gu(total, pad, hid):
+    n = total.shape[0]
+    block = n // 4
+    return pl.pallas_call(
+        spread_gu_kernel,
+        grid=(4,),
+        in_specs=[rows_spec(block, 2 * pad)],
+        out_specs=[rows_spec(block, hid)] * 2,
+        out_shape=[jax.ShapeDtypeStruct((n, hid), jnp.float32)] * 2,
+        compiler_params=pltpu.CompilerParams(vmem_limit_bytes=VMEM),
+        cost_estimate=HINT,
+    )(total)
+
+
+def spread_do_kernel(sum_ref, down_ref, out_ref):
+    n_down, n_out = down_ref.shape[0], out_ref.shape[0]
+    down_ref[...] = sum_ref[:n_down, :].astype(jnp.float32)
+    out_ref[...] = sum_ref[n_down : n_down + n_out, :].astype(jnp.float32)
+
+
+def spread_do(total, slots, down_rows, out_rows, width):
+    rows = total.shape[0] // slots
+    shapes = [(down_rows, width), (out_rows, width)]
+    return pl.pallas_call(
+        spread_do_kernel,
+        grid=(slots,),
+        in_specs=[rows_spec(rows, width)],
+        out_specs=[rows_spec(*s) for s in shapes],
+        out_shape=[jax.ShapeDtypeStruct((s[0] * slots, s[1]), jnp.float32) for s in shapes],
+        compiler_params=pltpu.CompilerParams(vmem_limit_bytes=VMEM),
+        cost_estimate=HINT,
+    )(total)
+
+
+def inner_kernel(*refs):
+    ins, outs = refs[:-4], refs[-4:]
+    for p, ref in enumerate(ins):
+        for i in range(4):
+            outs[i][:, p * 128 : (p + 1) * 128] = ref[:, i * 128 : (i + 1) * 128].astype(jnp.float32)
+
+
+def inner_spread(parts):
+    n = parts[0][0].shape[0]
+    block = n // 2
+    cols = 128 * len(parts)
+    at = lambda col: pl.BlockSpec((block, 512), lambda i: (i, col))
+    return pl.pallas_call(
+        inner_kernel,
+        grid=(2,),
+        in_specs=[at(col) for _, col in parts],
+        out_specs=[rows_spec(block, cols)] * 4,
+        out_shape=[jax.ShapeDtypeStruct((n, cols), jnp.float32)] * 4,
+        compiler_params=pltpu.CompilerParams(vmem_limit_bytes=VMEM),
+        cost_estimate=HINT,
+    )(*(a for a, _ in parts))
+
+
+def multiply_kernel(a_ref, b_ref, out_ref):
+    out_ref[...] = dot(a_ref[...], b_ref[...], 1, 0).astype(out_ref.dtype)
+
+
+def multiply(a, b):
+    n, width = a.shape[0], b.shape[1]
+    block = n // 4
+    return pl.pallas_call(
+        multiply_kernel,
+        grid=(4,),
+        in_specs=[rows_spec(block, a.shape[1]), fixed(b.shape)],
+        out_specs=rows_spec(block, width),
+        out_shape=jax.ShapeDtypeStruct((n, width), jnp.bfloat16),
+        compiler_params=pltpu.CompilerParams(vmem_limit_bytes=VMEM),
+        cost_estimate=HINT,
+    )(a, b)
 
 
 def moved(values, bit):
@@ -258,8 +528,7 @@
         rows = weight.shape[0] // self.slots
         return lax.dynamic_slice_in_dim(weight, self.slot * rows, rows, 0)
 
-    def quarters(self, part):
-        got = self.cross(part)
+    def quarters(self, part, got):
         far = self.side(got)
         first = jnp.where(self.own, part, got)
         second = jnp.where(self.own, got, far)
@@ -269,37 +538,53 @@
         return lax.all_gather(part, "dp", axis=0, tiled=True, axis_index_groups=self.sides)
 
     def gathered_direct(self, part):
+        every = jnp.concatenate([part] * self.slots, 0)
+        return lax.all_to_all(every, "dp", 0, 0, tiled=True, axis_index_groups=self.sides)
+
+    def gathered_steps(self, part):
         if self.slots != 4:
             return self.gathered(part)
         rows = part.shape[0]
-        whole_part = jnp.zeros((4 * rows, part.shape[1]), part.dtype)
+        every = jnp.zeros((4 * rows, part.shape[1]), part.dtype)
         for k, piece in enumerate((part, moved(part, 2), moved(part, 4), moved(part, 6))):
-            whole_part = lax.dynamic_update_slice_in_dim(whole_part, piece, (self.slot ^ k) * rows, 0)
-        return whole_part
+            every = lax.dynamic_update_slice_in_dim(every, piece, (self.slot ^ k) * rows, 0)
+        return every
+
+    def gathered_pairs(self, part):
+        return lax.all_to_all(jnp.concatenate([part] * self.n_dp, 0), "dp", 0, 0, tiled=True)
 
     def scattered(self, values):
         return lax.psum_scatter(values, "dp", scatter_dimension=0, tiled=True, axis_index_groups=self.sides)
 
-    def scattered_direct(self, values):
+    def pieces(self, values):
         if self.slots != 4:
-            return self.scattered(values)
+            return [self.scattered(values)]
         rows = values.shape[0] // 4
         pick = lambda k: lax.dynamic_slice_in_dim(values, (self.slot ^ k) * rows, rows, 0)
-        parts = [pick(0), moved(pick(1), 2), moved(pick(2), 4), moved(pick(3), 6)]
+        return [pick(0), moved(pick(1), 2), moved(pick(2), 4), moved(pick(3), 6)]
+
+    def added(self, parts):
         return sum(p.astype(jnp.float32) for p in parts).astype(jnp.bfloat16)
 
-    def returned(self, low, high):
-        f32, bf16 = jnp.float32, jnp.bfloat16
-        rows = low.shape[0]
+    def swapped(self, values):
+        every = lax.all_to_all(values, "dp", 0, 0, tiled=True, axis_index_groups=self.sides)
+        return list(every.reshape((self.slots, -1) + every.shape[1:]))
+
+    def bring(self, low, high):
         first = jnp.where(self.even, low, high)
         second = jnp.where(self.even, high, low)
-        total = (first.astype(f32) + self.side(second).astype(f32)).astype(bf16)
-        got = self.cross(jnp.where(self.own, second, total))
+        return first, second, self.side(second)
+
+    def bring_across(self, first, second, far):
+        total = (first.astype(jnp.float32) + far.astype(jnp.float32)).astype(jnp.bfloat16)
+        return self.cross(jnp.where(self.own, second, total))
+
+    def bring_home(self, first, got):
+        f32, bf16 = jnp.float32, jnp.bfloat16
         part = jnp.where(self.own, (first.astype(f32) + got.astype(f32)).astype(bf16), got)
-        half = rows // 2
+        half = first.shape[0] // 2
         cut = lambda which: lax.dynamic_slice_in_dim(part, which * half, half, 0)
-        done = (cut(self.core).astype(f32) + moved(cut(1 - self.core), 1).astype(f32)).astype(bf16)
-        return lax.all_gather(done, "dp", axis=0, tiled=True)
+        return (cut(self.core).astype(f32) + moved(cut(1 - self.core), 1).astype(f32)).astype(bf16)
 
 
 def exchanged(values):
@@ -351,28 +636,32 @@
     cols = w_query.shape[1]
     pairs = cols // 128
     hid = w_gate.shape[1]
+    pad = -(-hid // 256) * 256
     beside = lambda *parts: jnp.concatenate(parts, 1)
 
-    inner = [at.slice_of(w) for w in (w_query, w_key, w_value, w_first_value)]
-    w_pair = []
-    for p in range(pairs):
-        low, high = at.quarters(beside(*(w[:, p * 128 : (p + 1) * 128] for w in inner)))
-        w_pair.append(at.gathered_direct(beside(low, high)))
-    low, high = at.quarters(beside(at.slice_of(w_gate), at.slice_of(w_up)))
-    full_gu = at.gathered(beside(low[:, :hid], high[:, :hid], low[:, hid:], high[:, hid:]))
+    slot = at.slot.reshape(1).astype(jnp.int32)
+    parts = inner_slices(slot, (w_query, w_key, w_value, w_first_value), at.slots)
     down_rows, out_rows = hid // at.slots, cols // at.slots
-    low, high = at.quarters(jnp.concatenate([at.slice_of(w_down), at.slice_of(w_out)], 0))
-    both_do = at.gathered(beside(low, high)).reshape(at.slots, down_rows + out_rows, 2, width)
-    stack_rows = lambda a: jnp.concatenate([a[:, :, q].reshape(-1, width) for q in range(2)], 0)
-    full_d = stack_rows(both_do[:, :down_rows])
-    full_o = stack_rows(both_do[:, down_rows:])
-
-    x_all = at.ordered(hidden_in, moved(hidden_in, 1)).astype(f32)
-    first_all = at.ordered(first_in, moved(first_in, 1))
-    dy_own = lax.dynamic_slice_in_dim(out_cotangent, at.z * rows, rows, 0)
-    dy_all = at.ordered(dy_own, moved(dy_own, 1))
+    tall = width // at.slots
+    got_pair = []
+    before = ()
+    for part in parts:
+        part = tied(part, before)
+        before = at.cross(part)
+        got_pair.append((part, before))
+    wider = jnp.zeros((tall, pad - hid), bf16)
+    outer = jnp.concatenate(
+        [at.slice_of(w_down), at.slice_of(w_out), jnp.zeros((tall - down_rows - out_rows, width), bf16)], 0
+    )
+    part = tied(beside(at.slice_of(w_gate), wider, at.slice_of(w_up), wider, outer), before)
+    got_feed = (part, at.cross(part))
+    near = [beside(*at.quarters(part, got)) for part, got in got_pair]
+    w_pair = [at.gathered_direct(near[0])]
+
+    x_all = at.ordered(*tied((hidden_in, moved(hidden_in, 1)), near[0]))
+    first_all = at.ordered(*tied((first_in, moved(first_in, 1)), near[0]))
     facts = jnp.stack([segment_ids, valid_tokens])
-    facts = at.ordered(facts[None], moved(facts, 1)[None])
+    facts = tied(at.ordered(facts[None], moved(facts, 1)[None]), near[0])
     seq_places = jax.vmap(token_places)(facts[:, 0])
     live = lax.dynamic_slice_in_dim(facts[:, 1], at.z * rows, rows, 1).reshape(-1, 1).astype(bf16)
     places = lax.dynamic_slice_in_dim(seq_places, at.z * rows, rows, 1).reshape(-1)
@@ -389,111 +678,139 @@
     sine = jnp.concatenate([-sin_flat, sin_flat] * 2, 0).T
     flat = jnp.stack([cos_flat[:, n_here:], sin_flat[:, n_here:]])
 
-    normed_one, inverse_one = rms_parts(x_all)
+    normed_one, inverse_one = rms_parts(x_all.astype(f32))
     h_one = (normed_one * gain_attn).astype(bf16)
     kept = []
     mixed = []
     powers = 0.0
+    sends = []
     for p in range(pairs):
+        if p == 1:
+            part, got = got_feed
+            feed_part = tied(beside(*at.quarters(part, got)), (sends, first_key, flat, cosine, sine))
+        if p:
+            w_pair.append(at.gathered_steps(tied(near[p], feed_part)))
         sent, power = project(h_one, first_all, w_pair[p], cosine[:n_here], sine[:n_here])
         powers = powers + jnp.sum(power, 1)
-        qkv = exchanged(sent)
+        sends.append(sent)
+    full = at.gathered(feed_part)
+    span = 2 * pad + width
+    both_do = full.reshape(at.slots, tall, 2 * span)
+    lanes = lambda q: slice(q * span + 2 * pad, (q + 1) * span)
+    nothing = jnp.zeros((pad - hid, width), bf16)
+    full_d = jnp.concatenate(
+        [a for q in range(2) for a in (both_do[:, :down_rows, lanes(q)].reshape(hid, width), nothing)], 0
+    )
+    full_o = jnp.concatenate(
+        [both_do[:, down_rows : down_rows + out_rows, lanes(q)].reshape(cols, width) for q in range(2)], 0
+    )
+
+    for p in range(pairs):
+        qkv = exchanged(sends[p])
         attended, logsum = attend(first_key, qkv)
         kept.append((qkv, attended, logsum))
         mixed.append(exchanged(attended))
-    laid = lambda parts: jnp.concatenate(
-        [beside(*(parts[p][2 * s + q] for q in range(2) for p in range(pairs))) for s in range(2)], 0
-    )
-    attn_mixed = laid(mixed) * live
-
-    def both(partial):
-        sent = partial.astype(bf16)
-        return sent.astype(f32) + moved(sent, 1).astype(f32)
+    dy_own = tied(lax.dynamic_slice_in_dim(out_cotangent, at.z * rows, rows, 0), sends)
+    dy_all = at.ordered(dy_own, moved(dy_own, 1))
 
     own_rows = lambda a: lax.dynamic_slice_in_dim(a, at.core * rows, rows, 0)
     other_rows = lambda a: lax.dynamic_slice_in_dim(a, (1 - at.core) * rows, rows, 0)
 
-    residual = x_all + both(mm(attn_mixed, full_o))
-    normed_two, inverse_two = rms_parts(residual)
-    h_two = (normed_two * gain_mlp).astype(bf16)
-    d_hidden = mm_t(dy_all, full_d).astype(bf16).astype(f32)
-    gate_up = mm(h_two, full_gu)
-    gate, up = gate_up[:, : 2 * hid], gate_up[:, 2 * hid :]
-    sigmoid = jax.nn.sigmoid(gate)
-    silu = gate * sigmoid
-    hidden = (silu * up).astype(bf16)
-    d_gate = (d_hidden * up * sigmoid * (1.0 + gate * (1.0 - sigmoid))).astype(bf16)
-    d_up = (d_hidden * silu).astype(bf16)
-    d_gu = beside(d_gate, d_up)
-    d_h2 = both(mm_t(d_gu, full_gu))
-    d_res = dy_all.astype(f32) + rms_back(d_h2, normed_two, inverse_two, gain_mlp)
-    d_attn = d_res.astype(bf16)
-    d_mixed = mm_t(d_attn, full_o).astype(bf16) * live
-    incoming = []
+    attn_mixed, out_part = mix(mixed, live, full_o)
+    residual, h_two, hidden, d_gu, d_part = feed(
+        x_all, out_part, moved(out_part, 1), gain_mlp[None], dy_all, full, full_d
+    )
+    d_other = moved(d_part, 1)
+    g_gu = weigh(h_two, d_gu)
+    s_gu = at.scattered(g_gu)
+    d_res, d_attn, gains, *sends = turn(
+        at.core.reshape(1), tied(residual, g_gu), d_part, d_other, dy_all, gain_mlp[None], full_o, live
+    )
+    incoming = [exchanged(sent) for sent in sends]
+
+    g_down = weigh(tied(hidden, sends), dy_all)
+    g_out = weigh(attn_mixed, d_attn)
+    blank = jnp.zeros((at.slots, tall - down_rows - out_rows, width), bf16)
+    slotted = lambda g, first, n: g[first : first + n].reshape(at.slots, n // at.slots, width)
+    g_do = jnp.concatenate(
+        [
+            jnp.concatenate([slotted(g_down, q * pad, hid), slotted(g_out, q * cols, cols), blank], 1)
+            for q in range(2)
+        ],
+        2,
+    ).reshape(-1, 2 * width)
+    s_do = at.scattered(g_do)
+    backs = []
+    key = tied(first_key, (g_down, g_out))
     for p in range(pairs):
-        cut = lambda s, q: d_mixed[s * rows : (s + 1) * rows, (q * pairs + p) * 128 : (q * pairs + p + 1) * 128]
-        incoming.append(exchanged(jnp.stack([cut(s, q) for s in range(2) for q in range(2)])))
-
-    hidden, d_gu, h_two, d_attn = tied((hidden, d_gu, h_two, d_attn), d_mixed)
-    ffn = mm(hidden, full_d).astype(bf16)
+        qkv, attended, logsum = kept[p]
+        back = attend_back(key, qkv, attended, incoming[p], logsum, flat, cosine[n_here:], sine[n_here:])
+        backs.append(exchanged(back))
+        if p == 0:
+            ffn = multiply(tied(hidden, back), full_d)
+            tied_gu = tied(s_gu, back)
+            first_gu, second_gu, far_gu = at.bring(tied_gu[:, : 2 * pad], tied_gu[:, 2 * pad :])
+            key = tied(key, (far_gu, ffn))
+    got_gu = at.bring_across(first_gu, second_gu, far_gu)
+    near_gu = at.bring_home(first_gu, got_gu)
     ffn = own_rows(ffn).astype(f32) + moved(other_rows(ffn), 1).astype(f32)
     block_out = (own_rows(residual) + ffn).astype(bf16)
-    g_gu = t_mm(h_two, d_gu).astype(bf16)
-    s_gu = at.scattered(g_gu)
-    g_down = t_mm(hidden, dy_all).astype(bf16)
-    g_out = t_mm(attn_mixed, d_attn).astype(bf16)
-    slotted = lambda g, q, n: g[q * n : (q + 1) * n].reshape(at.slots, n // at.slots, width)
-    g_do = jnp.concatenate(
-        [jnp.concatenate([slotted(g_down, q, hid), slotted(g_out, q, cols)], 1) for q in range(2)], 2
-    ).reshape(-1, 2 * width)
-    s_do = at.scattered(g_do)
-    low = beside(s_gu[:, :hid], s_gu[:, 2 * hid : 3 * hid])
-    high = beside(s_gu[:, hid : 2 * hid], s_gu[:, 3 * hid :])
-    all_gu = at.returned(low, high)
-    all_do = at.returned(s_do[:, :width], s_do[:, width:]).reshape(at.slots, down_rows + out_rows, width)
 
     d_h1 = 0.0
-    inner_sums = []
+    parts = []
+    sent_pair = ()
     for p in range(pairs):
-        qkv, attended, logsum = kept[p]
-        back = attend_back(first_key, qkv, attended, incoming[p], logsum, flat, cosine[n_here:], sine[n_here:])
-        back = exchanged(back)
+        back = tied(backs[p], (block_out, got_gu, sent_pair))
         d_inner = jnp.concatenate([beside(back[2 * s], back[2 * s + 1]) for s in range(2)], 0)
         d_first = beside(d_inner[:, 256:384], d_inner[:, 640:768])
         w_inner = beside(w_pair[p][:, :384], w_pair[p][:, 512:896])
         d_h1 = d_h1 + mm_t(d_inner, w_inner)
-        g_inner = t_mm(h_one, d_inner).astype(bf16)
-        g_first = t_mm(first_all, d_first).astype(bf16)
+        g_inner = weigh(h_one, d_inner)
+        g_first = weigh(first_all, d_first)
         g_pair = beside(g_inner[:, :384], g_first[:, :128], g_inner[:, 384:], g_first[:, 128:])
-        s_pair = at.scattered_direct(g_pair)
-        inner_sums.append(at.returned(s_pair[:, :512], s_pair[:, 512:]))
+        parts.append(at.swapped(g_pair) if p else at.pieces(g_pair))
+        sent_pair = g_pair
+    sum_gu = lax.all_gather(near_gu, "dp", axis=0, tiled=True)
+    most = at.added(tied(parts[0], backs))
+    first, second, far = at.bring(
+        *(beside(s_do[:, q * width : (q + 1) * width], most[:, q * 512 : (q + 1) * 512]) for q in range(2))
+    )
+    got = at.bring_across(first, second, tied(far, parts))
+    late = [at.added(part) for part in parts[1:]]
+    late = [at.bring(part[:, :512], part[:, 512:]) for part in late]
+    most = at.bring_home(first, tied(got, (late, sum_gu)))
+    sum_do = lax.all_gather(most, "dp", axis=0, tiled=True)
+    late = [at.bring_home(one, at.bring_across(one, two, three)) for one, two, three in late]
+    inner_sums = [(sum_do, width // 512)] + [(at.gathered_pairs(part), 0) for part in late]
+    grad_gate, grad_up = spread_gu(sum_gu, pad, hid)
+    if down_rows % 16 == 0:
+        grad_down, grad_out = spread_do(sum_do, at.slots, down_rows, out_rows, width)
+    else:
+        all_do = sum_do[:, :width].reshape(at.slots, tall, width)
+        grad_down = all_do[:, :down_rows].reshape(hid, width).astype(f32)
+        grad_out = all_do[:, down_rows : down_rows + out_rows].reshape(cols, width).astype(f32)
     d_h1 = d_h1.astype(bf16)
     d_h1 = own_rows(d_h1).astype(f32) + moved(other_rows(d_h1), 1).astype(f32)
     own_normed = own_rows(normed_one)
     grad_input = (own_rows(d_res) + rms_back(d_h1, own_normed, own_rows(inverse_one), gain_attn)).astype(bf16)
 
-    gain_parts = jnp.stack([jnp.sum(d_h1 * own_normed, 0), jnp.sum(own_rows(d_h2 * normed_two), 0)])
+    gain_parts = jnp.stack([jnp.sum(d_h1 * own_normed, 0), gains[0]])
     small = jnp.concatenate([gain_parts.reshape(-1), powers[:2], jnp.zeros((126,), f32)])
     small = small.reshape(-1, 128)
-    bit = 1
-    while bit < at.n_dp:
-        small = small + moved(small, bit)
-        bit *= 2
-    for shift in (1, 2):
-        small = small + lax.ppermute(small, "mp", [(i, i ^ shift) for i in range(4)])
+    small = jnp.pad(small, ((0, -small.shape[0] % 8), (0, 0)))
+    for axis, size in (("dp", at.n_dp), ("mp", 4)):
+        every = lax.all_to_all(jnp.concatenate([small] * size, 0), axis, 0, 0, tiled=True)
+        small = jnp.sum(every.reshape((size,) + small.shape), 0)
     small = small.reshape(-1)
     count = float(rows * at.n_dp * 4 * width)
-    inner_out = [
-        beside(*(inner_sums[p][:, i * 128 : (i + 1) * 128] for p in range(pairs))).astype(f32) for i in range(4)
-    ]
     return (
         block_out,
         grad_input,
-        *inner_out,
-        all_do[:, down_rows:].reshape(cols, width).astype(f32),
-        all_gu[:, :hid].astype(f32),
-        all_gu[:, hid:].astype(f32),
-        all_do[:, :down_rows].reshape(hid, width).astype(f32),
+        *inner_spread(inner_sums),
+        grad_out,
+        grad_gate,
+        grad_up,
+        grad_down,
         small[:width],
         small[width : 2 * width],
         small[2 * width] / count,

time: 697 us -> 621 us (0.89)
  Pallas kernels: 67.8 us -> 140 us
  matrix products: 73.3 us -> 5.17 us
  starting transfers between devices: 149 us -> 110 us
  waiting for transfers between devices: 190 us -> 160 us
  blocking collectives: 0 us -> 19 us
  other arithmetic: 92.2 us -> 77.3 us
  local copies, waits for them, and re-layouts: 95.8 us -> 81.6 us
    pallas_call x0 -> x15, Pallas kernels: none -> 73.3 us  [the longest x1 24.6 us: feed(): pl.pallas_call(feed_kernel, grid=(n // block,), in_specs=[tokens, tokens,...]
    dot_general x15 -> x2, matrix products: 73.3 us -> 5.17 us  [dot(): lax.dot_general(a, b, (((ca,), (cb,)), ((), ())), preferred_element_type=...]
    ppermute x27 -> x17, starting transfers between devices: 91.5 us -> 25.3 us  [moved(): lax.ppermute(values, 'dp', [(i, i ^ bit) for i in range(lax.axis_size('dp...]
    all_to_all x8 -> x7, waiting for transfers between devices: 86.9 us -> 37.4 us  [exchanged(): return lax.all_to_all(values, 'mp', 0, 0, tiled=True)]
    reduce_scatter x2, waiting for transfers between devices: 0.01 us -> 32.7 us  [scattered(): lax.psum_scatter(values, 'dp', scatter_dimension=0, tiled=True, axis_inde...]
    ppermute x8 -> x6, waiting for transfers between devices: 43.8 us -> 11.5 us  [cross(): return lax.ppermute(values, ('dp', 'mp'), cross_pairs(self.n_dp))]
    all_to_all x0 -> x5, waiting for transfers between devices: none -> 23.9 us  [the longest x1 20.3 us: swapped(): lax.all_to_all(values, 'dp', 0, 0, tiled=True, axis_index_groups=self.sides)]
    convert_element_type x15 -> x4, other arithmetic: 27.2 us -> 3.99 us  [the longest x2 2.32 us: added(): return sum((p.astype(jnp.float32) for p in parts)).astype(jnp.bfloat16)]
  transfers between devices with their start and end apart: 61 -> 46, of which waited for: 22 -> 17; matrix products, arithmetic and copies ran while one was open for 28% -> 21% of each run, Pallas kernels for 10% -> 16%
where the time goes in v3:
time: 621 us; the launch traced here: 612 us
  waiting for transfers between devices  160 us (26%)
  Pallas kernels  140 us (23%)
  starting transfers between devices  110 us (18%)
  local copies, waits for them, and re-layouts  81.6 us (13%)
  other arithmetic  77.3 us (12%)
  between operations  19.2 us (3%)
  blocking collectives  19 us (3%)
    unnamed x185, local copies, waits for them, and re-layouts  47.5 us
    all_to_all x7, starting transfers between devices, exchanged(): return lax.all_to_all(values, 'mp', 0, 0, tiled=True)  47 us
    ppermute x17, waiting for transfers between devices, moved(): lax.ppermute(values, 'dp', [(i, i ^ bit) for i in range(lax.axis_size('dp...  40.3 us
    all_to_all x7, waiting for transfers between devices, exchanged(): return lax.all_to_all(values, 'mp', 0, 0, tiled=True)  37.4 us
    reduce_scatter x2, waiting for transfers between devices, scattered(): lax.psum_scatter(values, 'dp', scatter_dimension=0, tiled=True, axis_inde...  32.7 us
    pallas_call x2, Pallas kernels, attend_back(): pl.pallas_call(functools.partial(back_kernel, pieces=pieces, rows=rows),...  31.1 us
    ppermute x17, starting transfers between devices, moved(): lax.ppermute(values, 'dp', [(i, i ^ bit) for i in range(lax.axis_size('dp...  25.3 us
    pallas_call x1, Pallas kernels, feed(): pl.pallas_call(feed_kernel, grid=(n // block,), in_specs=[tokens, tokens,...  24.6 us
  transfers between devices with their start and end apart: 46, of which 17 were waited for; matrix products, arithmetic and copies ran while one was open for 21% of the time, Pallas kernels for 16%

profile of v3, /device:TPU:0, one launch (start us, length us, event | category | flops | bytes accessed | tf_op | source)
XLA Modules:
  0.0 611.7 jit_solution(15694127996520322165)
XLA Ops:
  36.7 13.3 %maximum_maximum_fusion.1 = bf16[1024,1024]{1,0:T(8,128)(2,1)} fusion(bf16[256,512]{1,0:T(8,128)(2,1)S(1)} %get-tuple-element.245, bf16[256,512]{1,0:T(8,128)(2,1)S(1)} %get-tuple-element.246), kind=kLoop, calls=%fused_computation.12 | loop fusion | flops 16777216 | bytes 2621440 | tf_op jit(solution)/shard_map/concatenate | solution.py:541
  56.1 7.0 %fusion.19 = (f32[32,3072]{0,1:T(8,128)}, f32[32,3072]{0,1:T(8,128)S(1)}, f32[32,3072]{0,1:T(8,128)S(1)}) fusion(f32[32]{0:T(128)S(1)} %multiply_exponential_fusion, f32[3072]{0:T(1024)S(1)} %add_convert_fusion.8), kind=kLoop, calls=%fused_computation.76 | loop fusion | flops 196608 | bytes 1192064 | tf_op jit(solution)/shard_map/neg | solution.py:678
  89.9 7.9 %shard_map.255 = (bf16[4,512,384]{2,1,0:T(8,128)(2,1)}, f32[8,128]{1,0:T(8,128)S(1)}) custom-call(bf16[1024,1024]{1,0:T(8,128)(2,1)S(1)} %get-tuple-element.195.h_ref.a_ref, bf16[1024,1024]{1,0:T(8,128)(2,1)} %maximum_select_fusion.1.first_ref.a_ref, bf16[1024,1024]{1,0:T(8,128)(2,1)} %bitcast.6.w_ref, f32[1024,128]{1,0:T(8,128)S(1)} %slice.256.cos_ref, ...), custom_call_target="tpu_custom_call" | custom-call | tf_op jit(solution)/shard_map/pallas_call | solution.py:68
  101.6 17.8 %all-to-all-start.1 = ((bf16[4,512,384]{2,1,0:T(8,128)(2,1)}), bf16[4,512,384]{2,1,0:T(8,128)(2,1)S(1)}, u32[]{:S(2)}, u32[]{:S(2)}) async-start(bf16[4,512,384]{2,1,0:T(8,128)(2,1)} %get-tuple-element.74), calls=%async_computation.1 | async-start | bytes 3145728 | tf_op jit(solution)/shard_map/all_to_all | solution.py:591
  123.4 14.4 %collective-permute-done.9 = bf16[256,1024]{1,0:T(8,128)(2,1)} collective-permute-done((bf16[256,1024]{1,0:T(8,128)(2,1)S(1)}, bf16[256,1024]{1,0:T(8,128)(2,1)}, u32[]{:S(2)}, u32[]{:S(2)}) %collective-permute-start.9) | collective-permute-done | bytes 524320 | tf_op jit(solution)/shard_map/ppermute | solution.py:487
  142.6 12.2 %collective-permute-done.11 = bf16[256,1024]{1,0:T(8,128)(2,1)S(1)} collective-permute-done((bf16[256,1024]{1,0:T(8,128)(2,1)S(1)}, bf16[256,1024]{1,0:T(8,128)(2,1)S(1)}, u32[]{:S(2)}, u32[]{:S(2)}) %collective-permute-start.11) | collective-permute-done | bytes 524320 | tf_op jit(solution)/shard_map/ppermute | solution.py:487
  156.3 6.5 %shard_map.257 = (bf16[4,512,384]{2,1,0:T(8,128)(2,1)S(1)}, f32[8,128]{1,0:T(8,128)S(1)}) custom-call(bf16[1024,1024]{1,0:T(8,128)(2,1)S(1)} %copy-done.6, bf16[1024,1024]{1,0:T(8,128)(2,1)} %maximum_select_fusion.1.first_ref.a_ref, bf16[1024,1024]{1,0:T(8,128)(2,1)} %copy-done.42, f32[1024,128]{1,0:T(8,128)S(1)} %copy-done.25, f32[1024,128]{1,0:T(8,128)S(1)} %copy-done.23), custom_call_target="tpu_custom_call" | custom-call | tf_op jit(solution)/shard_map/pallas_call | solution.py:68
  169.5 10.1 %shard_map.256 = (bf16[4,512,128]{2,1,0:T(8,128)(2,1)S(1)}, f32[2,2048]{1,0:T(2,128)S(1)}) custom-call(s32[1,2048]{1,0:T(1,128)S(1)} %get-tuple-element.102.start_ref, bf16[4,512,384]{2,1,0:T(8,128)(2,1)S(1)} %all-to-all-done.1.q_ref.k_ref.v_ref, bf16[4,512,384]{2,1,0:T(8,128)(2,1)S(1)} %all-to-all-done.1.q_ref.k_ref.v_ref, ...), custom_call_target="tpu_custom_call" | custom-call | tf_op jit(solution)/shard_map/pallas_call | solution.py:138
  180.4 16.2 %all-to-all-done.3.q_ref.k_ref.v_ref = bf16[4,512,384]{2,1,0:T(8,128)(2,1)S(1)} async-done(((bf16[4,512,384]{2,1,0:T(8,128)(2,1)}), bf16[4,512,384]{2,1,0:T(8,128)(2,1)S(1)}, u32[]{:S(2)}, u32[]{:S(2)}) %all-to-all-start.3) | async-done | bytes 1572896 | tf_op jit(solution)/shard_map/all_to_all | solution.py:591
  200.3 10.9 %shard_map.258 = (bf16[4,512,128]{2,1,0:T(8,128)(2,1)}, f32[2,2048]{1,0:T(2,128)S(1)}) custom-call(s32[1,2048]{1,0:T(1,128)S(1)} %get-tuple-element.102.start_ref, bf16[4,512,384]{2,1,0:T(8,128)(2,1)S(1)} %all-to-all-done.3.q_ref.k_ref.v_ref, bf16[4,512,384]{2,1,0:T(8,128)(2,1)S(1)} %all-to-all-done.3.q_ref.k_ref.v_ref, ...), custom_call_target="tpu_custom_call" | custom-call | tf_op jit(solution)/shard_map/pallas_call | solution.py:138
  216.7 13.9 %all-gather.4.cloned.1.call-done.refs_0_.refs_1_ = bf16[1024,5120]{1,0:T(8,128)(2,1)} async-done(((bf16[256,5120]{1,0:T(8,128)(2,1)}), bf16[1024,5120]{1,0:T(8,128)(2,1)}) %all-gather.4.cloned.1.call-update) | async-done | bytes 10485776 | tf_op jit(solution)/shard_map/all_gather | solution.py:538
  247.4 24.6 %shard_map.260 = (f32[1024,1024]{1,0:T(8,128)}, bf16[1024,1024]{1,0:T(8,128)(2,1)S(1)}, bf16[1024,1536]{1,0:T(8,128)(2,1)}, bf16[1024,3072]{1,0:T(8,128)(2,1)}, bf16[1024,1024]{1,0:T(8,128)(2,1)S(1)}) custom-call(bf16[1024,1024]{1,0:T(8,128)(2,1)} %copy-done.41, bf16[1024,1024]{1,0:T(8,128)(2,1)} %copy-done.29, bf16[1024,1024]{1,0:T(8,128)(2,1)} %copy-done.55, ...), custom_call_target="tpu_custom_call" | custom-call | tf_op jit(solution)/shard_map/pallas_call | solution.py:289
  272.0 11.0 %shard_map.261 = bf16[1024,3072]{1,0:T(8,128)(2,1)} custom-call(bf16[1024,1024]{1,0:T(8,128)(2,1)S(1)} %get-tuple-element.87.a_ref, bf16[1024,3072]{1,0:T(8,128)(2,1)} %get-tuple-element.88.b_ref), custom_call_target="tpu_custom_call" | custom-call | tf_op jit(solution)/shard_map/pallas_call | solution.py:370
  288.6 9.0 %shard_map.262 = (f32[1024,1024]{1,0:T(8,128)}, bf16[1024,1024]{1,0:T(8,128)(2,1)S(1)}, f32[8,1024]{1,0:T(8,128)S(1)}, bf16[4,512,128]{2,1,0:T(8,128)(2,1)S(1)}, bf16[4,512,128]{2,1,0:T(8,128)(2,1)}) custom-call(s32[1]{0:T(128)} %bitcast.18.core_ref, f32[1024,1024]{1,0:T(8,128)} %get-tuple-element.89.res_ref, bf16[1024,1024]{1,0:T(8,128)(2,1)} %copy-done.32, ...), custom_call_target="tpu_custom_call" | custom-call | tf_op jit(solution)/shard_map/pallas_call | solution.py:343
  297.7 5.5 shard_map.263
  307.1 19.0 %all_to_all.89.g_ref = bf16[4,512,128]{2,1,0:T(8,128)(2,1)S(1)} all-to-all(bf16[4,512,128]{2,1,0:T(8,128)(2,1)S(1)} %get-tuple-element.91), channel_id=1, replica_groups=mesh['dp'=8,'mp'=4] {'mp'}, dimensions={0} | all-to-all | bytes 1048576 | tf_op jit(solution)/shard_map/all_to_all | solution.py:591
  333.3 14.8 %shard_map.265 = bf16[4,512,384]{2,1,0:T(8,128)(2,1)S(1)} custom-call(s32[1,2048]{1,0:T(1,128)S(1)} %get-tuple-element.102.start_ref, bf16[4,512,384]{2,1,0:T(8,128)(2,1)} %copy-done.3, bf16[4,512,384]{2,1,0:T(8,128)(2,1)} %copy-done.3, bf16[4,512,384]{2,1,0:T(8,128)(2,1)} %copy-done.3, bf16[4,512,128]{2,1,0:T(8,128)(2,1)S(1)} %copy-done.31, ...), custom_call_target="tpu_custom_call" | custom-call | tf_op jit(solution)/shard_map/pallas_call | solution.py:201
  357.4 5.6 all-to-all-start.6
  363.1 5.9 shard_map.266
  379.6 29.4 %reduce-scatter.5.cloned.1.call-done = bf16[256,2048]{1,0:T(8,128)(2,1)} async-done(((bf16[1024,2048]{1,0:T(8,128)(2,1)}), bf16[256,2048]{1,0:T(8,128)(2,1)}) %reduce-scatter.5.cloned.1.call-update) | async-done | bytes 1048592 | tf_op jit(solution)/shard_map/reduce_scatter | solution.py:557
  411.2 16.3 %shard_map.267 = bf16[4,512,384]{2,1,0:T(8,128)(2,1)} custom-call(s32[1,2048]{1,0:T(1,128)S(1)} %get-tuple-element.102.start_ref, bf16[4,512,384]{2,1,0:T(8,128)(2,1)} %copy-done.2, bf16[4,512,384]{2,1,0:T(8,128)(2,1)} %copy-done.2, bf16[4,512,384]{2,1,0:T(8,128)(2,1)} %copy-done.2, bf16[4,512,128]{2,1,0:T(8,128)(2,1)} %get-tuple-element.82.o_ref, ...), custom_call_target="tpu_custom_call" | custom-call | tf_op jit(solution)/shard_map/pallas_call | solution.py:201
  449.8 21.1 %all-to-all-done.8 = bf16[4,512,384]{2,1,0:T(8,128)(2,1)} async-done(((bf16[4,512,384]{2,1,0:T(8,128)(2,1)}), bf16[4,512,384]{2,1,0:T(8,128)(2,1)}, u32[]{:S(2)}, u32[]{:S(2)}) %all-to-all-start.8) | async-done | bytes 1572896 | tf_op jit(solution)/shard_map/all_to_all | solution.py:591
  487.1 20.3 %all-to-all-done.9 = bf16[4,256,1024]{2,1,0:T(8,128)(2,1)S(1)} async-done(((bf16[4,256,1024]{2,1,0:T(8,128)(2,1)}), bf16[4,256,1024]{2,1,0:T(8,128)(2,1)S(1)}, u32[]{:S(2)}, u32[]{:S(2)}) %all-to-all-start.9) | async-done | bytes 2097184 | tf_op jit(solution)/shard_map/all_to_all | solution.py:570
  511.7 15.6 %collective-permute-start.26 = (bf16[128,1536]{1,0:T(8,128)(2,1)S(1)}, bf16[128,1536]{1,0:T(8,128)(2,1)S(1)}, u32[]{:S(2)}, u32[]{:S(2)}) collective-permute-start(bf16[128,1536]{1,0:T(8,128)(2,1)S(1)} %constant_dynamic-slice_fusion.1), channel_id=1, source_target_pairs={{0,4},{4,0},{8,12},{12,8},{16,20},{20,16},{24,28},{28,24},{1,5},{5... | collective-permute-start | bytes 1179656 | tf_op jit(solution)/shard_map/ppermute | solution.py:487
  (400 shorter events, 264.1 us)
Async XLA Ops:
  15.9 62.7 %collective-permute-start = (bf16[512,1024]{1,0:T(8,128)(2,1)}, bf16[512,1024]{1,0:T(8,128)(2,1)}, u32[]{:S(2)}, u32[]{:S(2)}) collective-permute-start(bf16[512,1024]{1,0:T(8,128)(2,1)} %param.15), channel_id=1, source_target_pairs={{0,4},{4,0},{8,12},{12,8},{16,20},{20,16},{24,28},{28,24},{1,5},{5... | collective-permute-start | bytes 3145736 | tf_op jit(solution)/shard_map/ppermute | solution.py:487
  16.0 62.6 %collective-permute-start.4 = (bf16[512,1024]{1,0:T(8,128)(2,1)}, bf16[512,1024]{1,0:T(8,128)(2,1)}, u32[]{:S(2)}, u32[]{:S(2)}) collective-permute-start(bf16[512,1024]{1,0:T(8,128)(2,1)} %param.16), channel_id=1, source_target_pairs={{0,4},{4,0},{8,12},{12,8},{16,20},{20,16},{24,28},{28,24},{1,5},{5... | collective-permute-start | bytes 3145736 | tf_op jit(solution)/shard_map/ppermute | solution.py:487
  33.7 42.3 %collective-permute-start.7 = (bf16[256,2560]{1,0:T(8,128)(2,1)}, bf16[256,2560]{1,0:T(8,128)(2,1)}, u32[]{:S(2)}, u32[]{:S(2)}) collective-permute-start(bf16[256,2560]{1,0:T(8,128)(2,1)} %concatenate.147), channel_id=1, source_target_pairs={{0,1},{1,0},{2,4},{3,5},{4,2},{5,3},{6,7},{7,6},{8,9},{9,8},{10,12... | collective-permute-start | bytes 3932168 | tf_op jit(solution)/shard_map/ppermute | solution.py:519
  51.3 38.6 %all-to-all-start = ((bf16[4,256,1024]{2,1,0:T(8,128)(2,1)}), bf16[4,256,1024]{2,1,0:T(8,128)(2,1)}, u32[]{:S(2)}, u32[]{:S(2)}) async-start(bf16[4,256,1024]{2,1,0:T(8,128)(2,1)} %bitcast.5), calls=%async_computation | async-start | bytes 4194304 | tf_op jit(solution)/shard_map/all_to_all | solution.py:542
  55.8 174.8 %all-gather.4.cloned.1.call-start = ((), (), s32[]{:S(2)}) async-start(), calls=%async_computation.15 | async-start | bytes 13107200 | tf_op jit(solution)/shard_map/all_gather | solution.py:538
  76.0 21.8 %collective-permute-start.8 = (bf16[256,2560]{1,0:T(8,128)(2,1)}, bf16[256,2560]{1,0:T(8,128)(2,1)}, u32[]{:S(2)}, u32[]{:S(2)}) collective-permute-start(bf16[256,2560]{1,0:T(8,128)(2,1)} %collective-permute-done.7), channel_id=1, source_target_pairs={{2,3},{3,2},{4,5},{5,4},{10,11},{11,10},{12,13},{13,12},{18,19},{1... | collective-permute-start | bytes 3932168 | tf_op jit(solution)/shard_map/ppermute | solution.py:522
  101.6 62.4 %all-to-all-start.1 = ((bf16[4,512,384]{2,1,0:T(8,128)(2,1)}), bf16[4,512,384]{2,1,0:T(8,128)(2,1)S(1)}, u32[]{:S(2)}, u32[]{:S(2)}) async-start(bf16[4,512,384]{2,1,0:T(8,128)(2,1)} %get-tuple-element.74), calls=%async_computation.1 | async-start | bytes 3145728 | tf_op jit(solution)/shard_map/all_to_all | solution.py:591
  121.5 21.1 %collective-permute-start.10 = (bf16[256,1024]{1,0:T(8,128)(2,1)S(1)}, bf16[256,1024]{1,0:T(8,128)(2,1)S(1)}, u32[]{:S(2)}, u32[]{:S(2)}) collective-permute-start(bf16[256,1024]{1,0:T(8,128)(2,1)S(1)} %pad_maximum_fusion.8), channel_id=1, source_target_pairs={{0,16},{4,20},{8,24},{12,28},{16,0},{20,4},{24,8},{28,12},{1,17},{... | collective-permute-start | bytes 1572872 | tf_op jit(solution)/shard_map/ppermute | solution.py:487
  122.9 31.9 %collective-permute-start.11 = (bf16[256,1024]{1,0:T(8,128)(2,1)S(1)}, bf16[256,1024]{1,0:T(8,128)(2,1)S(1)}, u32[]{:S(2)}, u32[]{:S(2)}) collective-permute-start(bf16[256,1024]{1,0:T(8,128)(2,1)S(1)} %pad_maximum_fusion.8), channel_id=1, source_target_pairs={{0,24},{4,28},{8,16},{12,20},{16,8},{20,12},{24,0},{28,4},{1,25},{... | collective-permute-start | bytes 1572872 | tf_op jit(solution)/shard_map/ppermute | solution.py:487
  164.0 32.6 %all-to-all-start.3 = ((bf16[4,512,384]{2,1,0:T(8,128)(2,1)}), bf16[4,512,384]{2,1,0:T(8,128)(2,1)S(1)}, u32[]{:S(2)}, u32[]{:S(2)}) async-start(bf16[4,512,384]{2,1,0:T(8,128)(2,1)} %copy-done.33), calls=%async_computation.3 | async-start | bytes 3145728 | tf_op jit(solution)/shard_map/all_to_all | solution.py:591
  216.2 137.2 %reduce-scatter.3.cloned.1.call-start = ((), (), s32[]{:S(2)}) async-start(), calls=%async_computation.16 | async-start | bytes 7864320 | tf_op jit(solution)/shard_map/reduce_scatter | solution.py:557
  283.0 126.1 %reduce-scatter.5.cloned.1.call-start = ((), (), s32[]{:S(2)}) async-start(), calls=%async_computation.17 | async-start | bytes 5242880 | tf_op jit(solution)/shard_map/reduce_scatter | solution.py:557
  326.1 31.3 %all-to-all-start.7 = ((bf16[4,512,128]{2,1,0:T(8,128)(2,1)}), bf16[4,512,128]{2,1,0:T(8,128)(2,1)}, u32[]{:S(2)}, u32[]{:S(2)}) async-start(bf16[4,512,128]{2,1,0:T(8,128)(2,1)} %get-tuple-element.92), calls=%async_computation.8 | async-start | bytes 1048576 | tf_op jit(solution)/shard_map/all_to_all | solution.py:591
  357.4 71.8 %all-to-all-start.6 = ((bf16[4,512,384]{2,1,0:T(8,128)(2,1)}), bf16[4,512,384]{2,1,0:T(8,128)(2,1)}, u32[]{:S(2)}, u32[]{:S(2)}) async-start(bf16[4,512,384]{2,1,0:T(8,128)(2,1)} %copy-done.21), calls=%async_computation.6 | async-start | bytes 3145728 | tf_op jit(solution)/shard_map/all_to_all | solution.py:591
  374.2 53.3 %collective-permute-start.17 = (bf16[256,1536]{1,0:T(8,128)(2,1)}, bf16[256,1536]{1,0:T(8,128)(2,1)}, u32[]{:S(2)}, u32[]{:S(2)}) collective-permute-start(bf16[256,1536]{1,0:T(8,128)(2,1)} %fusion.16), channel_id=1, source_target_pairs={{0,1},{1,0},{2,4},{3,5},{4,2},{5,3},{6,7},{7,6},{8,9},{9,8},{10,12... | collective-permute-start | bytes 2359304 | tf_op jit(solution)/shard_map/ppermute | solution.py:519
  429.3 41.7 %all-to-all-start.8 = ((bf16[4,512,384]{2,1,0:T(8,128)(2,1)}), bf16[4,512,384]{2,1,0:T(8,128)(2,1)}, u32[]{:S(2)}, u32[]{:S(2)}) async-start(bf16[4,512,384]{2,1,0:T(8,128)(2,1)} %shard_map.267), calls=%async_computation.9 | async-start | bytes 3145728 | tf_op jit(solution)/shard_map/all_to_all | solution.py:591
  433.9 76.0 %all-gather.6.cloned.1.call-start = ((), (), s32[]{:S(2)}) async-start(), calls=%async_computation.18 | async-start | bytes 3538944 | tf_op jit(solution)/shard_map/all_gather | solution.py:773
  446.3 36.4 %collective-permute-start.21 = (bf16[256,1024]{1,0:T(8,128)(2,1)}, bf16[256,1024]{1,0:T(8,128)(2,1)}, u32[]{:S(2)}, u32[]{:S(2)}) collective-permute-start(bf16[256,1024]{1,0:T(8,128)(2,1)} %get-tuple-element.196), channel_id=1, source_target_pairs={{0,24},{4,28},{8,16},{12,20},{16,8},{20,12},{24,0},{28,4},{1,25},{... | collective-permute-start | bytes 1572872 | tf_op jit(solution)/shard_map/ppermute | solution.py:487
  447.8 35.0 %collective-permute-start.20 = (bf16[256,1024]{1,0:T(8,128)(2,1)}, bf16[256,1024]{1,0:T(8,128)(2,1)}, u32[]{:S(2)}, u32[]{:S(2)}) collective-permute-start(bf16[256,1024]{1,0:T(8,128)(2,1)} %get-tuple-element.197), channel_id=1, source_target_pairs={{0,16},{4,20},{8,24},{12,28},{16,0},{20,4},{24,8},{28,12},{1,17},{... | collective-permute-start | bytes 1572872 | tf_op jit(solution)/shard_map/ppermute | solution.py:487
  449.2 33.6 %collective-permute-start.19 = (bf16[256,1024]{1,0:T(8,128)(2,1)}, bf16[256,1024]{1,0:T(8,128)(2,1)}, u32[]{:S(2)}, u32[]{:S(2)}) collective-permute-start(bf16[256,1024]{1,0:T(8,128)(2,1)} %get-tuple-element.198), channel_id=1, source_target_pairs={{0,8},{4,12},{8,0},{12,4},{16,24},{20,28},{24,16},{28,20},{1,9},{5... | collective-permute-start | bytes 1572872 | tf_op jit(solution)/shard_map/ppermute | solution.py:487
  479.1 28.3 %all-to-all-start.9 = ((bf16[4,256,1024]{2,1,0:T(8,128)(2,1)}), bf16[4,256,1024]{2,1,0:T(8,128)(2,1)S(1)}, u32[]{:S(2)}, u32[]{:S(2)}) async-start(bf16[4,256,1024]{2,1,0:T(8,128)(2,1)} %bitcast.108), calls=%async_computation.11 | async-start | bytes 4194304 | tf_op jit(solution)/shard_map/all_to_all | solution.py:570
  482.7 111.3 %all-gather.8.cloned.1.call-start = ((), (), s32[]{:S(2)}) async-start(), calls=%async_computation.19 | async-start | bytes 3538944 | tf_op jit(solution)/shard_map/all_gather | solution.py:782
  487.1 22.7 %collective-permute-start.23 = (bf16[256,1536]{1,0:T(8,128)(2,1)}, bf16[256,1536]{1,0:T(8,128)(2,1)}, u32[]{:S(2)}, u32[]{:S(2)}) collective-permute-start(bf16[256,1536]{1,0:T(8,128)(2,1)} %fusion.15), channel_id=1, source_target_pairs={{0,1},{1,0},{2,4},{3,5},{4,2},{5,3},{6,7},{7,6},{8,9},{9,8},{10,12... | collective-permute-start | bytes 2359304 | tf_op jit(solution)/shard_map/ppermute | solution.py:519
  570.9 27.5 %all-to-all-start.10 = ((bf16[8,128,512]{2,1,0:T(8,128)(2,1)}), bf16[8,128,512]{2,1,0:T(8,128)(2,1)S(1)}, u32[]{:S(2)}, u32[]{:S(2)}) async-start(bf16[8,128,512]{2,1,0:T(8,128)(2,1)} %bitcast.37), calls=%async_computation.12 | async-start | bytes 2097152 | tf_op jit(solution)/shard_map/all_to_all | solution.py:554
  (103 other events, 751.5 us)
Sparse Core Ops, SparseCore 0:
  101.7 128.8 all-gather.3
  283.1 70.2 reduce-scatter.2
  356.4 52.6 reduce-scatter.4
  438.8 48.0 all-gather.5
  532.2 34.7 all-gather.7

commit v4 on v3

--- a/solution.py
+++ b/solution.py
@@ -403,9 +403,9 @@
 
 
 def spread_gu_kernel(sum_ref, gate_ref, up_ref):
-    hid, pad = gate_ref.shape[1], sum_ref.shape[1] // 2
-    gate_ref[...] = sum_ref[:, :hid].astype(jnp.float32)
-    up_ref[...] = sum_ref[:, pad : pad + hid].astype(jnp.float32)
+    hid, pad = gate_ref.shape[0], sum_ref.shape[1] // 2
+    gate_ref[...] = jnp.transpose(sum_ref[:, :hid].astype(jnp.float32))
+    up_ref[...] = jnp.transpose(sum_ref[:, pad : pad + hid].astype(jnp.float32))
 
 
 def spread_gu(total, pad, hid):
@@ -415,8 +415,8 @@
         spread_gu_kernel,
         grid=(4,),
         in_specs=[rows_spec(block, 2 * pad)],
-        out_specs=[rows_spec(block, hid)] * 2,
-        out_shape=[jax.ShapeDtypeStruct((n, hid), jnp.float32)] * 2,
+        out_specs=[pl.BlockSpec((hid, block), lambda i: (0, i))] * 2,
+        out_shape=[jax.ShapeDtypeStruct((hid, n), jnp.float32)] * 2,
         compiler_params=pltpu.CompilerParams(vmem_limit_bytes=VMEM),
         cost_estimate=HINT,
     )(total)
@@ -770,25 +770,6 @@
         g_pair = beside(g_inner[:, :384], g_first[:, :128], g_inner[:, 384:], g_first[:, 128:])
         parts.append(at.swapped(g_pair) if p else at.pieces(g_pair))
         sent_pair = g_pair
-    sum_gu = lax.all_gather(near_gu, "dp", axis=0, tiled=True)
-    most = at.added(tied(parts[0], backs))
-    first, second, far = at.bring(
-        *(beside(s_do[:, q * width : (q + 1) * width], most[:, q * 512 : (q + 1) * 512]) for q in range(2))
-    )
-    got = at.bring_across(first, second, tied(far, parts))
-    late = [at.added(part) for part in parts[1:]]
-    late = [at.bring(part[:, :512], part[:, 512:]) for part in late]
-    most = at.bring_home(first, tied(got, (late, sum_gu)))
-    sum_do = lax.all_gather(most, "dp", axis=0, tiled=True)
-    late = [at.bring_home(one, at.bring_across(one, two, three)) for one, two, three in late]
-    inner_sums = [(sum_do, width // 512)] + [(at.gathered_pairs(part), 0) for part in late]
-    grad_gate, grad_up = spread_gu(sum_gu, pad, hid)
-    if down_rows % 16 == 0:
-        grad_down, grad_out = spread_do(sum_do, at.slots, down_rows, out_rows, width)
-    else:
-        all_do = sum_do[:, :width].reshape(at.slots, tall, width)
-        grad_down = all_do[:, :down_rows].reshape(hid, width).astype(f32)
-        grad_out = all_do[:, down_rows : down_rows + out_rows].reshape(cols, width).astype(f32)
     d_h1 = d_h1.astype(bf16)
     d_h1 = own_rows(d_h1).astype(f32) + moved(other_rows(d_h1), 1).astype(f32)
     own_normed = own_rows(normed_one)
@@ -801,6 +782,26 @@
     for axis, size in (("dp", at.n_dp), ("mp", 4)):
         every = lax.all_to_all(jnp.concatenate([small] * size, 0), axis, 0, 0, tiled=True)
         small = jnp.sum(every.reshape((size,) + small.shape), 0)
+    sum_gu = lax.all_gather(near_gu, "dp", axis=0, tiled=True)
+    most = at.added(tied(parts[0], backs))
+    first, second, far = at.bring(
+        *(beside(tied(s_do, back)[:, q * width : (q + 1) * width], most[:, q * 512 : (q + 1) * 512]) for q in range(2))
+    )
+    got = at.bring_across(first, second, tied(far, (parts, d_h1)))
+    late = [at.added(part) for part in parts[1:]]
+    late = [at.bring(part[:, :512], part[:, 512:]) for part in late]
+    most = at.bring_home(first, tied(got, (late, sum_gu)))
+    sum_do = lax.all_gather(most, "dp", axis=0, tiled=True)
+    late = [at.bring_home(one, at.bring_across(one, two, tied(three, small))) for one, two, three in late]
+    grad_gate, grad_up = spread_gu(sum_gu, pad, hid)
+    inner_sums = [(sum_do, width // 512)]
+    inner_sums += [(at.gathered_pairs(tied(part, (grad_gate, grad_up))), 0) for part in late]
+    if down_rows % 16 == 0:
+        grad_down, grad_out = spread_do(sum_do, at.slots, down_rows, out_rows, width)
+    else:
+        all_do = sum_do[:, :width].reshape(at.slots, tall, width)
+        grad_down = all_do[:, :down_rows].reshape(hid, width).astype(f32)
+        grad_out = all_do[:, down_rows : down_rows + out_rows].reshape(cols, width).astype(f32)
     small = small.reshape(-1)
     count = float(rows * at.n_dp * 4 * width)
     return (
@@ -808,8 +809,8 @@
         grad_input,
         *inner_spread(inner_sums),
         grad_out,
-        grad_gate,
-        grad_up,
+        grad_gate.T,
+        grad_up.T,
         grad_down,
         small[:width],
         small[width : 2 * width],

time: 621 us -> 603 us (0.971)
  local copies, waits for them, and re-layouts: 81.6 us -> 68.6 us
  blocking collectives: 19 us -> 8.69 us
    reduce_scatter x2, waiting for transfers between devices: 32.7 us -> 5.62 us  [scattered(): lax.psum_scatter(values, 'dp', scatter_dimension=0, tiled=True, axis_inde...]
    unnamed x185 -> x180, local copies, waits for them, and re-layouts: 47.5 us -> 36.2 us
    all_to_all x7 -> x8, waiting for transfers between devices: 37.4 us -> 48.4 us  [exchanged(): return lax.all_to_all(values, 'mp', 0, 0, tiled=True)]
    all_to_all x1, blocking collectives: 19 us -> 8.69 us  [shards(): lax.all_to_all(jnp.concatenate([small] * size, 0), axis, 0, 0, tiled=True)]
    ppermute x6, waiting for transfers between devices: 11.5 us -> 21.1 us  [cross(): return lax.ppermute(values, ('dp', 'mp'), cross_pairs(self.n_dp))]
    all_to_all x7 -> x8, starting transfers between devices: 47 us -> 51.4 us  [exchanged(): return lax.all_to_all(values, 'mp', 0, 0, tiled=True)]
  transfers between devices with their start and end apart: 46 -> 46, of which waited for: 17 -> 20; matrix products, arithmetic and copies ran while one was open for 21% -> 21% of each run, Pallas kernels for 16% -> 17%
where the time goes in v4:
time: 603 us; the launch traced here: 591 us
  waiting for transfers between devices  158 us (26%)
  Pallas kernels  139 us (23%)
  starting transfers between devices  107 us (18%)
  other arithmetic  82.1 us (14%)
  local copies, waits for them, and re-layouts  68.6 us (11%)
  between operations  19.3 us (3%)
  blocking collectives  8.69 us (1%)
  matrix products  7.88 us (1%)
    all_to_all x8, starting transfers between devices, exchanged(): return lax.all_to_all(values, 'mp', 0, 0, tiled=True)  51.4 us
    all_to_all x8, waiting for transfers between devices, exchanged(): return lax.all_to_all(values, 'mp', 0, 0, tiled=True)  48.4 us
    ppermute x17, waiting for transfers between devices, moved(): lax.ppermute(values, 'dp', [(i, i ^ bit) for i in range(lax.axis_size('dp...  40.6 us
    unnamed x180, local copies, waits for them, and re-layouts  36.2 us
    pallas_call x2, Pallas kernels, attend_back(): pl.pallas_call(functools.partial(back_kernel, pieces=pieces, rows=rows),...  31.7 us
    pallas_call x1, Pallas kernels, feed(): pl.pallas_call(feed_kernel, grid=(n // block,), in_specs=[tokens, tokens,...  24.6 us
    pallas_call x7, Pallas kernels, weigh(): pl.pallas_call(weigh_kernel, grid=(right // wide,), in_specs=[pl.BlockSpe...  23.2 us
    ppermute x17, starting transfers between devices, moved(): lax.ppermute(values, 'dp', [(i, i ^ bit) for i in range(lax.axis_size('dp...  22 us
  transfers between devices with their start and end apart: 46, of which 20 were waited for; matrix products, arithmetic and copies ran while one was open for 21% of the time, Pallas kernels for 17%

profile of v4, /device:TPU:0, one launch (start us, length us, event | category | flops | bytes accessed | tf_op | source)
XLA Modules:
  0.0 590.7 jit_solution(6682728887825616061)
XLA Ops:
  36.7 13.3 %maximum_maximum_fusion.1 = bf16[1024,1024]{1,0:T(8,128)(2,1)} fusion(bf16[256,512]{1,0:T(8,128)(2,1)S(1)} %get-tuple-element.193, bf16[256,512]{1,0:T(8,128)(2,1)S(1)} %get-tuple-element.194), kind=kLoop, calls=%fused_computation.12 | loop fusion | flops 16777216 | bytes 2621440 | tf_op jit(solution)/shard_map/concatenate | solution.py:541
  56.0 7.0 %fusion.18 = (f32[32,3072]{0,1:T(8,128)}, f32[32,3072]{0,1:T(8,128)S(1)}, f32[32,3072]{0,1:T(8,128)S(1)}) fusion(f32[32]{0:T(128)S(1)} %multiply_exponential_fusion, f32[3072]{0:T(1024)S(1)} %add_convert_fusion.8), kind=kLoop, calls=%fused_computation.75 | loop fusion | flops 196608 | bytes 1192064 | tf_op jit(solution)/shard_map/neg | solution.py:678
  89.8 7.9 %shard_map.255 = (bf16[4,512,384]{2,1,0:T(8,128)(2,1)}, f32[8,128]{1,0:T(8,128)S(1)}) custom-call(bf16[1024,1024]{1,0:T(8,128)(2,1)S(1)} %get-tuple-element.143.h_ref.a_ref, bf16[1024,1024]{1,0:T(8,128)(2,1)} %maximum_select_fusion.1.first_ref.a_ref, bf16[1024,1024]{1,0:T(8,128)(2,1)} %bitcast.6.w_ref, f32[1024,128]{1,0:T(8,128)S(1)} %slice.256.cos_ref, ...), custom_call_target="tpu_custom_call" | custom-call | tf_op jit(solution)/shard_map/pallas_call | solution.py:68
  101.5 17.9 %all-to-all-start.1 = ((bf16[4,512,384]{2,1,0:T(8,128)(2,1)}), bf16[4,512,384]{2,1,0:T(8,128)(2,1)S(1)}, u32[]{:S(2)}, u32[]{:S(2)}) async-start(bf16[4,512,384]{2,1,0:T(8,128)(2,1)} %get-tuple-element.77), calls=%async_computation.1 | async-start | bytes 3145728 | tf_op jit(solution)/shard_map/all_to_all | solution.py:591
  123.4 14.4 %collective-permute-done.9 = bf16[256,1024]{1,0:T(8,128)(2,1)} collective-permute-done((bf16[256,1024]{1,0:T(8,128)(2,1)S(1)}, bf16[256,1024]{1,0:T(8,128)(2,1)}, u32[]{:S(2)}, u32[]{:S(2)}) %collective-permute-start.9) | collective-permute-done | bytes 524320 | tf_op jit(solution)/shard_map/ppermute | solution.py:487
  142.6 12.3 %collective-permute-done.11 = bf16[256,1024]{1,0:T(8,128)(2,1)S(1)} collective-permute-done((bf16[256,1024]{1,0:T(8,128)(2,1)S(1)}, bf16[256,1024]{1,0:T(8,128)(2,1)S(1)}, u32[]{:S(2)}, u32[]{:S(2)}) %collective-permute-start.11) | collective-permute-done | bytes 524320 | tf_op jit(solution)/shard_map/ppermute | solution.py:487
  156.2 6.5 %shard_map.257 = (bf16[4,512,384]{2,1,0:T(8,128)(2,1)S(1)}, f32[8,128]{1,0:T(8,128)S(1)}) custom-call(bf16[1024,1024]{1,0:T(8,128)(2,1)S(1)} %copy-done.5, bf16[1024,1024]{1,0:T(8,128)(2,1)} %maximum_select_fusion.1.first_ref.a_ref, bf16[1024,1024]{1,0:T(8,128)(2,1)} %copy-done.43, f32[1024,128]{1,0:T(8,128)S(1)} %copy-done.25, f32[1024,128]{1,0:T(8,128)S(1)} %copy-done.23), custom_call_target="tpu_custom_call" | custom-call | tf_op jit(solution)/shard_map/pallas_call | solution.py:68
  169.4 10.1 %shard_map.256 = (bf16[4,512,128]{2,1,0:T(8,128)(2,1)S(1)}, f32[2,2048]{1,0:T(2,128)S(1)}) custom-call(s32[1,2048]{1,0:T(1,128)S(1)} %get-tuple-element.105.start_ref, bf16[4,512,384]{2,1,0:T(8,128)(2,1)S(1)} %all-to-all-done.1.q_ref.k_ref.v_ref, bf16[4,512,384]{2,1,0:T(8,128)(2,1)S(1)} %all-to-all-done.1.q_ref.k_ref.v_ref, ...), custom_call_target="tpu_custom_call" | custom-call | tf_op jit(solution)/shard_map/pallas_call | solution.py:138
  180.3 16.2 %all-to-all-done.3.q_ref.k_ref.v_ref = bf16[4,512,384]{2,1,0:T(8,128)(2,1)S(1)} async-done(((bf16[4,512,384]{2,1,0:T(8,128)(2,1)}), bf16[4,512,384]{2,1,0:T(8,128)(2,1)S(1)}, u32[]{:S(2)}, u32[]{:S(2)}) %all-to-all-start.3) | async-done | bytes 1572896 | tf_op jit(solution)/shard_map/all_to_all | solution.py:591
  200.2 10.9 %shard_map.258 = (bf16[4,512,128]{2,1,0:T(8,128)(2,1)}, f32[2,2048]{1,0:T(2,128)S(1)}) custom-call(s32[1,2048]{1,0:T(1,128)S(1)} %get-tuple-element.105.start_ref, bf16[4,512,384]{2,1,0:T(8,128)(2,1)S(1)} %all-to-all-done.3.q_ref.k_ref.v_ref, bf16[4,512,384]{2,1,0:T(8,128)(2,1)S(1)} %all-to-all-done.3.q_ref.k_ref.v_ref, ...), custom_call_target="tpu_custom_call" | custom-call | tf_op jit(solution)/shard_map/pallas_call | solution.py:138
  216.7 13.9 %all-gather.4.cloned.1.call-done.refs_0_.refs_1_ = bf16[1024,5120]{1,0:T(8,128)(2,1)} async-done(((bf16[256,5120]{1,0:T(8,128)(2,1)}), bf16[1024,5120]{1,0:T(8,128)(2,1)}) %all-gather.4.cloned.1.call-update) | async-done | bytes 10485776 | tf_op jit(solution)/shard_map/all_gather | solution.py:538
  247.4 24.6 %shard_map.260 = (f32[1024,1024]{1,0:T(8,128)}, bf16[1024,1024]{1,0:T(8,128)(2,1)S(1)}, bf16[1024,1536]{1,0:T(8,128)(2,1)}, bf16[1024,3072]{1,0:T(8,128)(2,1)}, bf16[1024,1024]{1,0:T(8,128)(2,1)S(1)}) custom-call(bf16[1024,1024]{1,0:T(8,128)(2,1)} %copy-done.42, bf16[1024,1024]{1,0:T(8,128)(2,1)} %copy-done.29, bf16[1024,1024]{1,0:T(8,128)(2,1)} %copy-done.57, ...), custom_call_target="tpu_custom_call" | custom-call | tf_op jit(solution)/shard_map/pallas_call | solution.py:289
  272.0 11.0 %shard_map.261 = bf16[1024,3072]{1,0:T(8,128)(2,1)} custom-call(bf16[1024,1024]{1,0:T(8,128)(2,1)S(1)} %get-tuple-element.90.a_ref, bf16[1024,3072]{1,0:T(8,128)(2,1)} %get-tuple-element.91.b_ref), custom_call_target="tpu_custom_call" | custom-call | tf_op jit(solution)/shard_map/pallas_call | solution.py:370
  288.6 9.0 %shard_map.262 = (f32[1024,1024]{1,0:T(8,128)}, bf16[1024,1024]{1,0:T(8,128)(2,1)S(1)}, f32[8,1024]{1,0:T(8,128)S(1)}, bf16[4,512,128]{2,1,0:T(8,128)(2,1)}, bf16[4,512,128]{2,1,0:T(8,128)(2,1)S(1)}) custom-call(s32[1]{0:T(128)} %bitcast.18.core_ref, f32[1024,1024]{1,0:T(8,128)} %get-tuple-element.92.res_ref, bf16[1024,1024]{1,0:T(8,128)(2,1)} %copy-done.32, ...), custom_call_target="tpu_custom_call" | custom-call | tf_op jit(solution)/shard_map/pallas_call | solution.py:343
  313.4 13.3 %all-to-all-done.5.g_ref = bf16[4,512,128]{2,1,0:T(8,128)(2,1)} async-done(((bf16[4,512,128]{2,1,0:T(8,128)(2,1)}), bf16[4,512,128]{2,1,0:T(8,128)(2,1)}, u32[]{:S(2)}, u32[]{:S(2)}) %all-to-all-start.5) | async-done | bytes 524320 | tf_op jit(solution)/shard_map/all_to_all | solution.py:591
  331.3 15.2 %shard_map.265 = bf16[4,512,384]{2,1,0:T(8,128)(2,1)S(1)} custom-call(s32[1,2048]{1,0:T(1,128)S(1)} %get-tuple-element.105.start_ref, bf16[4,512,384]{2,1,0:T(8,128)(2,1)} %copy-done.3, bf16[4,512,384]{2,1,0:T(8,128)(2,1)} %copy-done.3, bf16[4,512,384]{2,1,0:T(8,128)(2,1)} %copy-done.3, bf16[4,512,128]{2,1,0:T(8,128)(2,1)S(1)} %copy-done.31, ...), custom_call_target="tpu_custom_call" | custom-call | tf_op jit(solution)/shard_map/pallas_call | solution.py:201
  357.4 5.7 all-to-all-start.6
  363.2 5.9 shard_map.266
  385.0 16.5 %shard_map.267 = bf16[4,512,384]{2,1,0:T(8,128)(2,1)} custom-call(s32[1,2048]{1,0:T(1,128)S(1)} %get-tuple-element.105.start_ref, bf16[4,512,384]{2,1,0:T(8,128)(2,1)} %copy-done.2, bf16[4,512,384]{2,1,0:T(8,128)(2,1)} %copy-done.2, bf16[4,512,384]{2,1,0:T(8,128)(2,1)} %copy-done.2, bf16[4,512,128]{2,1,0:T(8,128)(2,1)} %get-tuple-element.85.o_ref, ...), custom_call_target="tpu_custom_call" | custom-call | tf_op jit(solution)/shard_map/pallas_call | solution.py:201
  409.3 10.7 %collective-permute-start.25 = (bf16[128,1536]{1,0:T(8,128)(2,1)}, bf16[128,1536]{1,0:T(8,128)(2,1)}, u32[]{:S(2)}, u32[]{:S(2)}) collective-permute-start(bf16[128,1536]{1,0:T(8,128)(2,1)} %constant_dynamic-slice_fusion.2), channel_id=1, source_target_pairs={{0,4},{4,0},{8,12},{12,8},{16,20},{20,16},{24,28},{28,24},{1,5},{5... | collective-permute-start | bytes 1179656 | tf_op jit(solution)/shard_map/ppermute | solution.py:487
  442.9 18.9 %all-to-all-done.8 = bf16[4,512,384]{2,1,0:T(8,128)(2,1)} async-done(((bf16[4,512,384]{2,1,0:T(8,128)(2,1)}), bf16[4,512,384]{2,1,0:T(8,128)(2,1)}, u32[]{:S(2)}, u32[]{:S(2)}) %all-to-all-start.8) | async-done | bytes 1572896 | tf_op jit(solution)/shard_map/all_to_all | solution.py:591
  493.3 18.8 %all-to-all-done.9 = bf16[4,256,1024]{2,1,0:T(8,128)(2,1)S(1)} async-done(((bf16[4,256,1024]{2,1,0:T(8,128)(2,1)}), bf16[4,256,1024]{2,1,0:T(8,128)(2,1)S(1)}, u32[]{:S(2)}, u32[]{:S(2)}) %all-to-all-start.9) | async-done | bytes 2097184 | tf_op jit(solution)/shard_map/all_to_all | solution.py:570
  520.6 8.7 %all_to_all.89 = f32[4,24,128]{2,1,0:T(8,128)S(1)} all-to-all(f32[4,24,128]{2,1,0:T(8,128)S(1)} %bitcast.127), channel_id=1, replica_groups=mesh['dp'=8,'mp'=4] {'mp'}, dimensions={0} | all-to-all | bytes 98304 | tf_op jit(solution)/shard_map/all_to_all | solution.py:783
  536.7 7.3 %collective-permute-done.27 = bf16[256,512]{1,0:T(8,128)(2,1)S(1)} collective-permute-done((bf16[256,512]{1,0:T(8,128)(2,1)}, bf16[256,512]{1,0:T(8,128)(2,1)S(1)}, u32[]{:S(2)}, u32[]{:S(2)}) %collective-permute-start.27) | collective-permute-done | bytes 262176 | tf_op jit(solution)/shard_map/ppermute | solution.py:519
  (395 shorter events, 275.4 us)
Async XLA Ops:
  15.9 62.7 %collective-permute-start = (bf16[512,1024]{1,0:T(8,128)(2,1)}, bf16[512,1024]{1,0:T(8,128)(2,1)}, u32[]{:S(2)}, u32[]{:S(2)}) collective-permute-start(bf16[512,1024]{1,0:T(8,128)(2,1)} %param.15), channel_id=1, source_target_pairs={{0,4},{4,0},{8,12},{12,8},{16,20},{20,16},{24,28},{28,24},{1,5},{5... | collective-permute-start | bytes 3145736 | tf_op jit(solution)/shard_map/ppermute | solution.py:487
  16.0 62.6 %collective-permute-start.4 = (bf16[512,1024]{1,0:T(8,128)(2,1)}, bf16[512,1024]{1,0:T(8,128)(2,1)}, u32[]{:S(2)}, u32[]{:S(2)}) collective-permute-start(bf16[512,1024]{1,0:T(8,128)(2,1)} %param.16), channel_id=1, source_target_pairs={{0,4},{4,0},{8,12},{12,8},{16,20},{20,16},{24,28},{28,24},{1,5},{5... | collective-permute-start | bytes 3145736 | tf_op jit(solution)/shard_map/ppermute | solution.py:487
  33.6 42.3 %collective-permute-start.7 = (bf16[256,2560]{1,0:T(8,128)(2,1)}, bf16[256,2560]{1,0:T(8,128)(2,1)}, u32[]{:S(2)}, u32[]{:S(2)}) collective-permute-start(bf16[256,2560]{1,0:T(8,128)(2,1)} %concatenate.147), channel_id=1, source_target_pairs={{0,1},{1,0},{2,4},{3,5},{4,2},{5,3},{6,7},{7,6},{8,9},{9,8},{10,12... | collective-permute-start | bytes 3932168 | tf_op jit(solution)/shard_map/ppermute | solution.py:519
  51.3 38.5 %all-to-all-start = ((bf16[4,256,1024]{2,1,0:T(8,128)(2,1)}), bf16[4,256,1024]{2,1,0:T(8,128)(2,1)}, u32[]{:S(2)}, u32[]{:S(2)}) async-start(bf16[4,256,1024]{2,1,0:T(8,128)(2,1)} %bitcast.5), calls=%async_computation | async-start | bytes 4194304 | tf_op jit(solution)/shard_map/all_to_all | solution.py:542
  55.7 174.8 %all-gather.4.cloned.1.call-start = ((), (), s32[]{:S(2)}) async-start(), calls=%async_computation.15 | async-start | bytes 13107200 | tf_op jit(solution)/shard_map/all_gather | solution.py:538
  76.0 21.7 %collective-permute-start.8 = (bf16[256,2560]{1,0:T(8,128)(2,1)}, bf16[256,2560]{1,0:T(8,128)(2,1)}, u32[]{:S(2)}, u32[]{:S(2)}) collective-permute-start(bf16[256,2560]{1,0:T(8,128)(2,1)} %collective-permute-done.7), channel_id=1, source_target_pairs={{2,3},{3,2},{4,5},{5,4},{10,11},{11,10},{12,13},{13,12},{18,19},{1... | collective-permute-start | bytes 3932168 | tf_op jit(solution)/shard_map/ppermute | solution.py:522
  101.5 62.4 %all-to-all-start.1 = ((bf16[4,512,384]{2,1,0:T(8,128)(2,1)}), bf16[4,512,384]{2,1,0:T(8,128)(2,1)S(1)}, u32[]{:S(2)}, u32[]{:S(2)}) async-start(bf16[4,512,384]{2,1,0:T(8,128)(2,1)} %get-tuple-element.77), calls=%async_computation.1 | async-start | bytes 3145728 | tf_op jit(solution)/shard_map/all_to_all | solution.py:591
  121.4 21.1 %collective-permute-start.10 = (bf16[256,1024]{1,0:T(8,128)(2,1)S(1)}, bf16[256,1024]{1,0:T(8,128)(2,1)S(1)}, u32[]{:S(2)}, u32[]{:S(2)}) collective-permute-start(bf16[256,1024]{1,0:T(8,128)(2,1)S(1)} %pad_maximum_fusion.8), channel_id=1, source_target_pairs={{0,16},{4,20},{8,24},{12,28},{16,0},{20,4},{24,8},{28,12},{1,17},{... | collective-permute-start | bytes 1572872 | tf_op jit(solution)/shard_map/ppermute | solution.py:487
  122.9 31.9 %collective-permute-start.11 = (bf16[256,1024]{1,0:T(8,128)(2,1)S(1)}, bf16[256,1024]{1,0:T(8,128)(2,1)S(1)}, u32[]{:S(2)}, u32[]{:S(2)}) collective-permute-start(bf16[256,1024]{1,0:T(8,128)(2,1)S(1)} %pad_maximum_fusion.8), channel_id=1, source_target_pairs={{0,24},{4,28},{8,16},{12,20},{16,8},{20,12},{24,0},{28,4},{1,25},{... | collective-permute-start | bytes 1572872 | tf_op jit(solution)/shard_map/ppermute | solution.py:487
  163.9 32.6 %all-to-all-start.3 = ((bf16[4,512,384]{2,1,0:T(8,128)(2,1)}), bf16[4,512,384]{2,1,0:T(8,128)(2,1)S(1)}, u32[]{:S(2)}, u32[]{:S(2)}) async-start(bf16[4,512,384]{2,1,0:T(8,128)(2,1)} %copy-done.33), calls=%async_computation.3 | async-start | bytes 3145728 | tf_op jit(solution)/shard_map/all_to_all | solution.py:591
  216.2 137.1 %reduce-scatter.3.cloned.1.call-start = ((), (), s32[]{:S(2)}) async-start(), calls=%async_computation.16 | async-start | bytes 7864320 | tf_op jit(solution)/shard_map/reduce_scatter | solution.py:557
  283.0 184.3 %reduce-scatter.5.cloned.1.call-start = ((), (), s32[]{:S(2)}) async-start(), calls=%async_computation.17 | async-start | bytes 5242880 | tf_op jit(solution)/shard_map/reduce_scatter | solution.py:557
  326.7 30.7 %all-to-all-start.7 = ((bf16[4,512,128]{2,1,0:T(8,128)(2,1)}), bf16[4,512,128]{2,1,0:T(8,128)(2,1)}, u32[]{:S(2)}, u32[]{:S(2)}) async-start(bf16[4,512,128]{2,1,0:T(8,128)(2,1)} %copy-done.40), calls=%async_computation.8 | async-start | bytes 1048576 | tf_op jit(solution)/shard_map/all_to_all | solution.py:591
  357.4 62.6 %all-to-all-start.6 = ((bf16[4,512,384]{2,1,0:T(8,128)(2,1)}), bf16[4,512,384]{2,1,0:T(8,128)(2,1)}, u32[]{:S(2)}, u32[]{:S(2)}) async-start(bf16[4,512,384]{2,1,0:T(8,128)(2,1)} %copy-done.21), calls=%async_computation.6 | async-start | bytes 3145728 | tf_op jit(solution)/shard_map/all_to_all | solution.py:591
  373.7 33.0 %collective-permute-start.17 = (bf16[256,1536]{1,0:T(8,128)(2,1)}, bf16[256,1536]{1,0:T(8,128)(2,1)}, u32[]{:S(2)}, u32[]{:S(2)}) collective-permute-start(bf16[256,1536]{1,0:T(8,128)(2,1)} %fusion.15), channel_id=1, source_target_pairs={{0,1},{1,0},{2,4},{3,5},{4,2},{5,3},{6,7},{7,6},{8,9},{9,8},{10,12... | collective-permute-start | bytes 2359304 | tf_op jit(solution)/shard_map/ppermute | solution.py:519
  409.3 31.8 %collective-permute-start.25 = (bf16[128,1536]{1,0:T(8,128)(2,1)}, bf16[128,1536]{1,0:T(8,128)(2,1)}, u32[]{:S(2)}, u32[]{:S(2)}) collective-permute-start(bf16[128,1536]{1,0:T(8,128)(2,1)} %constant_dynamic-slice_fusion.2), channel_id=1, source_target_pairs={{0,4},{4,0},{8,12},{12,8},{16,20},{20,16},{24,28},{28,24},{1,5},{5... | collective-permute-start | bytes 1179656 | tf_op jit(solution)/shard_map/ppermute | solution.py:487
  420.0 41.8 %all-to-all-start.8 = ((bf16[4,512,384]{2,1,0:T(8,128)(2,1)}), bf16[4,512,384]{2,1,0:T(8,128)(2,1)}, u32[]{:S(2)}, u32[]{:S(2)}) async-start(bf16[4,512,384]{2,1,0:T(8,128)(2,1)} %shard_map.267), calls=%async_computation.9 | async-start | bytes 3145728 | tf_op jit(solution)/shard_map/all_to_all | solution.py:591
  424.3 106.9 %all-gather.6.cloned.1.call-start = ((), (), s32[]{:S(2)}) async-start(), calls=%async_computation.18 | async-start | bytes 3538944 | tf_op jit(solution)/shard_map/all_gather | solution.py:785
  433.7 32.7 %collective-permute-start.21 = (bf16[256,1024]{1,0:T(8,128)(2,1)}, bf16[256,1024]{1,0:T(8,128)(2,1)S(1)}, u32[]{:S(2)}, u32[]{:S(2)}) collective-permute-start(bf16[256,1024]{1,0:T(8,128)(2,1)} %get-tuple-element.144), channel_id=1, source_target_pairs={{0,24},{4,28},{8,16},{12,20},{16,8},{20,12},{24,0},{28,4},{1,25},{... | collective-permute-start | bytes 1572872 | tf_op jit(solution)/shard_map/ppermute | solution.py:487
  435.2 31.3 %collective-permute-start.20 = (bf16[256,1024]{1,0:T(8,128)(2,1)}, bf16[256,1024]{1,0:T(8,128)(2,1)}, u32[]{:S(2)}, u32[]{:S(2)}) collective-permute-start(bf16[256,1024]{1,0:T(8,128)(2,1)} %get-tuple-element.145), channel_id=1, source_target_pairs={{0,16},{4,20},{8,24},{12,28},{16,0},{20,4},{24,8},{28,12},{1,17},{... | collective-permute-start | bytes 1572872 | tf_op jit(solution)/shard_map/ppermute | solution.py:487
  436.5 30.0 %collective-permute-start.19 = (bf16[256,1024]{1,0:T(8,128)(2,1)}, bf16[256,1024]{1,0:T(8,128)(2,1)}, u32[]{:S(2)}, u32[]{:S(2)}) collective-permute-start(bf16[256,1024]{1,0:T(8,128)(2,1)} %get-tuple-element.146), channel_id=1, source_target_pairs={{0,8},{4,12},{8,0},{12,4},{16,24},{20,28},{24,16},{28,20},{1,9},{5... | collective-permute-start | bytes 1572872 | tf_op jit(solution)/shard_map/ppermute | solution.py:487
  483.9 28.2 %all-to-all-start.9 = ((bf16[4,256,1024]{2,1,0:T(8,128)(2,1)}), bf16[4,256,1024]{2,1,0:T(8,128)(2,1)S(1)}, u32[]{:S(2)}, u32[]{:S(2)}) async-start(bf16[4,256,1024]{2,1,0:T(8,128)(2,1)} %bitcast.110), calls=%async_computation.11 | async-start | bytes 4194304 | tf_op jit(solution)/shard_map/all_to_all | solution.py:570
  490.5 40.7 %collective-permute-start.23 = (bf16[256,1536]{1,0:T(8,128)(2,1)}, bf16[256,1536]{1,0:T(8,128)(2,1)}, u32[]{:S(2)}, u32[]{:S(2)}) collective-permute-start(bf16[256,1536]{1,0:T(8,128)(2,1)} %fusion.14), channel_id=1, source_target_pairs={{0,1},{1,0},{2,4},{3,5},{4,2},{5,3},{6,7},{7,6},{8,9},{9,8},{10,12... | collective-permute-start | bytes 2359304 | tf_op jit(solution)/shard_map/ppermute | solution.py:519
  515.4 53.2 %all-gather.8.cloned.1.call-start = ((), (), s32[]{:S(2)}) async-start(), calls=%async_computation.19 | async-start | bytes 3538944 | tf_op jit(solution)/shard_map/all_gather | solution.py:794
  (101 other events, 819.5 us)
Sparse Core Ops, SparseCore 0:
  101.6 128.9 all-gather.3
  283.1 70.1 reduce-scatter.2
  356.3 52.6 reduce-scatter.4
  443.1 38.3 all-gather.5
  536.0 32.6 all-gather.7

commit v5 on v4

--- a/solution.py
+++ b/solution.py
@@ -656,7 +656,7 @@
     part = tied(beside(at.slice_of(w_gate), wider, at.slice_of(w_up), wider, outer), before)
     got_feed = (part, at.cross(part))
     near = [beside(*at.quarters(part, got)) for part, got in got_pair]
-    w_pair = [at.gathered_direct(near[0])]
+    w_pair = [at.gathered_direct(tied(near[0], ()))]
 
     x_all = at.ordered(*tied((hidden_in, moved(hidden_in, 1)), near[0]))
     first_all = at.ordered(*tied((first_in, moved(first_in, 1)), near[0]))

time: 603 us -> 592 us (0.982)
  the two profiles are of different devices: /device:TPU:0 before, /device:TPU:27 now
where the time goes in v5:
time: 592 us; the launch traced here: 582 us
  waiting for transfers between devices  164 us (28%)
  Pallas kernels  139 us (23%)
  starting transfers between devices  109 us (18%)
  other arithmetic  70.1 us (12%)
  local copies, waits for them, and re-layouts  65.9 us (11%)
  between operations  19.2 us (3%)
  matrix products  7.88 us (1%)
  blocking collectives  6.84 us (1%)
    all_to_all x8, starting transfers between devices, exchanged(): return lax.all_to_all(values, 'mp', 0, 0, tiled=True)  51.7 us
    all_to_all x8, waiting for transfers between devices, exchanged(): return lax.all_to_all(values, 'mp', 0, 0, tiled=True)  47.4 us
    all_gather x1, waiting for transfers between devices, gathered(): lax.all_gather(part, 'dp', axis=0, tiled=True, axis_index_groups=self.sides)  34.9 us
    unnamed x180, local copies, waits for them, and re-layouts  33.8 us
    pallas_call x2, Pallas kernels, attend_back(): pl.pallas_call(functools.partial(back_kernel, pieces=pieces, rows=rows),...  31.2 us
    pallas_call x1, Pallas kernels, feed(): pl.pallas_call(feed_kernel, grid=(n // block,), in_specs=[tokens, tokens,...  24.6 us
    ppermute x17, starting transfers between devices, moved(): lax.ppermute(values, 'dp', [(i, i ^ bit) for i in range(lax.axis_size('dp...  24.1 us
    ppermute x6, waiting for transfers between devices, cross(): return lax.ppermute(values, ('dp', 'mp'), cross_pairs(self.n_dp))  23.6 us
  transfers between devices with their start and end apart: 46, of which 22 were waited for; matrix products, arithmetic and copies ran while one was open for 19% of the time, Pallas kernels for 17%

profile of v5, /device:TPU:27, one launch (start us, length us, event | category | flops | bytes accessed | tf_op | source)
XLA Modules:
  0.0 581.9 jit_solution(17660946163048343502)
XLA Ops:
  37.7 7.0 %fusion.18 = (f32[32,3072]{0,1:T(8,128)}, f32[32,3072]{0,1:T(8,128)S(1)}, f32[32,3072]{0,1:T(8,128)S(1)}) fusion(f32[32]{0:T(128)S(1)} %multiply_exponential_fusion, f32[3072]{0:T(1024)S(1)} %add_convert_fusion.8), kind=kLoop, calls=%fused_computation.75 | loop fusion | flops 196608 | bytes 1192064 | tf_op jit(solution)/shard_map/neg | solution.py:678
  74.1 7.9 %shard_map.255 = (bf16[4,512,384]{2,1,0:T(8,128)(2,1)}, f32[8,128]{1,0:T(8,128)S(1)}) custom-call(bf16[1024,1024]{1,0:T(8,128)(2,1)S(1)} %get-tuple-element.143.h_ref.a_ref, bf16[1024,1024]{1,0:T(8,128)(2,1)} %maximum_select_fusion.1.first_ref.a_ref, bf16[1024,1024]{1,0:T(8,128)(2,1)} %bitcast.6.w_ref, f32[1024,128]{1,0:T(8,128)S(1)} %slice.256.cos_ref, ...), custom_call_target="tpu_custom_call" | custom-call | tf_op jit(solution)/shard_map/pallas_call | solution.py:68
  85.8 12.9 %all-to-all-start.1 = ((bf16[4,512,384]{2,1,0:T(8,128)(2,1)}), bf16[4,512,384]{2,1,0:T(8,128)(2,1)S(1)}, u32[]{:S(2)}, u32[]{:S(2)}) async-start(bf16[4,512,384]{2,1,0:T(8,128)(2,1)} %get-tuple-element.77), calls=%async_computation.1 | async-start | bytes 3145728 | tf_op jit(solution)/shard_map/all_to_all | solution.py:591
  108.1 7.3 %collective-permute-done.11 = bf16[256,1024]{1,0:T(8,128)(2,1)S(1)} collective-permute-done((bf16[256,1024]{1,0:T(8,128)(2,1)S(1)}, bf16[256,1024]{1,0:T(8,128)(2,1)S(1)}, u32[]{:S(2)}, u32[]{:S(2)}) %collective-permute-start.11) | collective-permute-done | bytes 524320 | tf_op jit(solution)/shard_map/ppermute | solution.py:487
  116.8 6.5 %shard_map.257 = (bf16[4,512,384]{2,1,0:T(8,128)(2,1)S(1)}, f32[8,128]{1,0:T(8,128)S(1)}) custom-call(bf16[1024,1024]{1,0:T(8,128)(2,1)S(1)} %copy-done.5, bf16[1024,1024]{1,0:T(8,128)(2,1)} %maximum_select_fusion.1.first_ref.a_ref, bf16[1024,1024]{1,0:T(8,128)(2,1)} %copy-done.43, f32[1024,128]{1,0:T(8,128)S(1)} %copy-done.25, f32[1024,128]{1,0:T(8,128)S(1)} %copy-done.23), custom_call_target="tpu_custom_call" | custom-call | tf_op jit(solution)/shard_map/pallas_call | solution.py:68
  134.8 10.1 %shard_map.256 = (bf16[4,512,128]{2,1,0:T(8,128)(2,1)S(1)}, f32[2,2048]{1,0:T(2,128)S(1)}) custom-call(s32[1,2048]{1,0:T(1,128)S(1)} %get-tuple-element.105.start_ref, bf16[4,512,384]{2,1,0:T(8,128)(2,1)S(1)} %all-to-all-done.1.q_ref.k_ref.v_ref, bf16[4,512,384]{2,1,0:T(8,128)(2,1)S(1)} %all-to-all-done.1.q_ref.k_ref.v_ref, ...), custom_call_target="tpu_custom_call" | custom-call | tf_op jit(solution)/shard_map/pallas_call | solution.py:138
  145.8 7.4 %all-to-all-done.3.q_ref.k_ref.v_ref = bf16[4,512,384]{2,1,0:T(8,128)(2,1)S(1)} async-done(((bf16[4,512,384]{2,1,0:T(8,128)(2,1)}), bf16[4,512,384]{2,1,0:T(8,128)(2,1)S(1)}, u32[]{:S(2)}, u32[]{:S(2)}) %all-to-all-start.3) | async-done | bytes 1572896 | tf_op jit(solution)/shard_map/all_to_all | solution.py:591
  159.1 10.9 %shard_map.258 = (bf16[4,512,128]{2,1,0:T(8,128)(2,1)}, f32[2,2048]{1,0:T(2,128)S(1)}) custom-call(s32[1,2048]{1,0:T(1,128)S(1)} %get-tuple-element.105.start_ref, bf16[4,512,384]{2,1,0:T(8,128)(2,1)S(1)} %all-to-all-done.3.q_ref.k_ref.v_ref, bf16[4,512,384]{2,1,0:T(8,128)(2,1)S(1)} %all-to-all-done.3.q_ref.k_ref.v_ref, ...), custom_call_target="tpu_custom_call" | custom-call | tf_op jit(solution)/shard_map/pallas_call | solution.py:138
  170.0 7.4 %all-to-all-done.2.refs_0_ = bf16[4,512,128]{2,1,0:T(8,128)(2,1)S(1)} async-done(((bf16[4,512,128]{2,1,0:T(8,128)(2,1)}), bf16[4,512,128]{2,1,0:T(8,128)(2,1)S(1)}, u32[]{:S(2)}, u32[]{:S(2)}) %all-to-all-start.2) | async-done | bytes 524320 | tf_op jit(solution)/shard_map/all_to_all | solution.py:591
  182.3 34.9 %all-gather.4.cloned.1.call-done.refs_0_.refs_1_ = bf16[1024,5120]{1,0:T(8,128)(2,1)} async-done(((bf16[256,5120]{1,0:T(8,128)(2,1)}), bf16[1024,5120]{1,0:T(8,128)(2,1)}) %all-gather.4.cloned.1.call-update) | async-done | bytes 10485776 | tf_op jit(solution)/shard_map/all_gather | solution.py:538
  234.3 24.6 %shard_map.260 = (f32[1024,1024]{1,0:T(8,128)}, bf16[1024,1024]{1,0:T(8,128)(2,1)S(1)}, bf16[1024,1536]{1,0:T(8,128)(2,1)}, bf16[1024,3072]{1,0:T(8,128)(2,1)}, bf16[1024,1024]{1,0:T(8,128)(2,1)S(1)}) custom-call(bf16[1024,1024]{1,0:T(8,128)(2,1)} %copy-done.42, bf16[1024,1024]{1,0:T(8,128)(2,1)} %copy-done.29, bf16[1024,1024]{1,0:T(8,128)(2,1)} %copy-done.57, ...), custom_call_target="tpu_custom_call" | custom-call | tf_op jit(solution)/shard_map/pallas_call | solution.py:289
  258.9 11.0 %shard_map.261 = bf16[1024,3072]{1,0:T(8,128)(2,1)} custom-call(bf16[1024,1024]{1,0:T(8,128)(2,1)S(1)} %get-tuple-element.90.a_ref, bf16[1024,3072]{1,0:T(8,128)(2,1)} %get-tuple-element.91.b_ref), custom_call_target="tpu_custom_call" | custom-call | tf_op jit(solution)/shard_map/pallas_call | solution.py:370
  275.5 8.9 %shard_map.262 = (f32[1024,1024]{1,0:T(8,128)}, bf16[1024,1024]{1,0:T(8,128)(2,1)S(1)}, f32[8,1024]{1,0:T(8,128)S(1)}, bf16[4,512,128]{2,1,0:T(8,128)(2,1)}, bf16[4,512,128]{2,1,0:T(8,128)(2,1)S(1)}) custom-call(s32[1]{0:T(128)} %bitcast.18.core_ref, f32[1024,1024]{1,0:T(8,128)} %get-tuple-element.92.res_ref, bf16[1024,1024]{1,0:T(8,128)(2,1)} %copy-done.32, ...), custom_call_target="tpu_custom_call" | custom-call | tf_op jit(solution)/shard_map/pallas_call | solution.py:343
  300.1 10.4 %all-to-all-done.5.g_ref = bf16[4,512,128]{2,1,0:T(8,128)(2,1)} async-done(((bf16[4,512,128]{2,1,0:T(8,128)(2,1)}), bf16[4,512,128]{2,1,0:T(8,128)(2,1)}, u32[]{:S(2)}, u32[]{:S(2)}) %all-to-all-start.5) | async-done | bytes 524320 | tf_op jit(solution)/shard_map/all_to_all | solution.py:591
  310.5 6.7 %all-to-all-start.7 = ((bf16[4,512,128]{2,1,0:T(8,128)(2,1)}), bf16[4,512,128]{2,1,0:T(8,128)(2,1)}, u32[]{:S(2)}, u32[]{:S(2)}) async-start(bf16[4,512,128]{2,1,0:T(8,128)(2,1)} %copy-done.40), calls=%async_computation.8 | async-start | bytes 1048576 | tf_op jit(solution)/shard_map/all_to_all | solution.py:591
  317.3 14.9 %shard_map.265 = bf16[4,512,384]{2,1,0:T(8,128)(2,1)S(1)} custom-call(s32[1,2048]{1,0:T(1,128)S(1)} %get-tuple-element.105.start_ref, bf16[4,512,384]{2,1,0:T(8,128)(2,1)} %copy-done.3, bf16[4,512,384]{2,1,0:T(8,128)(2,1)} %copy-done.3, bf16[4,512,384]{2,1,0:T(8,128)(2,1)} %copy-done.3, bf16[4,512,128]{2,1,0:T(8,128)(2,1)S(1)} %copy-done.31, ...), custom_call_target="tpu_custom_call" | custom-call | tf_op jit(solution)/shard_map/pallas_call | solution.py:201
  333.3 6.5 %reduce-scatter.3.cloned.1.call-done = bf16[256,3072]{1,0:T(8,128)(2,1)} async-done(((bf16[1024,3072]{1,0:T(8,128)(2,1)}), bf16[256,3072]{1,0:T(8,128)(2,1)}) %reduce-scatter.3.cloned.1.call-update) | async-done | bytes 1572880 | tf_op jit(solution)/shard_map/reduce_scatter | solution.py:557
  370.4 16.4 %shard_map.267 = bf16[4,512,384]{2,1,0:T(8,128)(2,1)} custom-call(s32[1,2048]{1,0:T(1,128)S(1)} %get-tuple-element.105.start_ref, bf16[4,512,384]{2,1,0:T(8,128)(2,1)} %copy-done.2, bf16[4,512,384]{2,1,0:T(8,128)(2,1)} %copy-done.2, bf16[4,512,384]{2,1,0:T(8,128)(2,1)} %copy-done.2, bf16[4,512,128]{2,1,0:T(8,128)(2,1)} %get-tuple-element.85.o_ref, ...), custom_call_target="tpu_custom_call" | custom-call | tf_op jit(solution)/shard_map/pallas_call | solution.py:201
  386.8 7.6 %collective-permute-done.17 = bf16[256,1536]{1,0:T(8,128)(2,1)} collective-permute-done((bf16[256,1536]{1,0:T(8,128)(2,1)}, bf16[256,1536]{1,0:T(8,128)(2,1)}, u32[]{:S(2)}, u32[]{:S(2)}) %collective-permute-start.17) | collective-permute-done | bytes 786464 | tf_op jit(solution)/shard_map/ppermute | solution.py:519
  397.0 8.4 %collective-permute-start.25 = (bf16[128,1536]{1,0:T(8,128)(2,1)}, bf16[128,1536]{1,0:T(8,128)(2,1)}, u32[]{:S(2)}, u32[]{:S(2)}) collective-permute-start(bf16[128,1536]{1,0:T(8,128)(2,1)} %constant_dynamic-slice_fusion.2), channel_id=1, source_target_pairs={{0,4},{4,0},{8,12},{12,8},{16,20},{20,16},{24,28},{28,24},{1,5},{5... | collective-permute-start | bytes 1179656 | tf_op jit(solution)/shard_map/ppermute | solution.py:487
  428.9 16.9 %all-to-all-done.8 = bf16[4,512,384]{2,1,0:T(8,128)(2,1)} async-done(((bf16[4,512,384]{2,1,0:T(8,128)(2,1)}), bf16[4,512,384]{2,1,0:T(8,128)(2,1)}, u32[]{:S(2)}, u32[]{:S(2)}) %all-to-all-start.8) | async-done | bytes 1572896 | tf_op jit(solution)/shard_map/all_to_all | solution.py:591
  479.3 15.9 %all-to-all-done.9 = bf16[4,256,1024]{2,1,0:T(8,128)(2,1)S(1)} async-done(((bf16[4,256,1024]{2,1,0:T(8,128)(2,1)}), bf16[4,256,1024]{2,1,0:T(8,128)(2,1)S(1)}, u32[]{:S(2)}, u32[]{:S(2)}) %all-to-all-start.9) | async-done | bytes 2097184 | tf_op jit(solution)/shard_map/all_to_all | solution.py:570
  504.4 6.8 %all_to_all.89 = f32[4,24,128]{2,1,0:T(8,128)S(1)} all-to-all(f32[4,24,128]{2,1,0:T(8,128)S(1)} %bitcast.127), channel_id=1, replica_groups=mesh['dp'=8,'mp'=4] {'mp'}, dimensions={0} | all-to-all | bytes 98304 | tf_op jit(solution)/shard_map/all_to_all | solution.py:783
  551.8 12.3 %all-gather.8.cloned.1.call-done.refs_0_.sum_ref = bf16[1024,1536]{1,0:T(8,128)(2,1)} async-done(((bf16[128,1536]{1,0:T(8,128)(2,1)}), bf16[1024,1536]{1,0:T(8,128)(2,1)}) %all-gather.8.cloned.1.call-update) | async-done | bytes 3145744 | tf_op jit(solution)/shard_map/all_gather | solution.py:794
  (396 shorter events, 283.0 us)
Async XLA Ops:
  12.5 50.4 %collective-permute-start = (bf16[512,1024]{1,0:T(8,128)(2,1)}, bf16[512,1024]{1,0:T(8,128)(2,1)}, u32[]{:S(2)}, u32[]{:S(2)}) collective-permute-start(bf16[512,1024]{1,0:T(8,128)(2,1)} %param.15), channel_id=1, source_target_pairs={{0,4},{4,0},{8,12},{12,8},{16,20},{20,16},{24,28},{28,24},{1,5},{5... | collective-permute-start | bytes 3145736 | tf_op jit(solution)/shard_map/ppermute | solution.py:487
  12.5 50.4 %collective-permute-start.4 = (bf16[512,1024]{1,0:T(8,128)(2,1)}, bf16[512,1024]{1,0:T(8,128)(2,1)}, u32[]{:S(2)}, u32[]{:S(2)}) collective-permute-start(bf16[512,1024]{1,0:T(8,128)(2,1)} %param.16), channel_id=1, source_target_pairs={{0,4},{4,0},{8,12},{12,8},{16,20},{20,16},{24,28},{28,24},{1,5},{5... | collective-permute-start | bytes 3145736 | tf_op jit(solution)/shard_map/ppermute | solution.py:487
  27.7 32.6 %collective-permute-start.7 = (bf16[256,2560]{1,0:T(8,128)(2,1)}, bf16[256,2560]{1,0:T(8,128)(2,1)}, u32[]{:S(2)}, u32[]{:S(2)}) collective-permute-start(bf16[256,2560]{1,0:T(8,128)(2,1)} %concatenate.147), channel_id=1, source_target_pairs={{0,1},{1,0},{2,4},{3,5},{4,2},{5,3},{6,7},{7,6},{8,9},{9,8},{10,12... | collective-permute-start | bytes 3932168 | tf_op jit(solution)/shard_map/ppermute | solution.py:519
  33.0 41.1 %all-to-all-start = ((bf16[4,256,1024]{2,1,0:T(8,128)(2,1)}), bf16[4,256,1024]{2,1,0:T(8,128)(2,1)}, u32[]{:S(2)}, u32[]{:S(2)}) async-start(bf16[4,256,1024]{2,1,0:T(8,128)(2,1)} %bitcast.5), calls=%async_computation | async-start | bytes 4194304 | tf_op jit(solution)/shard_map/all_to_all | solution.py:542
  37.7 179.5 %all-gather.4.cloned.1.call-start = ((), (), s32[]{:S(2)}) async-start(), calls=%async_computation.15 | async-start | bytes 13107200 | tf_op jit(solution)/shard_map/all_gather | solution.py:538
  85.8 44.0 %all-to-all-start.1 = ((bf16[4,512,384]{2,1,0:T(8,128)(2,1)}), bf16[4,512,384]{2,1,0:T(8,128)(2,1)S(1)}, u32[]{:S(2)}, u32[]{:S(2)}) async-start(bf16[4,512,384]{2,1,0:T(8,128)(2,1)} %get-tuple-element.77), calls=%async_computation.1 | async-start | bytes 3145728 | tf_op jit(solution)/shard_map/all_to_all | solution.py:591
  129.8 23.3 %all-to-all-start.3 = ((bf16[4,512,384]{2,1,0:T(8,128)(2,1)}), bf16[4,512,384]{2,1,0:T(8,128)(2,1)S(1)}, u32[]{:S(2)}, u32[]{:S(2)}) async-start(bf16[4,512,384]{2,1,0:T(8,128)(2,1)} %copy-done.33), calls=%async_computation.3 | async-start | bytes 3145728 | tf_op jit(solution)/shard_map/all_to_all | solution.py:591
  153.2 24.2 %all-to-all-start.2 = ((bf16[4,512,128]{2,1,0:T(8,128)(2,1)}), bf16[4,512,128]{2,1,0:T(8,128)(2,1)S(1)}, u32[]{:S(2)}, u32[]{:S(2)}) async-start(bf16[4,512,128]{2,1,0:T(8,128)(2,1)} %copy-done.30), calls=%async_computation.2 | async-start | bytes 1048576 | tf_op jit(solution)/shard_map/all_to_all | solution.py:591
  177.4 41.2 %all-to-all-start.4 = ((bf16[4,512,128]{2,1,0:T(8,128)(2,1)}), bf16[4,512,128]{2,1,0:T(8,128)(2,1)S(1)}, u32[]{:S(2)}, u32[]{:S(2)}) async-start(bf16[4,512,128]{2,1,0:T(8,128)(2,1)} %get-tuple-element.85.o_ref), calls=%async_computation.4 | async-start | bytes 1048576 | tf_op jit(solution)/shard_map/all_to_all | solution.py:591
  181.9 157.9 %reduce-scatter.3.cloned.1.call-start = ((), (), s32[]{:S(2)}) async-start(), calls=%async_computation.16 | async-start | bytes 7864320 | tf_op jit(solution)/shard_map/reduce_scatter | solution.py:557
  269.9 181.3 %reduce-scatter.5.cloned.1.call-start = ((), (), s32[]{:S(2)}) async-start(), calls=%async_computation.17 | async-start | bytes 5242880 | tf_op jit(solution)/shard_map/reduce_scatter | solution.py:557
  310.5 33.3 %all-to-all-start.7 = ((bf16[4,512,128]{2,1,0:T(8,128)(2,1)}), bf16[4,512,128]{2,1,0:T(8,128)(2,1)}, u32[]{:S(2)}, u32[]{:S(2)}) async-start(bf16[4,512,128]{2,1,0:T(8,128)(2,1)} %copy-done.40), calls=%async_computation.8 | async-start | bytes 1048576 | tf_op jit(solution)/shard_map/all_to_all | solution.py:591
  343.9 61.6 %all-to-all-start.6 = ((bf16[4,512,384]{2,1,0:T(8,128)(2,1)}), bf16[4,512,384]{2,1,0:T(8,128)(2,1)}, u32[]{:S(2)}, u32[]{:S(2)}) async-start(bf16[4,512,384]{2,1,0:T(8,128)(2,1)} %copy-done.21), calls=%async_computation.6 | async-start | bytes 3145728 | tf_op jit(solution)/shard_map/all_to_all | solution.py:591
  360.8 33.6 %collective-permute-start.17 = (bf16[256,1536]{1,0:T(8,128)(2,1)}, bf16[256,1536]{1,0:T(8,128)(2,1)}, u32[]{:S(2)}, u32[]{:S(2)}) collective-permute-start(bf16[256,1536]{1,0:T(8,128)(2,1)} %fusion.15), channel_id=1, source_target_pairs={{0,1},{1,0},{2,4},{3,5},{4,2},{5,3},{6,7},{7,6},{8,9},{9,8},{10,12... | collective-permute-start | bytes 2359304 | tf_op jit(solution)/shard_map/ppermute | solution.py:519
  397.0 30.0 %collective-permute-start.25 = (bf16[128,1536]{1,0:T(8,128)(2,1)}, bf16[128,1536]{1,0:T(8,128)(2,1)}, u32[]{:S(2)}, u32[]{:S(2)}) collective-permute-start(bf16[128,1536]{1,0:T(8,128)(2,1)} %constant_dynamic-slice_fusion.2), channel_id=1, source_target_pairs={{0,4},{4,0},{8,12},{12,8},{16,20},{20,16},{24,28},{28,24},{1,5},{5... | collective-permute-start | bytes 1179656 | tf_op jit(solution)/shard_map/ppermute | solution.py:487
  405.4 40.3 %all-to-all-start.8 = ((bf16[4,512,384]{2,1,0:T(8,128)(2,1)}), bf16[4,512,384]{2,1,0:T(8,128)(2,1)}, u32[]{:S(2)}, u32[]{:S(2)}) async-start(bf16[4,512,384]{2,1,0:T(8,128)(2,1)} %shard_map.267), calls=%async_computation.9 | async-start | bytes 3145728 | tf_op jit(solution)/shard_map/all_to_all | solution.py:591
  411.1 102.1 %all-gather.6.cloned.1.call-start = ((), (), s32[]{:S(2)}) async-start(), calls=%async_computation.18 | async-start | bytes 3538944 | tf_op jit(solution)/shard_map/all_gather | solution.py:785
  420.5 29.9 %collective-permute-start.21 = (bf16[256,1024]{1,0:T(8,128)(2,1)}, bf16[256,1024]{1,0:T(8,128)(2,1)S(1)}, u32[]{:S(2)}, u32[]{:S(2)}) collective-permute-start(bf16[256,1024]{1,0:T(8,128)(2,1)} %get-tuple-element.144), channel_id=1, source_target_pairs={{0,24},{4,28},{8,16},{12,20},{16,8},{20,12},{24,0},{28,4},{1,25},{... | collective-permute-start | bytes 1572872 | tf_op jit(solution)/shard_map/ppermute | solution.py:487
  421.6 29.3 %collective-permute-start.20 = (bf16[256,1024]{1,0:T(8,128)(2,1)}, bf16[256,1024]{1,0:T(8,128)(2,1)}, u32[]{:S(2)}, u32[]{:S(2)}) collective-permute-start(bf16[256,1024]{1,0:T(8,128)(2,1)} %get-tuple-element.145), channel_id=1, source_target_pairs={{0,16},{4,20},{8,24},{12,28},{16,0},{20,4},{24,8},{28,12},{1,17},{... | collective-permute-start | bytes 1572872 | tf_op jit(solution)/shard_map/ppermute | solution.py:487
  422.1 28.9 %collective-permute-start.19 = (bf16[256,1024]{1,0:T(8,128)(2,1)}, bf16[256,1024]{1,0:T(8,128)(2,1)}, u32[]{:S(2)}, u32[]{:S(2)}) collective-permute-start(bf16[256,1024]{1,0:T(8,128)(2,1)} %get-tuple-element.146), channel_id=1, source_target_pairs={{0,8},{4,12},{8,0},{12,4},{16,24},{20,28},{24,16},{28,20},{1,9},{5... | collective-permute-start | bytes 1572872 | tf_op jit(solution)/shard_map/ppermute | solution.py:487
  467.8 27.4 %all-to-all-start.9 = ((bf16[4,256,1024]{2,1,0:T(8,128)(2,1)}), bf16[4,256,1024]{2,1,0:T(8,128)(2,1)S(1)}, u32[]{:S(2)}, u32[]{:S(2)}) async-start(bf16[4,256,1024]{2,1,0:T(8,128)(2,1)} %bitcast.110), calls=%async_computation.11 | async-start | bytes 4194304 | tf_op jit(solution)/shard_map/all_to_all | solution.py:570
  474.8 38.4 %collective-permute-start.23 = (bf16[256,1536]{1,0:T(8,128)(2,1)}, bf16[256,1536]{1,0:T(8,128)(2,1)}, u32[]{:S(2)}, u32[]{:S(2)}) collective-permute-start(bf16[256,1536]{1,0:T(8,128)(2,1)} %fusion.14), channel_id=1, source_target_pairs={{0,1},{1,0},{2,4},{3,5},{4,2},{5,3},{6,7},{7,6},{8,9},{9,8},{10,12... | collective-permute-start | bytes 2359304 | tf_op jit(solution)/shard_map/ppermute | solution.py:519
  500.9 63.2 %all-gather.8.cloned.1.call-start = ((), (), s32[]{:S(2)}) async-start(), calls=%async_computation.19 | async-start | bytes 3538944 | tf_op jit(solution)/shard_map/all_gather | solution.py:794
  540.6 27.9 %all-to-all-start.12 = ((bf16[8,128,512]{2,1,0:T(8,128)(2,1)}), bf16[8,128,512]{2,1,0:T(8,128)(2,1)S(1)}, u32[]{:S(2)}, u32[]{:S(2)}) async-start(bf16[8,128,512]{2,1,0:T(8,128)(2,1)} %bitcast.41), calls=%async_computation.14 | async-start | bytes 2097152 | tf_op jit(solution)/shard_map/all_to_all | solution.py:554
  (101 other events, 724.7 us)
Sparse Core Ops, SparseCore 0:
  85.9 131.2 all-gather.3
  270.0 69.7 reduce-scatter.2
  342.8 52.7 reduce-scatter.4
  429.0 38.1 all-gather.5
  520.3 43.7 all-gather.7
